TPU v7x, 32 devices: a whole 2x2x4 slice. The times are simulated.
32 devices in a mesh: section: 2 (over y), dp: 4 (over z), ctx: 4 (over x, core).
Axes of the slice: x: 2, y: 2, z: 4, core: 2. Of those that a mesh axis runs over, the one named last changes fastest.
Arguments:
- token_ids: int32 [1024], P('ctx'), may hold values from 0 to 511
- embedding: bfloat16 [512, 4096], P(None, 'dp'), may hold values from -6 to 6
- project_in: bfloat16 [2, 4096, 3, 4096], P('section', 'ctx', None, 'dp'), may hold values from -0.09375 to 0.09375
- short_taps: float32 [2, 3, 3, 4096], P('section', None, None, 'dp'), may hold values from -3.5 to 3.5
- filter_taps: float32 [2, 128, 4096], P('section', None, 'dp'), may hold values from -0.5 to 0.5
- decay_rates: float32 [2, 4096], P('section', 'dp'), may hold values from 0.5 to 4
- project_out: bfloat16 [2, 4096, 4096], P('section', 'dp', 'ctx'), may hold values from -0.09375 to 0.09375
- cotangent: bfloat16 [1024, 4096], P('ctx', 'dp'), may hold values from -0.1875 to 0.1875
Outputs:
- grad_project_in: float32 [2, 4096, 3, 4096], P('section', 'ctx', None, 'dp')
- grad_project_out: float32 [2, 4096, 4096], P('section', 'dp', 'ctx')
- grad_filter: float32 [2, 128, 4096], P('section', None, 'dp')
- grad_decay: float32 [2, 4096], P('section', 'dp')
- grad_short: float32 [2, 3, 3, 4096], P('section', None, None, 'dp')
All inputs are finite; a program needn't handle non-finite values.
Results may differ from a plain program's by a relative error of at most 0.03.
Values may be sent and summed in bfloat16 or wider, within the bound.
No kernel may reach another device: no remote copies, remote signals or barrier semaphores. Data moves between devices by JAX's collectives and lax.ppermute only.
A program may use at most 192 MiB of HBM per device.

v0:
```python
import functools

import jax
import jax.numpy as jnp
import numpy as np
from jax import lax
from jax.experimental import pallas as pl
from jax.experimental.pallas import tpu as pltpu
from jax.sharding import PartitionSpec as P

EPSILON = 1e-06
F32 = jnp.float32
BF16 = jnp.bfloat16


def dot(left, right):
    return jnp.dot(left, right, preferred_element_type=F32)


def dot_t(left, right):
    return lax.dot_general(left, right, (((1,), (1,)), ((), ())), preferred_element_type=F32)


def exact(left, right):
    return jnp.dot(left, right, preferred_element_type=F32, precision=lax.Precision.HIGHEST)


def pick(stack, index):
    return lax.dynamic_index_in_dim(stack, index, 0, keepdims=False)


def send(value, axes, route):
    sizes = [lax.axis_size(axis) for axis in axes]
    pairs = []
    for source, place in enumerate(np.ndindex(*sizes)):
        target = route(*place)
        if target is not None:
            pairs.append((source, int(np.ravel_multi_index(target, sizes))))
    return lax.ppermute(value, axes, pairs)


def ctx_xor(value, mask, sections):
    return send(
        value, ("section", "ctx"), lambda s, k: (s, k ^ mask) if s in sections else None
    )


def ctx_gather(value, sections):
    count = lax.axis_size("ctx")
    held = {0: value}
    bit = count // 2
    while bit:
        for r in list(held):
            held[r | bit] = ctx_xor(held[r], bit, sections)
        bit //= 2
    return [held[r] for r in range(count)]


def far_gather(value, sections):
    held = {0: value}
    bit = lax.axis_size("ctx") // 2
    while bit > 1:
        for r in list(held):
            held[r | bit] = ctx_xor(held[r], bit, sections)
        bit //= 2
    return held


def scatter_order(count):
    if count == 1:
        return [0]
    inner = scatter_order(count // 2)
    return [2 * r for r in inner] + [2 * r + 1 for r in inner]


def dp_gather(value, section):
    count = lax.axis_size("dp")
    pieces = [value]
    for _ in range(count - 1):
        pieces.append(
            send(
                pieces[-1],
                ("section", "dp"),
                lambda s, z: (s, (z + 1) % count) if s == section else None,
            )
        )
    return pieces


def cross_gather(shares, base, source, early, late=()):
    count = lax.axis_size("dp")
    me = lax.axis_index("dp")
    half = base.shape[0] // 2
    arrivals = [
        [
            send(
                pick(shares, (me + shift) % count)[start : start + half],
                ("section", "dp"),
                lambda s, z: (1 - s, (z + shift) % count) if s == source else None,
            )
            for shift in range(count)
        ]
        for start in (0, half)
    ]

    def total(index, values):
        start = index * half
        result = base[start : start + half].astype(F32)
        for value in values:
            result = result + value.astype(F32)
        return result.astype(BF16)

    part, *early = together(total(0, arrivals[0]), *early)
    first = dp_gather(part, 1 - source)
    first[1], *arrivals[1] = together(first[1], *arrivals[1])
    part, *late = together(total(1, arrivals[1]), *late)
    second = dp_gather(part, 1 - source)
    stack = jnp.stack([jnp.concatenate(pair, axis=0) for pair in zip(first, second)])
    return stack, early, late


def in_order(stack, me):
    return [pick(stack, (me - q) % stack.shape[0]) for q in range(stack.shape[0])]


def spectra(taps):
    freq = np.arange(taps)[:, None]
    time = np.arange(taps)[None, :]
    angle = np.pi * freq * time / taps
    nyquist = np.where(time % 2 == 0, 1.0, -1.0)
    forward = np.concatenate(
        [np.cos(angle), np.where(freq == 0, nyquist, -np.sin(angle))], axis=0
    )
    weight = np.where(freq == 0, 1.0, 2.0) / (2 * taps)
    inverse = np.concatenate(
        [weight * np.cos(angle), np.where(freq == 0, nyquist, -2 * np.sin(angle)) * np.where(freq == 0, weight, 1.0 / (2 * taps))],
        axis=0,
    ).T
    sign = np.where(np.arange(2 * taps) % taps % 2 == 0, 1.0, -1.0)
    return [jnp.asarray(m, BF16) for m in (forward, inverse, inverse * sign[None, :])]


def later(current, before, steps, row):
    return jnp.where(row < steps, pltpu.roll(before, steps, 0), pltpu.roll(current, steps, 0))


def sooner(current, after, steps, row):
    count = current.shape[0]
    return jnp.where(
        row >= count - steps,
        pltpu.roll(after, count - steps, 0),
        pltpu.roll(current, count - steps, 0),
    )


def kernel_spectrum(fwd_ref, kern_ref, row):
    tap_count = kern_ref.shape[0]
    kern = dot(fwd_ref[...], kern_ref[...].astype(BF16))
    real, imag = kern[:tap_count], kern[tap_count:]
    return real, jnp.where(row == 0, 0.0, imag), jnp.where(row == 0, imag, real)


def proj_block(proj_ref, m, b, tap_count):
    chunk, start = divmod(b * tap_count, proj_ref.shape[2])
    return proj_ref[chunk, m, start : start + tap_count, :].astype(F32)


def short_filter(taps_ref, m, current, before, row):
    return (
        taps_ref[m : m + 1, :] * current
        + taps_ref[3 + m : 4 + m, :] * later(current, before, 1, row)
        + taps_ref[6 + m : 7 + m, :] * later(current, before, 2, row)
    )


def lookup_kernel(
    tokens_ref, table_ref, taps_ref, kern_ref, fwd_ref, inv_ref,
    gated_ref, filt_ref, spec_ref, proj_ref,
):
    tap_count, vocab = kern_ref.shape[0], table_ref.shape[1]
    entry = lax.broadcasted_iota(jnp.int32, (tap_count, vocab), 1)
    for b in range(filt_ref.shape[0] // tap_count):
        here = pl.ds(b * tap_count, tap_count)
        chosen = (entry == tokens_ref[here, :]).astype(F32).astype(BF16)
        for m in range(3):
            proj_ref[0, m, here, :] = dot(chosen, table_ref[m]).astype(BF16)
    forward_kernel(
        proj_ref, taps_ref, kern_ref, fwd_ref, inv_ref, gated_ref, filt_ref, spec_ref
    )


def collect_kernel(
    tokens_ref, scale_ref, gg_ref, proj_ref, taps_ref, kern_ref, fwd_ref, inv_ref, filt_ref, spec_ref,
    table_ref, gkern_ref, gtaps_ref, grad_spec, gproj_ref,
):
    backward_kernel(
        gg_ref, proj_ref, taps_ref, kern_ref, fwd_ref, inv_ref, filt_ref, spec_ref,
        gproj_ref, gkern_ref, gtaps_ref, grad_spec,
    )
    _, vocab, _ = table_ref.shape
    seq = filt_ref.shape[0]
    entry = lax.broadcasted_iota(jnp.int32, (vocab, seq), 0)
    chosen = (entry == tokens_ref[...]).astype(F32).astype(BF16)
    for m in range(3):
        table_ref[m] = (dot(chosen, gproj_ref[0, m]) * scale_ref[...]).astype(BF16)


def forward_kernel(proj_ref, taps_ref, kern_ref, fwd_ref, inv_ref, gated_ref, filt_ref, spec_ref):
    tap_count, chans = kern_ref.shape
    blocks = filt_ref.shape[0] // tap_count
    row = lax.broadcasted_iota(jnp.int32, (tap_count, chans), 0)
    sign = jnp.where(row % 2 == 0, 1.0, -1.0)
    kr, ki, kn = kernel_spectrum(fwd_ref, kern_ref, row)
    zero = jnp.zeros((tap_count, chans), F32)
    before = [zero] * 3
    last_r, last_i = zero, zero
    for b in range(blocks):
        here = pl.ds(b * tap_count, tap_count)
        streams = []
        for m in range(3):
            current = proj_block(proj_ref, m, b, tap_count)
            streams.append(short_filter(taps_ref, m, current, before[m], row))
            before[m] = current
        part = dot(fwd_ref[...], (streams[1] * streams[2]).astype(BF16))
        pr, pi = part[:tap_count], part[tap_count:]
        wr = last_r + sign * pr
        wi = last_i + sign * pi
        last_r, last_i = pr, pi
        spec_ref[b, :tap_count, :] = wr.astype(BF16)
        spec_ref[b, tap_count:, :] = wi.astype(BF16)
        mixed = jnp.concatenate([wr * kr - wi * ki, wr * ki + wi * kn], axis=0)
        filtered = dot(inv_ref[...], mixed.astype(BF16))
        filt_ref[here, :] = filtered.astype(BF16)
        gated_ref[here, :] = (streams[0] * filtered).astype(BF16)


def backward_kernel(
    gg_ref, proj_ref, taps_ref, kern_ref, fwd_ref, inv_ref, filt_ref, spec_ref,
    gproj_ref, gkern_ref, gtaps_ref, grad_spec,
):
    tap_count, chans = kern_ref.shape
    blocks = filt_ref.shape[0] // tap_count
    row = lax.broadcasted_iota(jnp.int32, (tap_count, chans), 0)
    sign = jnp.where(row % 2 == 0, 1.0, -1.0)
    kr, ki, kn = kernel_spectrum(fwd_ref, kern_ref, row)
    zero = jnp.zeros((tap_count, chans), F32)
    sum_r, sum_i = zero, zero
    last = zero
    for b in range(blocks):
        here = pl.ds(b * tap_count, tap_count)
        current = proj_block(proj_ref, 0, b, tap_count)
        query = short_filter(taps_ref, 0, current, last, row)
        last = current
        part = dot(fwd_ref[...], (gg_ref[here, :].astype(F32) * query).astype(BF16))
        grad_spec[b] = part
        gr, gi = sign * part[:tap_count], sign * part[tap_count:]
        wr = spec_ref[b, :tap_count, :].astype(F32)
        wi = spec_ref[b, tap_count:, :].astype(F32)
        rr, ii = wr * gr, wi * gi
        sum_r = sum_r + jnp.where(row == 0, rr, rr + ii)
        sum_i = sum_i + jnp.where(row == 0, ii, wr * gi - wi * gr)
    gkern_ref[...] = exact(
        inv_ref[...].astype(F32), jnp.concatenate([sum_r, sum_i], axis=0)
    )
    after = [zero] * 3
    next_r, next_i = zero, zero
    sums = [jnp.zeros((1, chans), F32) for _ in range(9)]
    for b in reversed(range(blocks)):
        chunk, start = divmod(b * tap_count, proj_ref.shape[2])
        here = pl.ds(b * tap_count, tap_count)
        gr, gi = grad_spec[b, :tap_count, :], grad_spec[b, tap_count:, :]
        vr, vi = gr + sign * next_r, gi + sign * next_i
        next_r, next_i = gr, gi
        mixed = jnp.concatenate([vr * kr + vi * ki, vi * kn - vr * ki], axis=0)
        grad_prod = dot(inv_ref[...], mixed.astype(BF16))
        shifts, shorts = [], []
        for m in range(3):
            current = proj_block(proj_ref, m, b, tap_count)
            before = proj_block(proj_ref, m, b - 1, tap_count) if b else zero
            shifts.append([current, later(current, before, 1, row), later(current, before, 2, row)])
            if m:
                shorts.append(sum(taps_ref[3 * j + m : 3 * j + m + 1, :] * shifts[m][j] for j in range(3)))
        grads = [
            gg_ref[here, :].astype(F32) * filt_ref[here, :].astype(F32),
            grad_prod * shorts[1],
            grad_prod * shorts[0],
        ]
        for m in range(3):
            grad = grads[m]
            out = (
                taps_ref[m : m + 1, :] * grad
                + taps_ref[3 + m : 4 + m, :] * sooner(grad, after[m], 1, row)
                + taps_ref[6 + m : 7 + m, :] * sooner(grad, after[m], 2, row)
            )
            after[m] = grad
            gproj_ref[chunk, m, start : start + tap_count, :] = out.astype(BF16)
            for j in range(3):
                sums[3 * j + m] = sums[3 * j + m] + jnp.sum(
                    grad * shifts[m][j], axis=0, keepdims=True
                )
    for index in range(9):
        gtaps_ref[index : index + 1, :] = sums[index]


PARAMS = pltpu.CompilerParams(vmem_limit_bytes=56 * 1024 * 1024)


def conv_forward(proj, taps, kern, matrices, tokens=None):
    tap_count, chans = kern.shape
    seq = proj.shape[0] * proj.shape[2] if tokens is None else tokens.shape[0]
    results = [
        jax.ShapeDtypeStruct((seq, chans), BF16),
        jax.ShapeDtypeStruct((seq, chans), BF16),
        jax.ShapeDtypeStruct((seq // tap_count, 2 * tap_count, chans), BF16),
    ]
    operands = (proj, taps, kern, matrices[0], matrices[2])
    if tokens is not None:
        results.append(jax.ShapeDtypeStruct((1, 3, seq, chans), BF16))
        operands = (tokens[:, None], *operands)
    return pl.pallas_call(
        forward_kernel if tokens is None else lookup_kernel,
        out_shape=results,
        compiler_params=PARAMS,
        name="conv_forward",
    )(*operands)


def conv_backward(gg, proj, taps, kern, matrices, saved, tokens=None, scale=None):
    tap_count, chans = kern.shape
    seq = gg.shape[0]
    scratch = [pltpu.VMEM((seq // tap_count, 2 * tap_count, chans), F32)]
    operands = (gg, proj, taps, kern, matrices[0], matrices[1], *saved)
    first = jax.ShapeDtypeStruct(proj.shape, BF16)
    if tokens is not None:
        first = jax.ShapeDtypeStruct((3, scale.shape[0], chans), BF16)
        scratch.append(pltpu.VMEM(proj.shape, BF16))
        operands = (tokens[None, :], scale, *operands)
    return pl.pallas_call(
        backward_kernel if tokens is None else collect_kernel,
        out_shape=(
            first,
            jax.ShapeDtypeStruct(kern.shape, F32),
            jax.ShapeDtypeStruct((9, chans), F32),
        ),
        scratch_shapes=scratch,
        compiler_params=PARAMS,
        name="conv_backward",
    )(*operands)


def table_projection(table, weights, ctx, order, kind):
    vocab, feats = table.shape
    sub = weights.shape[2] // lax.axis_size("ctx")
    if sub % 128:
        columns = jnp.stack(
            [lax.dynamic_slice_in_dim(weights, (ctx ^ r) * sub, sub, 2) for r in order]
        )
        return jnp.einsum("vd,rmdc->rmvc", table, columns, preferred_element_type=F32).astype(kind)

    def kernel(where_ref, table_ref, weights_ref, out_ref):
        for m in range(3):
            out_ref[0, m] = dot(table_ref[...], weights_ref[m]).astype(kind)

    return pl.pallas_call(
        kernel,
        grid_spec=pltpu.PrefetchScalarGridSpec(
            num_scalar_prefetch=1,
            grid=(len(order),),
            in_specs=[
                pl.BlockSpec((vocab, feats), lambda r, where: (0, 0)),
                pl.BlockSpec((3, feats, sub), lambda r, where: (0, 0, where[r])),
            ],
            out_specs=pl.BlockSpec((1, 3, vocab, sub), lambda r, where: (r, 0, 0, 0)),
        ),
        out_shape=jax.ShapeDtypeStruct((len(order), 3, vocab, sub), kind),
        compiler_params=PARAMS,
        name="table_projection",
    )(jnp.stack([ctx ^ r for r in order]), table, weights)


def input_projection(rows_in, pieces, ctx):
    rows, full_width = rows_in.shape
    feats, chans = pieces[0].shape[1:]
    count = len(pieces)
    sub = chans // count

    def kernel(ctx_ref, rows_ref, *refs):
        weights, (normed_ref, proj_ref, scale_ref) = refs[:count], refs[count:]

        @pl.when(pl.program_id(0) == 0)
        def _():
            total = jnp.zeros((rows, 1), F32)
            for q in range(count):
                part = rows_ref[:, q * feats : (q + 1) * feats].astype(F32)
                total = total + jnp.sum(part * part, axis=1, keepdims=True)
            scale_ref[...] = lax.rsqrt(total / full_width + EPSILON)
            for q in range(count):
                part = rows_ref[:, q * feats : (q + 1) * feats].astype(F32)
                normed_ref[q] = (part * scale_ref[...]).astype(BF16)

        total = jnp.zeros((rows, chans), F32)
        for r in range(count):
            start = pl.multiple_of((ctx_ref[0] ^ r) * feats, feats)
            total = total + dot(rows_ref[:, pl.ds(start, feats)], weights[r][0])
        total = (total * scale_ref[...]).astype(BF16)
        for q in range(count):
            proj_ref[q, 0] = total[:, q * sub : (q + 1) * sub]

    return pl.pallas_call(
        kernel,
        grid_spec=pltpu.PrefetchScalarGridSpec(
            num_scalar_prefetch=1,
            grid=(3,),
            in_specs=[pl.BlockSpec((rows, full_width), lambda m, ctx: (0, 0))]
            + [pl.BlockSpec((1, feats, chans), lambda m, ctx: (m, 0, 0))] * count,
            out_specs=[
                pl.BlockSpec((count, rows, feats), lambda m, ctx: (0, 0, 0)),
                pl.BlockSpec((count, 1, rows, sub), lambda m, ctx: (0, m, 0, 0)),
                pl.BlockSpec((rows, 1), lambda m, ctx: (0, 0)),
            ],
        ),
        out_shape=(
            jax.ShapeDtypeStruct((count, rows, feats), BF16),
            jax.ShapeDtypeStruct((count, 3, rows, sub), BF16),
            jax.ShapeDtypeStruct((rows, 1), F32),
        ),
        compiler_params=PARAMS,
        name="input_projection",
    )(ctx[None], rows_in, *pieces)


def input_gradient(gproj, pieces, rows_in, scale, ctx):
    rows, full_width = rows_in.shape
    feats, chans = pieces[0].shape[1:]
    count = len(pieces)
    sub = chans // count
    tile = min(256, feats)
    steps = feats // tile

    def kernel(ctx_ref, gproj_ref, rows_ref, scale_ref, *refs):
        weights, (out_ref, flat, grads) = refs[:count], refs[count:]
        step = pl.program_id(0)

        @pl.when(step == 0)
        def _():
            for m in range(3):
                for q in range(count):
                    flat[m, :, q * sub : (q + 1) * sub] = gproj_ref[q, m]

        columns = pl.ds(pl.multiple_of(step * tile, tile), tile)
        for r in range(count):
            total = dot_t(flat[0], weights[r][0])
            for m in (1, 2):
                total = total + dot_t(flat[m], weights[r][m])
            grads[ctx_ref[0] ^ r, :, columns] = total * scale_ref[...]

        @pl.when(step == steps - 1)
        def _():
            stat = jnp.zeros((rows, 1), F32)
            for q in range(count):
                part = rows_ref[:, q * feats : (q + 1) * feats].astype(F32)
                stat = stat + jnp.sum(part * grads[q], axis=1, keepdims=True)
            stat = stat * scale_ref[...] * scale_ref[...] / full_width
            for q in range(count):
                part = rows_ref[:, q * feats : (q + 1) * feats].astype(F32)
                out_ref[q] = (grads[q] - part * stat).astype(BF16)

    return pl.pallas_call(
        kernel,
        grid_spec=pltpu.PrefetchScalarGridSpec(
            num_scalar_prefetch=1,
            grid=(steps,),
            in_specs=[
                pl.BlockSpec(gproj.shape, lambda t, ctx: (0, 0, 0, 0)),
                pl.BlockSpec((rows, full_width), lambda t, ctx: (0, 0)),
                pl.BlockSpec((rows, 1), lambda t, ctx: (0, 0)),
            ]
            + [pl.BlockSpec((3, tile, chans), lambda t, ctx: (0, t, 0))] * count,
            out_specs=pl.BlockSpec((count, rows, feats), lambda t, ctx: (0, 0, 0)),
            scratch_shapes=[
                pltpu.VMEM((3, rows, chans), BF16),
                pltpu.VMEM((count, rows, feats), F32),
            ],
        ),
        out_shape=jax.ShapeDtypeStruct((count, rows, feats), BF16),
        compiler_params=PARAMS,
        name="input_gradient",
    )(ctx[None], gproj, rows_in, scale, *pieces)


def grad_in_kernel(left, pieces, ctx):
    feats, depth = left.shape
    count, sub = len(pieces), pieces[0].shape[2]
    if sub % 128:
        columns = jnp.concatenate([pick(jnp.stack(pieces), ctx ^ q) for q in range(count)], axis=2)
        columns = columns[:3]
        return jnp.einsum("dk,mkc->mdc", left, columns, preferred_element_type=F32)

    tile = min(256, feats)

    def kernel(ctx_ref, left_ref, *refs):
        out_ref = refs[count]
        for r in range(count):
            columns = pl.ds(pl.multiple_of((ctx_ref[0] ^ r) * sub, sub), sub)
            for m in range(3):
                out_ref[m, :, columns] = dot(left_ref[...], refs[r][m])

    return pl.pallas_call(
        kernel,
        grid_spec=pltpu.PrefetchScalarGridSpec(
            num_scalar_prefetch=1,
            grid=(feats // tile,),
            in_specs=[pl.BlockSpec((tile, depth), lambda t, ctx: (t, 0))]
            + [pl.BlockSpec((3, depth, sub), lambda t, ctx: (0, 0, 0))] * count,
            out_specs=pl.BlockSpec((3, tile, sub * count), lambda t, ctx: (0, t, 0)),
        ),
        out_shape=jax.ShapeDtypeStruct((3, feats, sub * count), F32),
        compiler_params=PARAMS,
        name="grad_project_in",
    )(ctx[None], left, *pieces)


def grad_out_kernel(pieces, right, ctx):
    depth, feats = right.shape
    count, sub = len(pieces), pieces[0].shape[1]

    def kernel(where_ref, right_ref, *refs):
        out_ref = refs[count]
        for r in range(count):

            @pl.when(pl.program_id(0) == r)
            def _():
                out_ref[...] = lax.dot_general(
                    refs[r][...],
                    right_ref[...],
                    (((0,), (0,)), ((), ())),
                    preferred_element_type=F32,
                )

    return pl.pallas_call(
        kernel,
        grid_spec=pltpu.PrefetchScalarGridSpec(
            num_scalar_prefetch=1,
            grid=(count,),
            in_specs=[pl.BlockSpec((depth, feats), lambda r, where: (0, 0))]
            + [pl.BlockSpec((depth, sub), lambda r, where: (0, 0))] * count,
            out_specs=pl.BlockSpec((sub, feats), lambda r, where: (where[r], 0)),
        ),
        out_shape=jax.ShapeDtypeStruct((sub * count, feats), F32),
        compiler_params=PARAMS,
        name="grad_project_out",
    )(jnp.stack([ctx ^ r for r in range(count)]), right, *pieces)


def together(*values):
    return lax.optimization_barrier(values)


def projection_specs(pieces, tile):
    specs, operands = [], []
    for piece in pieces:
        for array, place in piece:
            height = array.shape[0] if place is None else array.shape[0] // 2
            specs.append(pl.BlockSpec((height, tile), functools.partial(place_of, place or 0)))
            operands.append(array)
    return specs, operands


def place_of(row, t, ctx):
    return (row, t)


def output_projection(gated, pieces, ctx):
    count, rows, sub = gated.shape
    chans, feats = count * sub, pieces[0][0][0].shape[1]
    half, tile = chans // 2, min(256, feats)
    specs, operands = projection_specs(pieces, tile)

    def kernel(ctx_ref, gated_ref, *refs):
        weights, (out_ref, flat) = refs[: 2 * count], refs[2 * count :]

        @pl.when(pl.program_id(0) == 0)
        def _():
            for q in range(count):
                flat[:, q * sub : (q + 1) * sub] = gated_ref[q]

        for r in range(count):
            total = dot(flat[:, :half], weights[2 * r][...])
            total = total + dot(flat[:, half:], weights[2 * r + 1][...])
            out_ref[ctx_ref[0] ^ r] = total.astype(BF16)

    return pl.pallas_call(
        kernel,
        grid_spec=pltpu.PrefetchScalarGridSpec(
            num_scalar_prefetch=1,
            grid=(feats // tile,),
            in_specs=[pl.BlockSpec(gated.shape, lambda t, ctx: (0, 0, 0))] + specs,
            out_specs=pl.BlockSpec((count, rows, tile), lambda t, ctx: (0, 0, t)),
            scratch_shapes=[pltpu.VMEM((rows, chans), BF16)],
        ),
        out_shape=jax.ShapeDtypeStruct((count, rows, feats), BF16),
        compiler_params=PARAMS,
        name="output_projection",
    )(ctx[None], gated, *operands)


def gated_gradient(grads, pieces, ctx):
    count, rows, feats = grads.shape
    chans = pieces[0][0][0].shape[0]
    half, tile, sub = chans // 2, min(256, feats), chans // count
    specs, operands = projection_specs(pieces, tile)

    def kernel(ctx_ref, grads_ref, *refs):
        weights, (out_ref, total) = refs[: 2 * count], refs[2 * count :]
        step = pl.program_id(0)

        @pl.when(step == 0)
        def _():
            total[...] = jnp.zeros_like(total)

        for side in range(2):
            part = dot_t(grads_ref[ctx_ref[0]], weights[side][...])
            for r in range(1, count):
                part = part + dot_t(grads_ref[ctx_ref[0] ^ r], weights[2 * r + side][...])
            total[:, side * half : (side + 1) * half] += part

        @pl.when(step == feats // tile - 1)
        def _():
            for q in range(count):
                out_ref[q] = total[:, q * sub : (q + 1) * sub].astype(BF16)

    return pl.pallas_call(
        kernel,
        grid_spec=pltpu.PrefetchScalarGridSpec(
            num_scalar_prefetch=1,
            grid=(feats // tile,),
            in_specs=[pl.BlockSpec((count, rows, tile), lambda t, ctx: (0, 0, t))] + specs,
            out_specs=pl.BlockSpec((count, rows, sub), lambda t, ctx: (0, 0, 0)),
            scratch_shapes=[pltpu.VMEM((rows, chans), F32)],
        ),
        out_shape=jax.ShapeDtypeStruct((count, rows, sub), BF16),
        compiler_params=PARAMS,
        name="gated_gradient",
    )(ctx[None], grads, *operands)


def ctx_swap_in(value, section):
    me = lax.axis_index("ctx")
    count = value.shape[0]
    came = [pick(value, me)]
    for r in range(1, count):
        came.append(ctx_xor(pick(value, me ^ r), r, (section,)))
    came = jnp.stack(came)
    return [pick(came, me ^ q) for q in range(count)]


def ctx_swap(value):
    return lax.all_to_all(value, "ctx", split_axis=0, concat_axis=0, tiled=True)


def local(
    token_ids, embedding, project_in, short_taps, filter_taps, decay_rates, project_out, cotangent
):
    n_ctx, n_dp = lax.axis_size("ctx"), lax.axis_size("dp")
    sec, dp, ctx = (lax.axis_index(axis) for axis in ("section", "dp", "ctx"))
    first = sec == 0
    rows, vocab = token_ids.shape[0], embedding.shape[0]
    seq = rows * n_ctx
    weights_in = jnp.transpose(project_in[0], (1, 0, 2))
    weights_out = project_out[0]
    feats, chans = weights_out.shape[1], weights_out.shape[0]
    full_width = feats * n_ctx
    sub = chans // n_ctx

    if n_ctx == n_dp:
        half = vocab // 2
        mine = lax.dynamic_slice_in_dim(embedding, sec * half, half, 0)
        came = []
        for i in range(1, n_dp):
            shifts = (i, i % (n_dp - 1) + 1)
            came.append(
                send(
                    mine,
                    ("section", "dp", "ctx"),
                    lambda s, z, k: (0, (z + shifts[s]) % n_dp, k) if z == k else None,
                )
            )
        offset = (dp - ctx) % n_dp
        low, high = embedding[:half], embedding[half:]
        for i in range(1, n_dp):
            low = jnp.where(offset == i, came[i - 1], low)
            high = jnp.where(offset == i % (n_dp - 1) + 1, came[i - 1], high)
        table = jnp.concatenate([low, high], axis=0)
    else:
        table = lax.dynamic_slice_in_dim(
            lax.all_gather(embedding, "dp", axis=1, tiled=True), ctx * feats, feats, 1
        )
    half = chans // 2
    out_far = [far_gather(weights_out[start : start + half], (0,)) for start in (0, half)]
    far = sorted(out_far[0])[1:]
    table, *late = together(table, *[out_far[0][r] for r in far])
    out_far[0].update(zip(far, late))
    table_float = table.astype(F32)
    squares = jnp.sum(table_float * table_float, axis=1)
    tokens = token_ids.astype(F32)[None]
    held = [0]
    bit = n_ctx // 2
    while bit:
        came = ctx_xor(jnp.concatenate([squares, tokens.reshape(-1)]), bit, (0,))
        squares = squares + came[:vocab]
        tokens = jnp.concatenate([tokens, came[vocab:].reshape(-1, rows)], axis=0)
        held += [r | bit for r in held]
        bit //= 2
    table_inv = lax.rsqrt(squares[:, None] / full_width + EPSILON)
    tokens = jnp.stack([tokens[held.index(r)] for r in range(n_ctx)])
    tokens = jnp.concatenate([pick(tokens, ctx ^ q) for q in range(n_ctx)]).astype(jnp.int32)

    def own(value):
        return lax.dynamic_slice_in_dim(value, ctx * sub, sub, value.ndim - 1)

    taps = own(short_taps[0]).reshape(9, sub)
    filters = own(filter_taps[0])
    tap_count = filters.shape[0]
    positions = jnp.arange(tap_count).astype(F32)[:, None]
    damping = jnp.exp(-own(decay_rates) * positions / tap_count)
    kern = filters * damping
    matrices = spectra(tap_count)

    vocabulary = jnp.arange(vocab, dtype=jnp.int32)[None, :]
    first_input = dot((token_ids[:, None] == vocabulary).astype(BF16), embedding)

    in_far = far_gather(weights_in, (1,))

    order = scatter_order(n_ctx)
    kept = order[: n_ctx // 2]
    sent = table_projection(table, weights_in, ctx, [r | 1 for r in kept], BF16)
    arrived = ctx_xor(sent, 1, (0,))
    partial = table_projection(table, weights_in, ctx, kept, F32) + arrived.astype(F32)
    partial, *late = together(partial, *[out_far[1][r] for r in far])
    out_far[1].update(zip(far, late))
    bit = 2
    while bit < n_ctx:
        stays, gone = jnp.split(partial, 2, axis=0)
        partial = stays + ctx_xor(gone.astype(BF16), bit, (0,)).astype(F32)
        bit *= 2
    table_proj = (partial[0] * table_inv).astype(BF16)
    out_pieces = [[(weights_out, 0), (weights_out, 1)]]
    for r in sorted(out_far[0]):
        if r:
            out_pieces.append([(side[r], None) for side in out_far])
        out_pieces.append([(ctx_xor(side[r], 1, (0,)), None) for side in out_far])
    gated_0, *saved_0, proj_0 = conv_forward(table_proj, taps, kern, matrices, tokens)
    cot_stack = jnp.stack(dp_gather(cotangent, 1))
    gated_0, cot_stack = together(gated_0, cot_stack)
    gated_rows = jnp.stack(ctx_swap_in(gated_0.reshape(n_ctx, rows, sub), 0))
    shares = output_projection(gated_rows, out_pieces, ctx)
    middle_stack, (gated_0,), late = cross_gather(
        shares, first_input, 0, [gated_0], [in_far[r] for r in far]
    )
    gated_all_0 = ctx_gather(gated_0, (0,))

    in_far.update(zip(far, late))
    in_pieces = []
    for r in sorted(in_far):
        in_pieces += [in_far[r], ctx_xor(in_far[r], 1, (1,))]
    weights_late, *_ = together(weights_out, *late)
    late_far = far_gather(weights_late, (1,))
    middle_all = jnp.concatenate(in_order(middle_stack, dp), axis=1)
    normed, proj_rows, scale = input_projection(middle_all, in_pieces, ctx)
    proj_rows, *late = together(proj_rows, *[late_far[r] for r in far])
    late_far.update(zip(far, late))
    out_late = []
    for r in sorted(late_far):
        out_late += [late_far[r], ctx_xor(late_far[r], 1, (1,))]
    out_late = [[(piece, 0), (piece, 1)] for piece in out_late]
    proj_1 = ctx_swap(proj_rows)
    gated_1, *saved_1 = conv_forward(proj_1, taps, kern, matrices)

    cot_parts = jnp.stack(in_order(cot_stack, dp))
    gated_grad = ctx_swap(gated_gradient(cot_parts, out_late, ctx)).reshape(seq, sub)
    gproj_1, gkern_1, gtaps_1 = conv_backward(
        gated_grad, proj_1, taps, kern, matrices, saved_1
    )
    gproj_1, *gated_all_0 = together(gproj_1, *gated_all_0)
    gproj_rows = ctx_swap(gproj_1)
    shares = input_gradient(gproj_rows, in_pieces, middle_all, scale, ctx)
    back_stack, (normed, gproj_1, gated_1), _ = cross_gather(
        shares, cotangent, 1, [normed, gproj_1, gated_1]
    )

    normed_cols = jnp.concatenate([part.T for part in ctx_swap_in(normed, 1)], axis=1)
    gproj_1 = gproj_1.transpose(1, 0, 2, 3).reshape(3, seq, sub)
    gproj_all = ctx_gather(jnp.concatenate([gproj_1, gated_1[None]]), (1,))
    gated_all = [jnp.where(first, a, b[3]) for a, b in zip(gated_all_0, gproj_all)]

    back_stack, normed_cols, *rest = together(back_stack, normed_cols, *gproj_all, *gated_all)
    gproj_all, gated_all = rest[:n_ctx], rest[n_ctx:]
    back_parts = jnp.stack(in_order(back_stack, dp))
    gated_grad = ctx_swap(gated_gradient(back_parts, out_pieces, ctx)).reshape(seq, sub)
    table_grad, gkern_0, gtaps_0 = conv_backward(
        gated_grad, proj_0, taps, kern, matrices, saved_0, tokens, table_inv
    )

    grads = jnp.where(first, back_parts, cot_parts)
    grad_cols = ctx_swap(grads).reshape(seq, feats)
    grad_out = grad_out_kernel(gated_all, grad_cols, ctx)
    table_pieces = ctx_gather(table_grad, (0,))
    grad_in = lax.cond(
        first,
        lambda: grad_in_kernel(table.T, table_pieces, ctx),
        lambda: grad_in_kernel(normed_cols, gproj_all, ctx),
    )

    gkern = jnp.where(first, gkern_0, gkern_1)
    gtaps = jnp.where(first, gtaps_0, gtaps_1)
    gdecay = -jnp.sum(gkern * kern * positions, axis=0, keepdims=True) / tap_count
    small = jnp.concatenate([gkern * damping, gdecay, gtaps], axis=0)
    small = jnp.stack(ctx_gather(small, (0, 1)))
    small = jnp.concatenate([pick(small, ctx ^ q) for q in range(n_ctx)], axis=1)
    return (
        jnp.transpose(grad_in, (1, 0, 2))[None],
        grad_out[None],
        small[:tap_count][None],
        small[tap_count][None],
        small[tap_count + 1 :].reshape(1, 3, 3, chans),
    )


def solution(mesh):
    return jax.shard_map(
        local,
        mesh=mesh,
        in_specs=(
            P("ctx"),
            P(None, "dp"),
            P("section", "ctx", None, "dp"),
            P("section", None, None, "dp"),
            P("section", None, "dp"),
            P("section", "dp"),
            P("section", "dp", "ctx"),
            P("ctx", "dp"),
        ),
        out_specs=(
            P("section", "ctx", None, "dp"),
            P("section", "dp", "ctx"),
            P("section", None, "dp"),
            P("section", "dp"),
            P("section", None, None, "dp"),
        ),
        check_vma=False,
    )
```

profile of v0, /device:TPU:1, one launch (start us, length us, event | category | flops | bytes accessed | tf_op | source)
XLA Modules:
  0.0 567.2 jit_solution(10587387237317154998)
XLA Ops:
  22.7 8.1 %collective-permute-done.3.refs_4_ = bf16[512,1024]{1,0:T(8,128)(2,1)S(1)} collective-permute-done((bf16[512,1024]{1,0:T(8,128)(2,1)}, bf16[512,1024]{1,0:T(8,128)(2,1)S(1)}, u32[]{:S(2)}, u32[]{:S(2)}) %collective-permute-start.3) | collective-permute-done | bytes 1048608 | tf_op jit(solution)/shard_map/ppermute | solution.py:39
  40.6 19.0 %collective-permute-start.7 = (bf16[512,1024]{1,0:T(8,128)(2,1)}, bf16[512,1024]{1,0:T(8,128)(2,1)}, u32[]{:S(2)}, u32[]{:S(2)}) collective-permute-start(bf16[512,1024]{1,0:T(8,128)(2,1)} %get-tuple-element.242), channel_id=1, source_target_pairs={{0,2},{1,3},{2,0},{3,1},{4,6},{5,7},{6,4},{7,5},{8,10},{9,11},{10,... | collective-permute-start | bytes 3145736 | tf_op jit(solution)/shard_map/ppermute | solution.py:39
  73.7 9.9 %collective-permute-done.4 = f32[768]{0:T(1024)S(1)} collective-permute-done((f32[768]{0:T(1024)S(1)}, f32[768]{0:T(1024)S(1)}, u32[]{:S(2)}, u32[]{:S(2)}) %collective-permute-start.4) | collective-permute-done | bytes 3104 | tf_op jit(solution)/shard_map/ppermute | solution.py:39
  99.1 13.6 %collective-permute-done.8 = bf16[1,3,512,256]{3,2,1,0:T(8,128)(2,1)} collective-permute-done((bf16[1,3,512,256]{3,2,1,0:T(8,128)(2,1)}, bf16[1,3,512,256]{3,2,1,0:T(8,128)(2,1)}, u32[]{:S(2)}, u32[]{:S(2)}) %collective-permute-start.8) | collective-permute-done | bytes 786464 | tf_op jit(solution)/shard_map/ppermute | solution.py:39
  142.1 7.1 %output_projection.1 = bf16[4,256,1024]{2,1,0:T(8,128)(2,1)} custom-call(s32[1]{0:T(128)} %bitcast.3.ctx_ref, bf16[4,256,256]{2,1,0:T(8,128)(2,1)} %pad_maximum_fusion.13.gated_ref, bf16[1024,1024]{1,0:T(8,128)(2,1)} %bitcast.170, bf16[1024,1024]{1,0:T(8,128)(2,1)} %bitcast.171, bf16[512,1024]{1,0:T(8,128)(2,1)} %collective-permute-done.15.refs_2_, ...), custom_call_target="tpu_custom_call" | custom-call | tf_op jit(solution)/shard_map/output_projection/pallas_call | solution.py:592
  156.7 11.2 %collective-permute-done.19 = bf16[128,1024]{1,0:T(8,128)(2,1)S(1)} collective-permute-done((bf16[128,1024]{1,0:T(8,128)(2,1)S(1)}, bf16[128,1024]{1,0:T(8,128)(2,1)S(1)}, u32[]{:S(2)}, u32[]{:S(2)}) %collective-permute-start.19) | collective-permute-done | bytes 262176 | tf_op jit(solution)/shard_map/ppermute | solution.py:39
  178.2 6.5 %collective-permute-start.27 = (bf16[128,1024]{1,0:T(8,128)(2,1)S(1)}, bf16[128,1024]{1,0:T(8,128)(2,1)S(1)}, u32[]{:S(2)}, u32[]{:S(2)}) collective-permute-start(bf16[128,1024]{1,0:T(8,128)(2,1)S(1)} %get-tuple-element.230), channel_id=1, source_target_pairs={{0,28},{4,16},{8,20},{12,24},{1,29},{5,17},{9,21},{13,25},{2,30},{... | collective-permute-start | bytes 786440 | tf_op jit(solution)/shard_map/ppermute | solution.py:39
  185.0 9.0 %collective-permute-done.24 = bf16[128,1024]{1,0:T(8,128)(2,1)S(1)} collective-permute-done((bf16[128,1024]{1,0:T(8,128)(2,1)S(1)}, bf16[128,1024]{1,0:T(8,128)(2,1)S(1)}, u32[]{:S(2)}, u32[]{:S(2)}) %collective-permute-start.24) | collective-permute-done | bytes 262176 | tf_op jit(solution)/shard_map/ppermute | solution.py:39
  217.1 15.5 %input_projection.1 = (bf16[4,256,1024]{2,1,0:T(8,128)(2,1)}, bf16[4,3,256,256]{3,2,1,0:T(8,128)(2,1)}, f32[256,1]{1,0:T(8,128)}) custom-call(s32[1]{0:T(128)} %bitcast.3.ctx_ref, bf16[256,4096]{1,0:T(8,128)(2,1)} %pad_maximum_fusion.3.rows_ref, bf16[3,1024,1024]{2,1,0:T(8,128)(2,1)} %bitcast.182, bf16[3,1024,1024]{2,1,0:T(8,128)(2,1)} %collective-permute-done.35.refs_1_, ...), custom_call_target="tpu_custom_call" | custom-call | tf_op jit(solution)/shard_map/input_projection/pallas_call | solution.py:409
  247.9 23.0 %collective-permute-done.40 = bf16[1024,256]{1,0:T(8,128)(2,1)} collective-permute-done((bf16[1024,256]{1,0:T(8,128)(2,1)}, bf16[1024,256]{1,0:T(8,128)(2,1)}, u32[]{:S(2)}, u32[]{:S(2)}) %collective-permute-start.40) | collective-permute-done | bytes 524320 | tf_op jit(solution)/shard_map/ppermute | solution.py:39
  275.3 6.8 %gated_gradient.2 = bf16[4,256,256]{2,1,0:T(8,128)(2,1)} custom-call(s32[1]{0:T(128)} %bitcast.3.ctx_ref, bf16[4,256,1024]{2,1,0:T(8,128)(2,1)} %pad_maximum_fusion.1.grads_ref, bf16[1024,1024]{1,0:T(8,128)(2,1)} %bitcast.172, bf16[1024,1024]{1,0:T(8,128)(2,1)} %bitcast.173, bf16[1024,1024]{1,0:T(8,128)(2,1)} %collective-permute-done.29.refs_2_.refs_3_, ...), custom_call_target="tpu_custom_call" | custom-call | tf_op jit(solution)/shard_map/gated_gradient/pallas_call | solution.py:632
  294.3 7.5 %conv_backward.2 = (bf16[4,3,256,256]{3,2,1,0:T(8,128)(2,1)}, f32[128,256]{1,0:T(8,128)}, f32[9,256]{1,0:T(8,128)}) custom-call(bf16[1024,256]{1,0:T(8,128)(2,1)} %bitcast.189, bf16[4,3,256,256]{3,2,1,0:T(8,128)(2,1)} %all-to-all-done.1.proj_ref, f32[9,256]{1,0:T(8,128)} %reshape.194.taps_ref, f32[128,256]{1,0:T(8,128)} %bitcast_multiply_fusion.1.kern_ref, ...), custom_call_target="tpu_custom_call" | custom-call | tf_op jit(solution)/shard_map/conv_backward/pallas_call | solution.py:338
  301.8 24.5 %all_to_all.25.gproj_ref = bf16[4,3,256,256]{3,2,1,0:T(8,128)(2,1)} all-to-all(bf16[4,3,256,256]{3,2,1,0:T(8,128)(2,1)} %get-tuple-element.136), channel_id=1, replica_groups=mesh['section'=2,'dp'=4,'ctx'=4] {'ctx'}, dimensions={0} | all-to-all | bytes 3145728 | tf_op jit(solution)/shard_map/all_to_all | solution.py:658
  326.4 15.1 %input_gradient.1 = bf16[4,256,1024]{2,1,0:T(8,128)(2,1)} custom-call(s32[1]{0:T(128)} %bitcast.3.ctx_ref, bf16[4,3,256,256]{3,2,1,0:T(8,128)(2,1)} %all_to_all.25.gproj_ref, bf16[256,4096]{1,0:T(8,128)(2,1)} %pad_maximum_fusion.3.rows_ref, f32[256,1]{1,0:T(8,128)} %get-tuple-element.126.scale_ref, bf16[3,1024,1024]{2,1,0:T(8,128)(2,1)} %bitcast.183, ...), custom_call_target="tpu_custom_call" | custom-call | tf_op jit(solution)/shard_map/input_gradient/pallas_call | solution.py:468
  348.6 28.4 %collective-permute-done.42 = bf16[128,1024]{1,0:T(8,128)(2,1)S(1)} collective-permute-done((bf16[128,1024]{1,0:T(8,128)(2,1)S(1)}, bf16[128,1024]{1,0:T(8,128)(2,1)S(1)}, u32[]{:S(2)}, u32[]{:S(2)}) %collective-permute-start.42) | collective-permute-done | bytes 262176 | tf_op jit(solution)/shard_map/ppermute | solution.py:39
  385.8 20.9 %collective-permute-done.47 = bf16[128,1024]{1,0:T(8,128)(2,1)S(1)} collective-permute-done((bf16[128,1024]{1,0:T(8,128)(2,1)S(1)}, bf16[128,1024]{1,0:T(8,128)(2,1)S(1)}, u32[]{:S(2)}, u32[]{:S(2)}) %collective-permute-start.47) | collective-permute-done | bytes 262176 | tf_op jit(solution)/shard_map/ppermute | solution.py:39
  462.9 6.8 %gated_gradient.3 = bf16[4,256,256]{2,1,0:T(8,128)(2,1)} custom-call(s32[1]{0:T(128)} %bitcast.3.ctx_ref, bf16[4,256,1024]{2,1,0:T(8,128)(2,1)} %get-tuple-element.205.grads_ref, bf16[1024,1024]{1,0:T(8,128)(2,1)} %bitcast.174, bf16[1024,1024]{1,0:T(8,128)(2,1)} %bitcast.175, bf16[512,1024]{1,0:T(8,128)(2,1)} %collective-permute-done.15.refs_2_, ...), custom_call_target="tpu_custom_call" | custom-call | tf_op jit(solution)/shard_map/gated_gradient/pallas_call | solution.py:632
  469.7 9.4 %all-to-all-start.3 = ((bf16[4,256,256]{2,1,0:T(8,128)(2,1)}), bf16[4,256,256]{2,1,0:T(8,128)(2,1)}, u32[]{:S(2)}, u32[]{:S(2)}) async-start(bf16[4,256,256]{2,1,0:T(8,128)(2,1)} %gated_gradient.3), calls=%async_computation.3 | async-start | bytes 1048576 | tf_op jit(solution)/shard_map/all_to_all | solution.py:658
  480.6 6.6 %all-to-all-done.3 = bf16[4,256,256]{2,1,0:T(8,128)(2,1)} async-done(((bf16[4,256,256]{2,1,0:T(8,128)(2,1)}), bf16[4,256,256]{2,1,0:T(8,128)(2,1)}, u32[]{:S(2)}, u32[]{:S(2)}) %all-to-all-start.3) | async-done | bytes 524320 | tf_op jit(solution)/shard_map/all_to_all | solution.py:658
  492.8 8.3 %conv_backward.3 = (bf16[3,512,256]{2,1,0:T(8,128)(2,1)}, f32[128,256]{1,0:T(8,128)}, f32[9,256]{1,0:T(8,128)}) custom-call(s32[1,1024]{1,0:T(1,128)} %maximum_convert_fusion.1.tokens_ref, f32[512,1]{1,0:T(8,128)} %copy.33.scale_ref, bf16[1024,256]{1,0:T(8,128)(2,1)} %bitcast.85.gg_ref, bf16[1,3,1024,256]{3,2,1,0:T(8,128)(2,1)} %get-tuple-element.148.proj_ref, ...), custom_call_target="tpu_custom_call" | custom-call | tf_op jit(solution)/shard_map/conv_backward/pallas_call | solution.py:338
  507.7 29.9 %collective-permute-done.66 = f32[138,256]{1,0:T(8,128)S(1)} collective-permute-done((f32[138,256]{1,0:T(8,128)}, f32[138,256]{1,0:T(8,128)S(1)}, u32[]{:S(2)}, u32[]{:S(2)}) %collective-permute-start.66) | collective-permute-done | bytes 141344 | tf_op jit(solution)/shard_map/ppermute | solution.py:39
  549.2 7.1 %grad_project_out.1 = f32[1024,1024]{1,0:T(8,128)} custom-call(s32[4]{0:T(128)} %pad_add_fusion.2.where_ref, bf16[1024,1024]{1,0:T(8,128)(2,1)} %bitcast.88.right_ref, bf16[1024,256]{1,0:T(8,128)(2,1)} %broadcast_select_fusion.1.refs_0_, bf16[1024,256]{1,0:T(8,128)(2,1)} %fusion.3.refs_1_, bf16[1024,256]{1,0:T(8,128)(2,1)} %fusion.2.refs_2_, ...), custom_call_target="tpu_custom_call" | custom-call | tf_op jit(solution)/shard_map/grad_project_out/pallas_call | solution.py:540
  556.2 9.7 %conditional.1 = (f32[3,1024,1024]{2,1,0:T(8,128)}) conditional(s32[]{:T(128)} %convert_element_type.114, (s32[]{:T(128)}, bf16[1024,1024]{0,1:T(8,128)(2,1)}, bf16[4,1024,256]{2,1,0:T(8,128)(2,1)S(1)}, bf16[4,1024,256]{2,1,0:T(8,128)(2,1)}, bf16[4,1024,256]{2,1,0:T(8,128)(2,1)}, /*index=5*/bf16[4,1024,256]{2,1,0:T(8,128)(2,1)}) %tuple.96, ...), branch_computations={%region_1.2_spmd, %region_2.3_spmd} | conditional | bytes 4194312 | solution.py:808
  557.6 8.4 %grad_project_in.3 = f32[3,1024,1024]{2,1,0:T(8,128)} custom-call(s32[1]{0:T(128)} %bitcast.1.ctx_ref, bf16[1024,512]{1,0:T(8,128)(2,1)} %bitcast.187, bf16[3,512,256]{2,1,0:T(8,128)(2,1)} %get-tuple-element.35.refs_0_, bf16[3,512,256]{2,1,0:T(8,128)(2,1)} %get-tuple-element.36.refs_1_, bf16[3,512,256]{2,1,0:T(8,128)(2,1)} %get-tuple-element.37.refs_2_, ...), custom_call_target="tpu_custom_call" | custom-call | tf_op jit(solution)/shard_map/cond/branch_1_fun/grad_project_in/pallas_call | solution.py:508
  (283 shorter events, 262.1 us)
Async XLA Ops:
  11.9 187.0 %collective-permute-start.28 = (bf16[3,1024,1024]{2,1,0:T(8,128)(2,1)}, bf16[3,1024,1024]{2,1,0:T(8,128)(2,1)}, u32[]{:S(2)}, u32[]{:S(2)}) collective-permute-start(bf16[3,1024,1024]{2,1,0:T(8,128)(2,1)} %bitcast.178), channel_id=1, source_target_pairs={{16,18},{17,19},{18,16},{19,17},{20,22},{21,23},{22,20},{23,21},{2... | collective-permute-start | bytes 18874376 | tf_op jit(solution)/shard_map/ppermute | solution.py:39
  18.0 42.3 %collective-permute-start.9 = (bf16[256,1024]{1,0:T(8,128)(2,1)}, bf16[256,1024]{1,0:T(8,128)(2,1)}, u32[]{:S(2)}, u32[]{:S(2)}) collective-permute-start(bf16[256,1024]{1,0:T(8,128)(2,1)} %param.20), channel_id=1, source_target_pairs={{16,20},{20,24},{24,28},{28,16},{17,21},{21,25},{25,29},{29,17},{1... | collective-permute-start | bytes 1572872 | tf_op jit(solution)/shard_map/ppermute | solution.py:39
  35.8 50.3 %collective-permute-start.6 = (bf16[2,3,512,256]{3,2,1,0:T(8,128)(2,1)}, bf16[2,3,512,256]{3,2,1,0:T(8,128)(2,1)}, u32[]{:S(2)}, u32[]{:S(2)}) collective-permute-start(bf16[2,3,512,256]{3,2,1,0:T(8,128)(2,1)} %table_projection.3), channel_id=1, source_target_pairs={{0,1},{1,0},{2,3},{3,2},{4,5},{5,4},{6,7},{7,6},{8,9},{9,8},{10,11... | collective-permute-start | bytes 4718600 | tf_op jit(solution)/shard_map/ppermute | solution.py:39
  40.6 48.1 %collective-permute-start.7 = (bf16[512,1024]{1,0:T(8,128)(2,1)}, bf16[512,1024]{1,0:T(8,128)(2,1)}, u32[]{:S(2)}, u32[]{:S(2)}) collective-permute-start(bf16[512,1024]{1,0:T(8,128)(2,1)} %get-tuple-element.242), channel_id=1, source_target_pairs={{0,2},{1,3},{2,0},{3,1},{4,6},{5,7},{6,4},{7,5},{8,10},{9,11},{10,... | collective-permute-start | bytes 3145736 | tf_op jit(solution)/shard_map/ppermute | solution.py:39
  202.2 30.4 %collective-permute-start.37 = (bf16[1024,1024]{1,0:T(8,128)(2,1)S(1)}, bf16[1024,1024]{1,0:T(8,128)(2,1)}, u32[]{:S(2)}, u32[]{:S(2)}) collective-permute-start(bf16[1024,1024]{1,0:T(8,128)(2,1)S(1)} %bitcast.176), channel_id=1, source_target_pairs={{16,18},{17,19},{18,16},{19,17},{20,22},{21,23},{22,20},{23,21},{2... | collective-permute-start | bytes 6291464 | tf_op jit(solution)/shard_map/ppermute | solution.py:39
  212.9 62.4 %collective-permute-start.29 = (bf16[1024,1024]{1,0:T(8,128)(2,1)S(1)}, bf16[1024,1024]{1,0:T(8,128)(2,1)}, u32[]{:S(2)}, u32[]{:S(2)}) collective-permute-start(bf16[1024,1024]{1,0:T(8,128)(2,1)S(1)} %bitcast.177), channel_id=1, source_target_pairs={{16,17},{17,16},{18,19},{19,18},{20,21},{21,20},{22,23},{23,22},{2... | collective-permute-start | bytes 6291464 | tf_op jit(solution)/shard_map/ppermute | solution.py:39
  232.6 42.6 %collective-permute-start.38 = (bf16[1024,1024]{1,0:T(8,128)(2,1)}, bf16[1024,1024]{1,0:T(8,128)(2,1)}, u32[]{:S(2)}, u32[]{:S(2)}) collective-permute-start(bf16[1024,1024]{1,0:T(8,128)(2,1)} %collective-permute-done.37.refs_4_.refs_5_), channel_id=1, source_target_pairs={{16,17},{17,16},{18,19},{19,18},{20,21},{21,20},{22,23},{23,22},{2... | collective-permute-start | bytes 6291464 | tf_op jit(solution)/shard_map/ppermute | solution.py:39
  234.6 47.5 %all-to-all-start.1 = ((bf16[4,3,256,256]{3,2,1,0:T(8,128)(2,1)}), bf16[4,3,256,256]{3,2,1,0:T(8,128)(2,1)}, u32[]{:S(2)}, u32[]{:S(2)}) async-start(bf16[4,3,256,256]{3,2,1,0:T(8,128)(2,1)} %get-tuple-element.120), calls=%async_computation.1 | async-start | bytes 3145728 | tf_op jit(solution)/shard_map/all_to_all | solution.py:658
  240.3 30.6 %collective-permute-start.40 = (bf16[1024,256]{1,0:T(8,128)(2,1)}, bf16[1024,256]{1,0:T(8,128)(2,1)}, u32[]{:S(2)}, u32[]{:S(2)}) collective-permute-start(bf16[1024,256]{1,0:T(8,128)(2,1)} %get-tuple-element.138), channel_id=1, source_target_pairs={{0,2},{1,3},{2,0},{3,1},{4,6},{5,7},{6,4},{7,5},{8,10},{9,11},{10,... | collective-permute-start | bytes 1572872 | tf_op jit(solution)/shard_map/ppermute | solution.py:39
  245.3 56.5 %collective-permute-start.39 = (bf16[1024,256]{1,0:T(8,128)(2,1)}, bf16[1024,256]{1,0:T(8,128)(2,1)}, u32[]{:S(2)}, u32[]{:S(2)}) collective-permute-start(bf16[1024,256]{1,0:T(8,128)(2,1)} %get-tuple-element.138), channel_id=1, source_target_pairs={{0,1},{1,0},{2,3},{3,2},{4,5},{5,4},{6,7},{7,6},{8,9},{9,8},{10,11... | collective-permute-start | bytes 1572872 | tf_op jit(solution)/shard_map/ppermute | solution.py:39
  270.8 31.0 %collective-permute-start.41 = (bf16[1024,256]{1,0:T(8,128)(2,1)}, bf16[1024,256]{1,0:T(8,128)(2,1)}, u32[]{:S(2)}, u32[]{:S(2)}) collective-permute-start(bf16[1024,256]{1,0:T(8,128)(2,1)} %collective-permute-done.40), channel_id=1, source_target_pairs={{0,1},{1,0},{2,3},{3,2},{4,5},{5,4},{6,7},{7,6},{8,9},{9,8},{10,11... | collective-permute-start | bytes 1572872 | tf_op jit(solution)/shard_map/ppermute | solution.py:39
  343.3 33.8 %collective-permute-start.42 = (bf16[128,1024]{1,0:T(8,128)(2,1)S(1)}, bf16[128,1024]{1,0:T(8,128)(2,1)S(1)}, u32[]{:S(2)}, u32[]{:S(2)}) collective-permute-start(bf16[128,1024]{1,0:T(8,128)(2,1)S(1)} %get-tuple-element.222), channel_id=1, source_target_pairs={{16,0},{20,4},{24,8},{28,12},{17,1},{21,5},{25,9},{29,13},{18,2},{... | collective-permute-start | bytes 786440 | tf_op jit(solution)/shard_map/ppermute | solution.py:39
  344.6 32.5 %collective-permute-start.43 = (bf16[128,1024]{1,0:T(8,128)(2,1)S(1)}, bf16[128,1024]{1,0:T(8,128)(2,1)S(1)}, u32[]{:S(2)}, u32[]{:S(2)}) collective-permute-start(bf16[128,1024]{1,0:T(8,128)(2,1)S(1)} %get-tuple-element.221), channel_id=1, source_target_pairs={{16,4},{20,8},{24,12},{28,0},{17,5},{21,9},{25,13},{29,1},{18,6},{... | collective-permute-start | bytes 786440 | tf_op jit(solution)/shard_map/ppermute | solution.py:39
  345.9 31.2 %collective-permute-start.44 = (bf16[128,1024]{1,0:T(8,128)(2,1)S(1)}, bf16[128,1024]{1,0:T(8,128)(2,1)S(1)}, u32[]{:S(2)}, u32[]{:S(2)}) collective-permute-start(bf16[128,1024]{1,0:T(8,128)(2,1)S(1)} %get-tuple-element.220), channel_id=1, source_target_pairs={{16,8},{20,12},{24,0},{28,4},{17,9},{21,13},{25,1},{29,5},{18,10},... | collective-permute-start | bytes 786440 | tf_op jit(solution)/shard_map/ppermute | solution.py:39
  347.2 29.9 %collective-permute-start.45 = (bf16[128,1024]{1,0:T(8,128)(2,1)S(1)}, bf16[128,1024]{1,0:T(8,128)(2,1)S(1)}, u32[]{:S(2)}, u32[]{:S(2)}) collective-permute-start(bf16[128,1024]{1,0:T(8,128)(2,1)S(1)} %get-tuple-element.219), channel_id=1, source_target_pairs={{16,12},{20,0},{24,4},{28,8},{17,13},{21,1},{25,5},{29,9},{18,14},... | collective-permute-start | bytes 786440 | tf_op jit(solution)/shard_map/ppermute | solution.py:39
  378.6 39.3 %collective-permute-start.60 = (bf16[4,1024,256]{2,1,0:T(8,128)(2,1)S(1)}, bf16[4,1024,256]{2,1,0:T(8,128)(2,1)}, u32[]{:S(2)}, u32[]{:S(2)}) collective-permute-start(bf16[4,1024,256]{2,1,0:T(8,128)(2,1)S(1)} %pad_maximum_fusion.7), channel_id=1, source_target_pairs={{16,18},{17,19},{18,16},{19,17},{20,22},{21,23},{22,20},{23,21},{2... | collective-permute-start | bytes 6291464 | tf_op jit(solution)/shard_map/ppermute | solution.py:39
  383.2 28.3 %collective-permute-start.49 = (bf16[128,1024]{1,0:T(8,128)(2,1)S(1)}, bf16[128,1024]{1,0:T(8,128)(2,1)S(1)}, u32[]{:S(2)}, u32[]{:S(2)}) collective-permute-start(bf16[128,1024]{1,0:T(8,128)(2,1)S(1)} %get-tuple-element.223), channel_id=1, source_target_pairs={{16,8},{20,12},{24,0},{28,4},{17,9},{21,13},{25,1},{29,5},{18,10},... | collective-permute-start | bytes 786440 | tf_op jit(solution)/shard_map/ppermute | solution.py:39
  384.5 28.5 %collective-permute-start.50 = (bf16[128,1024]{1,0:T(8,128)(2,1)S(1)}, bf16[128,1024]{1,0:T(8,128)(2,1)S(1)}, u32[]{:S(2)}, u32[]{:S(2)}) collective-permute-start(bf16[128,1024]{1,0:T(8,128)(2,1)S(1)} %get-tuple-element.218), channel_id=1, source_target_pairs={{16,12},{20,0},{24,4},{28,8},{17,13},{21,1},{25,5},{29,9},{18,14},... | collective-permute-start | bytes 786440 | tf_op jit(solution)/shard_map/ppermute | solution.py:39
  413.7 41.0 %collective-permute-start.59 = (bf16[4,1024,256]{2,1,0:T(8,128)(2,1)S(1)}, bf16[4,1024,256]{2,1,0:T(8,128)(2,1)}, u32[]{:S(2)}, u32[]{:S(2)}) collective-permute-start(bf16[4,1024,256]{2,1,0:T(8,128)(2,1)S(1)} %pad_maximum_fusion.7), channel_id=1, source_target_pairs={{16,17},{17,16},{18,19},{19,18},{20,21},{21,20},{22,23},{23,22},{2... | collective-permute-start | bytes 6291464 | tf_op jit(solution)/shard_map/ppermute | solution.py:39
  417.9 39.0 %collective-permute-start.61 = (bf16[4,1024,256]{2,1,0:T(8,128)(2,1)}, bf16[4,1024,256]{2,1,0:T(8,128)(2,1)S(1)}, u32[]{:S(2)}, u32[]{:S(2)}) collective-permute-start(bf16[4,1024,256]{2,1,0:T(8,128)(2,1)} %collective-permute-done.60), channel_id=1, source_target_pairs={{16,17},{17,16},{18,19},{19,18},{20,21},{21,20},{22,23},{23,22},{2... | collective-permute-start | bytes 6291464 | tf_op jit(solution)/shard_map/ppermute | solution.py:39
  487.2 61.9 %all-to-all-start.4 = ((bf16[4,256,1024]{2,1,0:T(8,128)(2,1)}), bf16[4,256,1024]{2,1,0:T(8,128)(2,1)}, u32[]{:S(2)}, u32[]{:S(2)}) async-start(bf16[4,256,1024]{2,1,0:T(8,128)(2,1)} %get-tuple-element.204), calls=%async_computation.4 | async-start | bytes 4194304 | tf_op jit(solution)/shard_map/all_to_all | solution.py:658
  501.2 39.9 %collective-permute-start.63 = (bf16[3,512,256]{2,1,0:T(8,128)(2,1)}, bf16[3,512,256]{2,1,0:T(8,128)(2,1)}, u32[]{:S(2)}, u32[]{:S(2)}) collective-permute-start(bf16[3,512,256]{2,1,0:T(8,128)(2,1)} %get-tuple-element.151), channel_id=1, source_target_pairs={{0,2},{1,3},{2,0},{3,1},{4,6},{5,7},{6,4},{7,5},{8,10},{9,11},{10,... | collective-permute-start | bytes 2359304 | tf_op jit(solution)/shard_map/ppermute | solution.py:39
  507.0 30.6 %collective-permute-start.66 = (f32[138,256]{1,0:T(8,128)}, f32[138,256]{1,0:T(8,128)S(1)}, u32[]{:S(2)}, u32[]{:S(2)}) collective-permute-start(f32[138,256]{1,0:T(8,128)} %pad_maximum_fusion.14), channel_id=1, source_target_pairs={{0,2},{1,3},{2,0},{3,1},{16,18},{17,19},{18,16},{19,17},{4,6},{5,7... | collective-permute-start | bytes 423944 | tf_op jit(solution)/shard_map/ppermute | solution.py:39
  507.1 36.4 %collective-permute-start.65 = (f32[138,256]{1,0:T(8,128)}, f32[138,256]{1,0:T(8,128)}, u32[]{:S(2)}, u32[]{:S(2)}) collective-permute-start(f32[138,256]{1,0:T(8,128)} %pad_maximum_fusion.14), channel_id=1, source_target_pairs={{0,1},{1,0},{2,3},{3,2},{16,17},{17,16},{18,19},{19,18},{4,5},{5,4... | collective-permute-start | bytes 423944 | tf_op jit(solution)/shard_map/ppermute | solution.py:39
  (81 other events, 1242.5 us)
where the time goes:
time: 578 us; the launch traced here: 567 us
  waiting for transfers between devices  186 us (32%)
  starting transfers between devices  178 us (31%)
  Pallas kernels  104 us (18%)
  other arithmetic  47.3 us (8%)
  local copies, waits for them, and re-layouts  24.7 us (4%)
  blocking collectives  24.5 us (4%)
    ppermute x68, waiting for transfers between devices, send(): return lax.ppermute(value, axes, pairs)  177 us
    ppermute x68, starting transfers between devices, send(): return lax.ppermute(value, axes, pairs)  154 us
    all_to_all x1, blocking collectives, ctx_swap(): return lax.all_to_all(value, 'ctx', split_axis=0, concat_axis=0, tiled=True)  24.5 us
    all_to_all x4, starting transfers between devices, ctx_swap(): return lax.all_to_all(value, 'ctx', split_axis=0, concat_axis=0, tiled=True)  24.2 us
    pallas_call x2, Pallas kernels, conv_backward(): pl.pallas_call(backward_kernel if tokens is None else collect_kernel, out...  15.8 us
    pallas_call x1, Pallas kernels, input_projection(): pl.pallas_call(kernel, grid_spec=pltpu.PrefetchScalarGridSpec(num_scalar_...  15.5 us
    pallas_call x1, Pallas kernels, input_gradient(): pl.pallas_call(kernel, grid_spec=pltpu.PrefetchScalarGridSpec(num_scalar_...  15.1 us
    pallas_call x2, Pallas kernels, gated_gradient(): pl.pallas_call(kernel, grid_spec=pltpu.PrefetchScalarGridSpec(num_scalar_...  13.7 us
  transfers between devices with their start and end apart: 72, of which 20 were waited for; matrix products, arithmetic and copies ran while one was open for 9% of the time, Pallas kernels for 13%

commit v1 on v0

--- a/solution.py
+++ b/solution.py
@@ -89,18 +89,17 @@
 
 def cross_gather(shares, base, source, early, late=()):
     count = lax.axis_size("dp")
-    me = lax.axis_index("dp")
     half = base.shape[0] // 2
     arrivals = [
         [
             send(
-                pick(shares, (me + shift) % count)[start : start + half],
+                side[shift],
                 ("section", "dp"),
                 lambda s, z: (1 - s, (z + shift) % count) if s == source else None,
             )
             for shift in range(count)
         ]
-        for start in (0, half)
+        for side in shares
     ]
 
     def total(index, values):
@@ -160,9 +159,9 @@
     return real, jnp.where(row == 0, 0.0, imag), jnp.where(row == 0, imag, real)
 
 
-def proj_block(proj_ref, m, b, tap_count):
-    chunk, start = divmod(b * tap_count, proj_ref.shape[2])
-    return proj_ref[chunk, m, start : start + tap_count, :].astype(F32)
+def proj_block(projs, m, b, tap_count):
+    chunk, start = divmod(b * tap_count, projs[m].shape[1])
+    return projs[m][chunk, start : start + tap_count, :].astype(F32)
 
 
 def short_filter(taps_ref, m, current, before, row):
@@ -206,6 +205,7 @@
 
 
 def forward_kernel(proj_ref, taps_ref, kern_ref, fwd_ref, inv_ref, gated_ref, filt_ref, spec_ref):
+    projs = [proj_ref.at[:, m] for m in range(3)]
     tap_count, chans = kern_ref.shape
     blocks = filt_ref.shape[0] // tap_count
     row = lax.broadcasted_iota(jnp.int32, (tap_count, chans), 0)
@@ -218,7 +218,7 @@
         here = pl.ds(b * tap_count, tap_count)
         streams = []
         for m in range(3):
-            current = proj_block(proj_ref, m, b, tap_count)
+            current = proj_block(projs, m, b, tap_count)
             streams.append(short_filter(taps_ref, m, current, before[m], row))
             before[m] = current
         part = dot(fwd_ref[...], (streams[1] * streams[2]).astype(BF16))
@@ -238,6 +238,7 @@
     gg_ref, proj_ref, taps_ref, kern_ref, fwd_ref, inv_ref, filt_ref, spec_ref,
     gproj_ref, gkern_ref, gtaps_ref, grad_spec,
 ):
+    projs = [proj_ref.at[:, m] for m in range(3)]
     tap_count, chans = kern_ref.shape
     blocks = filt_ref.shape[0] // tap_count
     row = lax.broadcasted_iota(jnp.int32, (tap_count, chans), 0)
@@ -248,7 +249,7 @@
     last = zero
     for b in range(blocks):
         here = pl.ds(b * tap_count, tap_count)
-        current = proj_block(proj_ref, 0, b, tap_count)
+        current = proj_block(projs, 0, b, tap_count)
         query = short_filter(taps_ref, 0, current, last, row)
         last = current
         part = dot(fwd_ref[...], (gg_ref[here, :].astype(F32) * query).astype(BF16))
@@ -266,7 +267,7 @@
     next_r, next_i = zero, zero
     sums = [jnp.zeros((1, chans), F32) for _ in range(9)]
     for b in reversed(range(blocks)):
-        chunk, start = divmod(b * tap_count, proj_ref.shape[2])
+        chunk, start = divmod(b * tap_count, projs[0].shape[1])
         here = pl.ds(b * tap_count, tap_count)
         gr, gi = grad_spec[b, :tap_count, :], grad_spec[b, tap_count:, :]
         vr, vi = gr + sign * next_r, gi + sign * next_i
@@ -275,8 +276,8 @@
         grad_prod = dot(inv_ref[...], mixed.astype(BF16))
         shifts, shorts = [], []
         for m in range(3):
-            current = proj_block(proj_ref, m, b, tap_count)
-            before = proj_block(proj_ref, m, b - 1, tap_count) if b else zero
+            current = proj_block(projs, m, b, tap_count)
+            before = proj_block(projs, m, b - 1, tap_count) if b else zero
             shifts.append([current, later(current, before, 1, row), later(current, before, 2, row)])
             if m:
                 shorts.append(sum(taps_ref[3 * j + m : 3 * j + m + 1, :] * shifts[m][j] for j in range(3)))
@@ -429,16 +430,16 @@
     )(ctx[None], rows_in, *pieces)
 
 
-def input_gradient(gproj, pieces, rows_in, scale, ctx):
+def input_gradient(gproj, pieces, rows_in, scale, ctx, dp):
     rows, full_width = rows_in.shape
     feats, chans = pieces[0].shape[1:]
     count = len(pieces)
     sub = chans // count
     tile = min(256, feats)
-    steps = feats // tile
+    steps, half = feats // tile, rows // 2
 
     def kernel(ctx_ref, gproj_ref, rows_ref, scale_ref, *refs):
-        weights, (out_ref, flat, grads) = refs[:count], refs[count:]
+        weights, outs, (flat, grads) = refs[:count], refs[count:-2], refs[-2:]
         step = pl.program_id(0)
 
         @pl.when(step == 0)
@@ -461,11 +462,15 @@
                 part = rows_ref[:, q * feats : (q + 1) * feats].astype(F32)
                 stat = stat + jnp.sum(part * grads[q], axis=1, keepdims=True)
             stat = stat * scale_ref[...] * scale_ref[...] / full_width
-            for q in range(count):
-                part = rows_ref[:, q * feats : (q + 1) * feats].astype(F32)
-                out_ref[q] = (grads[q] - part * stat).astype(BF16)
-
-    return pl.pallas_call(
+            for shift in range(count):
+                q = ctx_ref[1 + shift]
+                start = pl.multiple_of(q * feats, feats)
+                part = rows_ref[:, pl.ds(start, feats)].astype(F32)
+                total = (grads[q] - part * stat).astype(BF16)
+                outs[shift][...] = total[:half]
+                outs[count + shift][...] = total[half:]
+
+    outs = pl.pallas_call(
         kernel,
         grid_spec=pltpu.PrefetchScalarGridSpec(
             num_scalar_prefetch=1,
@@ -476,16 +481,17 @@
                 pl.BlockSpec((rows, 1), lambda t, ctx: (0, 0)),
             ]
             + [pl.BlockSpec((3, tile, chans), lambda t, ctx: (0, t, 0))] * count,
-            out_specs=pl.BlockSpec((count, rows, feats), lambda t, ctx: (0, 0, 0)),
+            out_specs=[pl.BlockSpec((half, feats), lambda t, ctx: (0, 0))] * (2 * count),
             scratch_shapes=[
                 pltpu.VMEM((3, rows, chans), BF16),
                 pltpu.VMEM((count, rows, feats), F32),
             ],
         ),
-        out_shape=jax.ShapeDtypeStruct((count, rows, feats), BF16),
+        out_shape=[jax.ShapeDtypeStruct((half, feats), BF16)] * (2 * count),
         compiler_params=PARAMS,
         name="input_gradient",
-    )(ctx[None], gproj, rows_in, scale, *pieces)
+    )(jnp.concatenate([ctx[None], targets(dp, count)]), gproj, rows_in, scale, *pieces)
+    return outs[:count], outs[count:]
 
 
 def grad_in_kernel(left, pieces, ctx):
@@ -520,22 +526,23 @@
     )(ctx[None], left, *pieces)
 
 
-def grad_out_kernel(pieces, right, ctx):
+def grad_out_kernel(early, late, right, ctx, sec):
     depth, feats = right.shape
-    count, sub = len(pieces), pieces[0].shape[1]
+    count, sub = len(early), early[0].shape[1]
 
     def kernel(where_ref, right_ref, *refs):
-        out_ref = refs[count]
+        out_ref = refs[2 * count]
         for r in range(count):
-
-            @pl.when(pl.program_id(0) == r)
-            def _():
-                out_ref[...] = lax.dot_general(
-                    refs[r][...],
-                    right_ref[...],
-                    (((0,), (0,)), ((), ())),
-                    preferred_element_type=F32,
-                )
+            for index, piece in ((0, refs[r].at[...]), (1, refs[count + r].at[0])):
+
+                @pl.when((pl.program_id(0) == r) & (where_ref[count] == index))
+                def _():
+                    out_ref[...] = lax.dot_general(
+                        piece[...],
+                        right_ref[...],
+                        (((0,), (0,)), ((), ())),
+                        preferred_element_type=F32,
+                    )
 
     return pl.pallas_call(
         kernel,
@@ -543,105 +550,63 @@
             num_scalar_prefetch=1,
             grid=(count,),
             in_specs=[pl.BlockSpec((depth, feats), lambda r, where: (0, 0))]
-            + [pl.BlockSpec((depth, sub), lambda r, where: (0, 0))] * count,
+            + [pl.BlockSpec((depth, sub), lambda r, where: (0, 0))] * count
+            + [pl.BlockSpec((1, depth, sub), lambda r, where: (3, 0, 0))] * count,
             out_specs=pl.BlockSpec((sub, feats), lambda r, where: (where[r], 0)),
         ),
         out_shape=jax.ShapeDtypeStruct((sub * count, feats), F32),
         compiler_params=PARAMS,
         name="grad_project_out",
-    )(jnp.stack([ctx ^ r for r in range(count)]), right, *pieces)
+    )(jnp.stack([ctx ^ r for r in range(count)] + [sec]), right, *early, *late)
 
 
 def together(*values):
     return lax.optimization_barrier(values)
 
 
-def projection_specs(pieces, tile):
-    specs, operands = [], []
-    for piece in pieces:
-        for array, place in piece:
-            height = array.shape[0] if place is None else array.shape[0] // 2
-            specs.append(pl.BlockSpec((height, tile), functools.partial(place_of, place or 0)))
-            operands.append(array)
-    return specs, operands
-
-
-def place_of(row, t, ctx):
-    return (row, t)
-
-
-def output_projection(gated, pieces, ctx):
+def targets(dp, count):
+    return (dp + jnp.arange(count, dtype=jnp.int32)) % count
+
+
+def output_projection(gated, weights, dp):
     count, rows, sub = gated.shape
-    chans, feats = count * sub, pieces[0][0][0].shape[1]
-    half, tile = chans // 2, min(256, feats)
-    specs, operands = projection_specs(pieces, tile)
-
-    def kernel(ctx_ref, gated_ref, *refs):
-        weights, (out_ref, flat) = refs[: 2 * count], refs[2 * count :]
+    chans, full_width = weights.shape
+    parts = lax.axis_size("dp")
+    width, half = full_width // parts, rows // 2
+
+    def kernel(where_ref, gated_ref, weights_ref, *refs):
+        outs, flat = refs[:-1], refs[-1]
 
         @pl.when(pl.program_id(0) == 0)
         def _():
             for q in range(count):
                 flat[:, q * sub : (q + 1) * sub] = gated_ref[q]
 
-        for r in range(count):
-            total = dot(flat[:, :half], weights[2 * r][...])
-            total = total + dot(flat[:, half:], weights[2 * r + 1][...])
-            out_ref[ctx_ref[0] ^ r] = total.astype(BF16)
-
-    return pl.pallas_call(
+        total = dot(flat[...], weights_ref[...]).astype(BF16)
+        for shift in range(parts):
+
+            @pl.when(pl.program_id(0) == shift)
+            def _():
+                outs[shift][...] = total[:half]
+                outs[parts + shift][...] = total[half:]
+
+    outs = pl.pallas_call(
         kernel,
         grid_spec=pltpu.PrefetchScalarGridSpec(
             num_scalar_prefetch=1,
-            grid=(feats // tile,),
-            in_specs=[pl.BlockSpec(gated.shape, lambda t, ctx: (0, 0, 0))] + specs,
-            out_specs=pl.BlockSpec((count, rows, tile), lambda t, ctx: (0, 0, t)),
+            grid=(parts,),
+            in_specs=[
+                pl.BlockSpec(gated.shape, lambda q, where: (0, 0, 0)),
+                pl.BlockSpec((chans, width), lambda q, where: (0, where[q])),
+            ],
+            out_specs=[pl.BlockSpec((half, width), lambda q, where: (0, 0))] * (2 * parts),
             scratch_shapes=[pltpu.VMEM((rows, chans), BF16)],
         ),
-        out_shape=jax.ShapeDtypeStruct((count, rows, feats), BF16),
+        out_shape=[jax.ShapeDtypeStruct((half, width), BF16)] * (2 * parts),
         compiler_params=PARAMS,
         name="output_projection",
-    )(ctx[None], gated, *operands)
-
-
-def gated_gradient(grads, pieces, ctx):
-    count, rows, feats = grads.shape
-    chans = pieces[0][0][0].shape[0]
-    half, tile, sub = chans // 2, min(256, feats), chans // count
-    specs, operands = projection_specs(pieces, tile)
-
-    def kernel(ctx_ref, grads_ref, *refs):
-        weights, (out_ref, total) = refs[: 2 * count], refs[2 * count :]
-        step = pl.program_id(0)
-
-        @pl.when(step == 0)
-        def _():
-            total[...] = jnp.zeros_like(total)
-
-        for side in range(2):
-            part = dot_t(grads_ref[ctx_ref[0]], weights[side][...])
-            for r in range(1, count):
-                part = part + dot_t(grads_ref[ctx_ref[0] ^ r], weights[2 * r + side][...])
-            total[:, side * half : (side + 1) * half] += part
-
-        @pl.when(step == feats // tile - 1)
-        def _():
-            for q in range(count):
-                out_ref[q] = total[:, q * sub : (q + 1) * sub].astype(BF16)
-
-    return pl.pallas_call(
-        kernel,
-        grid_spec=pltpu.PrefetchScalarGridSpec(
-            num_scalar_prefetch=1,
-            grid=(feats // tile,),
-            in_specs=[pl.BlockSpec((count, rows, tile), lambda t, ctx: (0, 0, t))] + specs,
-            out_specs=pl.BlockSpec((count, rows, sub), lambda t, ctx: (0, 0, 0)),
-            scratch_shapes=[pltpu.VMEM((rows, chans), F32)],
-        ),
-        out_shape=jax.ShapeDtypeStruct((count, rows, sub), BF16),
-        compiler_params=PARAMS,
-        name="gated_gradient",
-    )(ctx[None], grads, *operands)
+    )(targets(dp, parts), gated, weights)
+    return outs[:parts], outs[parts:]
 
 
 def ctx_swap_in(value, section):
@@ -695,11 +660,6 @@
         table = lax.dynamic_slice_in_dim(
             lax.all_gather(embedding, "dp", axis=1, tiled=True), ctx * feats, feats, 1
         )
-    half = chans // 2
-    out_far = [far_gather(weights_out[start : start + half], (0,)) for start in (0, half)]
-    far = sorted(out_far[0])[1:]
-    table, *late = together(table, *[out_far[0][r] for r in far])
-    out_far[0].update(zip(far, late))
     table_float = table.astype(F32)
     squares = jnp.sum(table_float * table_float, axis=1)
     tokens = token_ids.astype(F32)[None]
@@ -729,31 +689,26 @@
     vocabulary = jnp.arange(vocab, dtype=jnp.int32)[None, :]
     first_input = dot((token_ids[:, None] == vocabulary).astype(BF16), embedding)
 
+    out_full = lax.all_gather(weights_out, "ctx", axis=1, tiled=True)
     in_far = far_gather(weights_in, (1,))
+    far = sorted(in_far)[1:]
 
     order = scatter_order(n_ctx)
     kept = order[: n_ctx // 2]
     sent = table_projection(table, weights_in, ctx, [r | 1 for r in kept], BF16)
     arrived = ctx_xor(sent, 1, (0,))
     partial = table_projection(table, weights_in, ctx, kept, F32) + arrived.astype(F32)
-    partial, *late = together(partial, *[out_far[1][r] for r in far])
-    out_far[1].update(zip(far, late))
     bit = 2
     while bit < n_ctx:
         stays, gone = jnp.split(partial, 2, axis=0)
         partial = stays + ctx_xor(gone.astype(BF16), bit, (0,)).astype(F32)
         bit *= 2
     table_proj = (partial[0] * table_inv).astype(BF16)
-    out_pieces = [[(weights_out, 0), (weights_out, 1)]]
-    for r in sorted(out_far[0]):
-        if r:
-            out_pieces.append([(side[r], None) for side in out_far])
-        out_pieces.append([(ctx_xor(side[r], 1, (0,)), None) for side in out_far])
     gated_0, *saved_0, proj_0 = conv_forward(table_proj, taps, kern, matrices, tokens)
     cot_stack = jnp.stack(dp_gather(cotangent, 1))
     gated_0, cot_stack = together(gated_0, cot_stack)
     gated_rows = jnp.stack(ctx_swap_in(gated_0.reshape(n_ctx, rows, sub), 0))
-    shares = output_projection(gated_rows, out_pieces, ctx)
+    shares = output_projection(gated_rows, out_full, dp)
     middle_stack, (gated_0,), late = cross_gather(
         shares, first_input, 0, [gated_0], [in_far[r] for r in far]
     )
@@ -763,27 +718,23 @@
     in_pieces = []
     for r in sorted(in_far):
         in_pieces += [in_far[r], ctx_xor(in_far[r], 1, (1,))]
-    weights_late, *_ = together(weights_out, *late)
-    late_far = far_gather(weights_late, (1,))
     middle_all = jnp.concatenate(in_order(middle_stack, dp), axis=1)
     normed, proj_rows, scale = input_projection(middle_all, in_pieces, ctx)
-    proj_rows, *late = together(proj_rows, *[late_far[r] for r in far])
-    late_far.update(zip(far, late))
-    out_late = []
-    for r in sorted(late_far):
-        out_late += [late_far[r], ctx_xor(late_far[r], 1, (1,))]
-    out_late = [[(piece, 0), (piece, 1)] for piece in out_late]
     proj_1 = ctx_swap(proj_rows)
     gated_1, *saved_1 = conv_forward(proj_1, taps, kern, matrices)
 
-    cot_parts = jnp.stack(in_order(cot_stack, dp))
-    gated_grad = ctx_swap(gated_gradient(cot_parts, out_late, ctx)).reshape(seq, sub)
+    def gated_gradient(parts):
+        total = dot_t(jnp.concatenate(parts, axis=1), out_full).astype(BF16)
+        split = jnp.transpose(total.reshape(rows, n_ctx, sub), (1, 0, 2))
+        return ctx_swap(split).reshape(seq, sub)
+
+    cot_parts = in_order(cot_stack, dp)
     gproj_1, gkern_1, gtaps_1 = conv_backward(
-        gated_grad, proj_1, taps, kern, matrices, saved_1
+        gated_gradient(cot_parts), proj_1, taps, kern, matrices, saved_1
     )
     gproj_1, *gated_all_0 = together(gproj_1, *gated_all_0)
     gproj_rows = ctx_swap(gproj_1)
-    shares = input_gradient(gproj_rows, in_pieces, middle_all, scale, ctx)
+    shares = input_gradient(gproj_rows, in_pieces, middle_all, scale, ctx, dp)
     back_stack, (normed, gproj_1, gated_1), _ = cross_gather(
         shares, cotangent, 1, [normed, gproj_1, gated_1]
     )
@@ -791,19 +742,16 @@
     normed_cols = jnp.concatenate([part.T for part in ctx_swap_in(normed, 1)], axis=1)
     gproj_1 = gproj_1.transpose(1, 0, 2, 3).reshape(3, seq, sub)
     gproj_all = ctx_gather(jnp.concatenate([gproj_1, gated_1[None]]), (1,))
-    gated_all = [jnp.where(first, a, b[3]) for a, b in zip(gated_all_0, gproj_all)]
-
-    back_stack, normed_cols, *rest = together(back_stack, normed_cols, *gproj_all, *gated_all)
-    gproj_all, gated_all = rest[:n_ctx], rest[n_ctx:]
-    back_parts = jnp.stack(in_order(back_stack, dp))
-    gated_grad = ctx_swap(gated_gradient(back_parts, out_pieces, ctx)).reshape(seq, sub)
+
+    back_stack, normed_cols, *gproj_all = together(back_stack, normed_cols, *gproj_all)
+    back_parts = in_order(back_stack, dp)
     table_grad, gkern_0, gtaps_0 = conv_backward(
-        gated_grad, proj_0, taps, kern, matrices, saved_0, tokens, table_inv
-    )
-
-    grads = jnp.where(first, back_parts, cot_parts)
+        gated_gradient(back_parts), proj_0, taps, kern, matrices, saved_0, tokens, table_inv
+    )
+
+    grads = jnp.stack([jnp.where(first, a, b) for a, b in zip(back_parts, cot_parts)])
     grad_cols = ctx_swap(grads).reshape(seq, feats)
-    grad_out = grad_out_kernel(gated_all, grad_cols, ctx)
+    grad_out = grad_out_kernel(gated_all_0, gproj_all, grad_cols, ctx, sec)
     table_pieces = ctx_gather(table_grad, (0,))
     grad_in = lax.cond(
         first,

time: 578 us -> 561 us (0.971)
  blocking collectives: 24.5 us -> 0 us
  starting transfers between devices: 178 us -> 196 us
  between operations: 2.3 us -> 15.4 us
  Pallas kernels: 104 us -> 92.3 us
  other arithmetic: 47.3 us -> 39 us
  matrix products: 0.49 us -> 8.58 us
  waiting for transfers between devices: 186 us -> 180 us
    ppermute x68 -> x59, waiting for transfers between devices: 177 us -> 146 us  [send(): return lax.ppermute(value, axes, pairs)]
    all_to_all x1 -> x0, blocking collectives: 24.5 us -> none  [ctx_swap(): return lax.all_to_all(value, 'ctx', split_axis=0, concat_axis=0, tiled=True)]
    all_to_all x4 -> x5, waiting for transfers between devices: 9.5 us -> 33.3 us  [ctx_swap(): return lax.all_to_all(value, 'ctx', split_axis=0, concat_axis=0, tiled=True)]
    all_to_all x4 -> x5, starting transfers between devices: 24.2 us -> 39.1 us  [ctx_swap(): return lax.all_to_all(value, 'ctx', split_axis=0, concat_axis=0, tiled=True)]
    pallas_call x2 -> x0, Pallas kernels: 13.7 us -> none  [gated_gradient(): pl.pallas_call(kernel, grid_spec=pltpu.PrefetchScalarGridSpec(num_scalar_...]
    select_n x5 -> x2, other arithmetic: 10.6 us -> 1.97 us  [the longest x1 1.45 us: local(): jnp.where(first, a, b)]
    dot_general x0 -> x2, matrix products: none -> 8.1 us  [dot_t(): lax.dot_general(left, right, (((1,), (1,)), ((), ())), preferred_element_...]
    slice x3 -> x0, local copies, waits for them, and re-layouts: 6.67 us -> none  [the longest x2 3.54 us: cross_gather(): pick(shares, (me + shift) % count)[start:start + half]]
  transfers between devices with their start and end apart: 72 -> 65, of which waited for: 20 -> 22; matrix products, arithmetic and copies ran while one was open for 9% -> 10% of each run, Pallas kernels for 13% -> 12%
where the time goes in v1:
time: 561 us; the launch traced here: 552 us
  starting transfers between devices  196 us (35%)
  waiting for transfers between devices  180 us (32%)
  Pallas kernels  92.3 us (16%)
  other arithmetic  39 us (7%)
  local copies, waits for them, and re-layouts  20.5 us (4%)
  between operations  15.4 us (3%)
  matrix products  8.58 us (2%)
    ppermute x59, starting transfers between devices, send(): return lax.ppermute(value, axes, pairs)  157 us
    ppermute x59, waiting for transfers between devices, send(): return lax.ppermute(value, axes, pairs)  146 us
    all_to_all x5, starting transfers between devices, ctx_swap(): return lax.all_to_all(value, 'ctx', split_axis=0, concat_axis=0, tiled=True)  39.1 us
    all_to_all x5, waiting for transfers between devices, ctx_swap(): return lax.all_to_all(value, 'ctx', split_axis=0, concat_axis=0, tiled=True)  33.3 us
    pallas_call x1, Pallas kernels, input_gradient(): pl.pallas_call(kernel, grid_spec=pltpu.PrefetchScalarGridSpec(num_scalar_...  16 us
    pallas_call x2, Pallas kernels, conv_backward(): pl.pallas_call(backward_kernel if tokens is None else collect_kernel, out...  15.9 us
    pallas_call x1, Pallas kernels, input_projection(): pl.pallas_call(kernel, grid_spec=pltpu.PrefetchScalarGridSpec(num_scalar_...  15.5 us
  transfers between devices with their start and end apart: 65, of which 22 were waited for; matrix products, arithmetic and copies ran while one was open for 10% of the time, Pallas kernels for 12%

profile of v1, /device:TPU:1, one launch (start us, length us, event | category | flops | bytes accessed | tf_op | source)
XLA Modules:
  0.0 551.6 jit_solution(3105742958060473359)
XLA Ops:
  15.9 5.3 collective-permute-done
  31.8 12.8 %collective-permute-start.5 = (bf16[2,3,512,256]{3,2,1,0:T(8,128)(2,1)}, bf16[2,3,512,256]{3,2,1,0:T(8,128)(2,1)}, u32[]{:S(2)}, u32[]{:S(2)}) collective-permute-start(bf16[2,3,512,256]{3,2,1,0:T(8,128)(2,1)} %table_projection.3), channel_id=1, source_target_pairs={{0,1},{1,0},{2,3},{3,2},{4,5},{5,4},{6,7},{7,6},{8,9},{9,8},{10,11... | collective-permute-start | bytes 4718600 | tf_op jit(solution)/shard_map/ppermute | solution.py:39
  47.9 14.9 %collective-permute-start.3 = (f32[768]{0:T(1024)S(1)}, f32[768]{0:T(1024)S(1)}, u32[]{:S(2)}, u32[]{:S(2)}) collective-permute-start(f32[768]{0:T(1024)S(1)} %pad_maximum_fusion.16), channel_id=1, source_target_pairs={{0,2},{1,3},{2,0},{3,1},{4,6},{5,7},{6,4},{7,5},{8,10},{9,11},{10,... | collective-permute-start | bytes 9224 | tf_op jit(solution)/shard_map/ppermute | solution.py:39
  84.1 14.6 %collective-permute-done.6 = bf16[1,3,512,256]{3,2,1,0:T(8,128)(2,1)} collective-permute-done((bf16[1,3,512,256]{3,2,1,0:T(8,128)(2,1)}, bf16[1,3,512,256]{3,2,1,0:T(8,128)(2,1)}, u32[]{:S(2)}, u32[]{:S(2)}) %collective-permute-start.6) | collective-permute-done | bytes 786464 | tf_op jit(solution)/shard_map/ppermute | solution.py:39
  100.9 5.6 %conv_forward.2 = (bf16[1024,256]{1,0:T(8,128)(2,1)}, bf16[1024,256]{1,0:T(8,128)(2,1)}, bf16[8,256,256]{2,1,0:T(8,128)(2,1)}, bf16[1,3,1024,256]{3,2,1,0:T(8,128)(2,1)}) custom-call(s32[1024,1]{1,0:T(8,128)} %copy.37.tokens_ref, bf16[3,512,256]{2,1,0:T(8,128)(2,1)} %fusion.18.table_ref, f32[9,256]{1,0:T(8,128)} %reshape.182.taps_ref, ...), custom_call_target="tpu_custom_call" | custom-call | tf_op jit(solution)/shard_map/conv_forward/pallas_call | solution.py:321
  121.5 8.0 %output_projection.1 = (bf16[128,1024]{1,0:T(8,128)(2,1)}, bf16[128,1024]{1,0:T(8,128)(2,1)}, bf16[128,1024]{1,0:T(8,128)(2,1)}, bf16[128,1024]{1,0:T(8,128)(2,1...) custom-call(s32[4]{0:T(128)} %and_select_fusion.where_ref, ...), custom_call_target="tpu_custom_call" | custom-call | tf_op jit(solution)/shard_map/output_projection/pallas_call | solution.py:593
  135.4 18.4 %collective-permute-done.13 = bf16[128,1024]{1,0:T(8,128)(2,1)S(1)} collective-permute-done((bf16[128,1024]{1,0:T(8,128)(2,1)}, bf16[128,1024]{1,0:T(8,128)(2,1)S(1)}, u32[]{:S(2)}, u32[]{:S(2)}) %collective-permute-start.13) | collective-permute-done | bytes 262176 | tf_op jit(solution)/shard_map/ppermute | solution.py:39
  169.8 5.6 %collective-permute-done.21 = bf16[128,1024]{1,0:T(8,128)(2,1)S(1)} collective-permute-done((bf16[128,1024]{1,0:T(8,128)(2,1)S(1)}, bf16[128,1024]{1,0:T(8,128)(2,1)S(1)}, u32[]{:S(2)}, u32[]{:S(2)}) %collective-permute-start.21) | collective-permute-done | bytes 262176 | tf_op jit(solution)/shard_map/ppermute | solution.py:39
  186.2 13.3 %collective-permute-start.27 = (bf16[128,1024]{1,0:T(8,128)(2,1)}, bf16[128,1024]{1,0:T(8,128)(2,1)S(1)}, u32[]{:S(2)}, u32[]{:S(2)}) collective-permute-start(bf16[128,1024]{1,0:T(8,128)(2,1)} %collective-permute-done.25), channel_id=1, source_target_pairs={{16,20},{20,24},{24,28},{28,16},{17,21},{21,25},{25,29},{29,17},{1... | collective-permute-start | bytes 786440 | tf_op jit(solution)/shard_map/ppermute | solution.py:39
  204.8 15.5 %input_projection.1 = (bf16[4,256,1024]{2,1,0:T(8,128)(2,1)}, bf16[4,3,256,256]{3,2,1,0:T(8,128)(2,1)}, f32[256,1]{1,0:T(8,128)}) custom-call(s32[1]{0:T(128)} %bitcast.3.ctx_ref, bf16[256,4096]{1,0:T(8,128)(2,1)} %pad_maximum_fusion.2.rows_ref, bf16[3,1024,1024]{2,1,0:T(8,128)(2,1)} %bitcast.14.weights_ref.refs_0_, ...), custom_call_target="tpu_custom_call" | custom-call | tf_op jit(solution)/shard_map/input_projection/pallas_call | solution.py:410
  220.2 15.3 %all-to-all-start.1 = ((bf16[4,3,256,256]{3,2,1,0:T(8,128)(2,1)}), bf16[4,3,256,256]{3,2,1,0:T(8,128)(2,1)}, u32[]{:S(2)}, u32[]{:S(2)}) async-start(bf16[4,3,256,256]{3,2,1,0:T(8,128)(2,1)} %get-tuple-element.126), calls=%async_computation.1 | async-start | bytes 3145728 | tf_op jit(solution)/shard_map/all_to_all | solution.py:623
  240.0 5.7 %fusion.22 = bf16[256,1024]{1,0:T(8,128)(2,1)S(1)} fusion(bf16[256,1024]{1,0:T(8,128)(2,1)S(1)} %get-tuple-element.235, bf16[256,1024]{1,0:T(8,128)(2,1)S(1)} %get-tuple-element.236, bf16[256,1024]{1,0:T(8,128)(2,1)S(1)} %get-tuple-element.237, bf16[256,1024]{1,0:T(8,128)(2,1)S(1)} %get-tuple-element.234, ...), kind=kOutput, calls=%fused_computation.32 | convolution fusion | flops 2156134400 | bytes 11010048 | tf_op jit(solution)/shard_map/dot_general | solution.py:21
  246.6 8.2 %all-to-all-done.1.proj_ref = bf16[4,3,256,256]{3,2,1,0:T(8,128)(2,1)} async-done(((bf16[4,3,256,256]{3,2,1,0:T(8,128)(2,1)}), bf16[4,3,256,256]{3,2,1,0:T(8,128)(2,1)}, u32[]{:S(2)}, u32[]{:S(2)}) %all-to-all-start.1) | async-done | bytes 1572896 | tf_op jit(solution)/shard_map/all_to_all | solution.py:623
  267.9 7.5 %conv_backward.2 = (bf16[4,3,256,256]{3,2,1,0:T(8,128)(2,1)}, f32[128,256]{1,0:T(8,128)}, f32[9,256]{1,0:T(8,128)}) custom-call(bf16[1024,256]{1,0:T(8,128)(2,1)} %bitcast.167, bf16[4,3,256,256]{3,2,1,0:T(8,128)(2,1)} %all-to-all-done.1.proj_ref, f32[9,256]{1,0:T(8,128)} %reshape.182.taps_ref, f32[128,256]{1,0:T(8,128)} %bitcast_multiply_fusion.kern_ref, ...), custom_call_target="tpu_custom_call" | custom-call | tf_op jit(solution)/shard_map/conv_backward/pallas_call | solution.py:339
  281.4 18.6 %all-to-all-done.2.gproj_ref = bf16[4,3,256,256]{3,2,1,0:T(8,128)(2,1)S(1)} async-done(((bf16[4,3,256,256]{3,2,1,0:T(8,128)(2,1)}), bf16[4,3,256,256]{3,2,1,0:T(8,128)(2,1)S(1)}, u32[]{:S(2)}, u32[]{:S(2)}) %all-to-all-start.2) | async-done | bytes 1572896 | tf_op jit(solution)/shard_map/all_to_all | solution.py:623
  301.2 16.0 %input_gradient.1 = (bf16[128,1024]{1,0:T(8,128)(2,1)}, bf16[128,1024]{1,0:T(8,128)(2,1)}, bf16[128,1024]{1,0:T(8,128)(2,1)}, bf16[128,1024]{1,0:T(8,128)(2,1)},...) custom-call(s32[5]{0:T(128)} %pad_add_fusion.ctx_ref, ...), custom_call_target="tpu_custom_call" | custom-call | tf_op jit(solution)/shard_map/input_gradient/pallas_call | solution.py:473
  322.6 44.3 %collective-permute-done.33 = bf16[128,1024]{1,0:T(8,128)(2,1)S(1)} collective-permute-done((bf16[128,1024]{1,0:T(8,128)(2,1)}, bf16[128,1024]{1,0:T(8,128)(2,1)S(1)}, u32[]{:S(2)}, u32[]{:S(2)}) %collective-permute-start.33) | collective-permute-done | bytes 262176 | tf_op jit(solution)/shard_map/ppermute | solution.py:39
  383.2 17.7 %collective-permute-start.37 = (bf16[128,1024]{1,0:T(8,128)(2,1)S(1)}, bf16[128,1024]{1,0:T(8,128)(2,1)}, u32[]{:S(2)}, u32[]{:S(2)}) collective-permute-start(bf16[128,1024]{1,0:T(8,128)(2,1)S(1)} %add_convert_fusion.1), channel_id=1, source_target_pairs={{0,4},{4,8},{8,12},{12,0},{1,5},{5,9},{9,13},{13,1},{2,6},{6,10},{... | collective-permute-start | bytes 786440 | tf_op jit(solution)/shard_map/ppermute | solution.py:39
  446.6 9.9 %all-to-all-start.3 = ((bf16[4,256,256]{2,1,0:T(8,128)(2,1)}), bf16[4,256,256]{2,1,0:T(8,128)(2,1)}, u32[]{:S(2)}, u32[]{:S(2)}) async-start(bf16[4,256,256]{2,1,0:T(8,128)(2,1)} %bitcast.168), calls=%async_computation.3 | async-start | bytes 1048576 | tf_op jit(solution)/shard_map/all_to_all | solution.py:623
  469.8 8.4 %conv_backward.3 = (bf16[3,512,256]{2,1,0:T(8,128)(2,1)}, f32[128,256]{1,0:T(8,128)}, f32[9,256]{1,0:T(8,128)}) custom-call(s32[1,1024]{1,0:T(1,128)} %maximum_convert_fusion.1.tokens_ref, f32[512,1]{1,0:T(8,128)} %copy.41.scale_ref, bf16[1024,256]{1,0:T(8,128)(2,1)} %bitcast.74.gg_ref, bf16[1,3,1024,256]{3,2,1,0:T(8,128)(2,1)} %get-tuple-element.158.proj_ref, ...), custom_call_target="tpu_custom_call" | custom-call | tf_op jit(solution)/shard_map/conv_backward/pallas_call | solution.py:339
  484.7 29.9 %collective-permute-done.57 = f32[138,256]{1,0:T(8,128)S(1)} collective-permute-done((f32[138,256]{1,0:T(8,128)}, f32[138,256]{1,0:T(8,128)S(1)}, u32[]{:S(2)}, u32[]{:S(2)}) %collective-permute-start.57) | collective-permute-done | bytes 141344 | tf_op jit(solution)/shard_map/ppermute | solution.py:39
  526.4 7.7 %grad_project_out.1 = f32[1024,1024]{1,0:T(8,128)} custom-call(s32[5]{0:T(128)} %stack.160.where_ref, bf16[1024,1024]{1,0:T(8,128)(2,1)} %bitcast.78.right_ref, bf16[1024,256]{1,0:T(8,128)(2,1)} %get-tuple-element.162.refs_0_, bf16[1024,256]{1,0:T(8,128)(2,1)} %copy-done.17, bf16[1024,256]{1,0:T(8,128)(2,1)} %collective-permute-done.31.refs_2_, ...), custom_call_target="tpu_custom_call" | custom-call | tf_op jit(solution)/shard_map/grad_project_out/pallas_call | solution.py:547
  534.1 9.8 %conditional.1 = (f32[3,1024,1024]{2,1,0:T(8,128)}) conditional(s32[]{:T(128)} %convert_element_type.120, (s32[]{:T(128)}, bf16[1024,1024]{0,1:T(8,128)(2,1)}, bf16[4,1024,256]{2,1,0:T(8,128)(2,1)S(1)}, bf16[4,1024,256]{2,1,0:T(8,128)(2,1)}, bf16[4,1024,256]{2,1,0:T(8,128)(2,1)}, /*index=5*/bf16[4,1024,256]{2,1,0:T(8,128)(2,1)}) %tuple.30, ...), branch_computations={%region_1.2_spmd, %region_2.3_spmd} | conditional | bytes 4194312 | solution.py:756
  535.4 8.4 %grad_project_in.3 = f32[3,1024,1024]{2,1,0:T(8,128)} custom-call(s32[1]{0:T(128)} %bitcast.1.ctx_ref, bf16[1024,512]{1,0:T(8,128)(2,1)} %bitcast.166, bf16[3,512,256]{2,1,0:T(8,128)(2,1)} %get-tuple-element.35.refs_0_, bf16[3,512,256]{2,1,0:T(8,128)(2,1)} %get-tuple-element.36.refs_1_, bf16[3,512,256]{2,1,0:T(8,128)(2,1)} %get-tuple-element.37.refs_2_, ...), custom_call_target="tpu_custom_call" | custom-call | tf_op jit(solution)/shard_map/cond/branch_1_fun/grad_project_in/pallas_call | solution.py:514
  (274 shorter events, 224.8 us)
Async XLA Ops:
  7.2 114.3 %all-gather.3.cloned.1.call-start = ((), (), s32[]{:S(2)}) async-start(), calls=%async_computation.5 | async-start | bytes 10485760 | tf_op jit(solution)/shard_map/all_gather | solution.py:692
  7.9 167.7 %collective-permute-start.22 = (bf16[3,1024,1024]{2,1,0:T(8,128)(2,1)}, bf16[3,1024,1024]{2,1,0:T(8,128)(2,1)}, u32[]{:S(2)}, u32[]{:S(2)}) collective-permute-start(bf16[3,1024,1024]{2,1,0:T(8,128)(2,1)} %bitcast.14.weights_ref.refs_0_), channel_id=1, source_target_pairs={{16,18},{17,19},{18,16},{19,17},{20,22},{21,23},{22,20},{23,21},{2... | collective-permute-start | bytes 18874376 | tf_op jit(solution)/shard_map/ppermute | solution.py:39
  31.8 40.5 %collective-permute-start.5 = (bf16[2,3,512,256]{3,2,1,0:T(8,128)(2,1)}, bf16[2,3,512,256]{3,2,1,0:T(8,128)(2,1)}, u32[]{:S(2)}, u32[]{:S(2)}) collective-permute-start(bf16[2,3,512,256]{3,2,1,0:T(8,128)(2,1)} %table_projection.3), channel_id=1, source_target_pairs={{0,1},{1,0},{2,3},{3,2},{4,5},{5,4},{6,7},{7,6},{8,9},{9,8},{10,11... | collective-permute-start | bytes 4718600 | tf_op jit(solution)/shard_map/ppermute | solution.py:39
  131.0 27.0 %collective-permute-start.14 = (bf16[128,1024]{1,0:T(8,128)(2,1)}, bf16[128,1024]{1,0:T(8,128)(2,1)S(1)}, u32[]{:S(2)}, u32[]{:S(2)}) collective-permute-start(bf16[128,1024]{1,0:T(8,128)(2,1)} %get-tuple-element.111), channel_id=1, source_target_pairs={{0,20},{4,24},{8,28},{12,16},{1,21},{5,25},{9,29},{13,17},{2,22},{... | collective-permute-start | bytes 786440 | tf_op jit(solution)/shard_map/ppermute | solution.py:39
  132.3 27.0 %collective-permute-start.15 = (bf16[128,1024]{1,0:T(8,128)(2,1)}, bf16[128,1024]{1,0:T(8,128)(2,1)S(1)}, u32[]{:S(2)}, u32[]{:S(2)}) collective-permute-start(bf16[128,1024]{1,0:T(8,128)(2,1)} %get-tuple-element.112), channel_id=1, source_target_pairs={{0,24},{4,28},{8,16},{12,20},{1,25},{5,29},{9,17},{13,21},{2,26},{... | collective-permute-start | bytes 786440 | tf_op jit(solution)/shard_map/ppermute | solution.py:39
  133.6 27.0 %collective-permute-start.16 = (bf16[128,1024]{1,0:T(8,128)(2,1)}, bf16[128,1024]{1,0:T(8,128)(2,1)S(1)}, u32[]{:S(2)}, u32[]{:S(2)}) collective-permute-start(bf16[128,1024]{1,0:T(8,128)(2,1)} %get-tuple-element.113), channel_id=1, source_target_pairs={{0,28},{4,16},{8,20},{12,24},{1,29},{5,17},{9,21},{13,25},{2,30},{... | collective-permute-start | bytes 786440 | tf_op jit(solution)/shard_map/ppermute | solution.py:39
  164.2 40.5 %collective-permute-start.28 = (bf16[3,1024,1024]{2,1,0:T(8,128)(2,1)}, bf16[3,1024,1024]{2,1,0:T(8,128)(2,1)}, u32[]{:S(2)}, u32[]{:S(2)}) collective-permute-start(bf16[3,1024,1024]{2,1,0:T(8,128)(2,1)} %bitcast.14.weights_ref.refs_0_), channel_id=1, source_target_pairs={{16,17},{17,16},{18,19},{19,18},{20,21},{21,20},{22,23},{23,22},{2... | collective-permute-start | bytes 18874376 | tf_op jit(solution)/shard_map/ppermute | solution.py:39
  175.7 29.1 %collective-permute-start.29 = (bf16[3,1024,1024]{2,1,0:T(8,128)(2,1)}, bf16[3,1024,1024]{2,1,0:T(8,128)(2,1)}, u32[]{:S(2)}, u32[]{:S(2)}) collective-permute-start(bf16[3,1024,1024]{2,1,0:T(8,128)(2,1)} %collective-permute-done.22.refs_2_), channel_id=1, source_target_pairs={{16,17},{17,16},{18,19},{19,18},{20,21},{21,20},{22,23},{23,22},{2... | collective-permute-start | bytes 18874376 | tf_op jit(solution)/shard_map/ppermute | solution.py:39
  183.1 54.6 %collective-permute-start.31 = (bf16[1024,256]{1,0:T(8,128)(2,1)}, bf16[1024,256]{1,0:T(8,128)(2,1)}, u32[]{:S(2)}, u32[]{:S(2)}) collective-permute-start(bf16[1024,256]{1,0:T(8,128)(2,1)} %get-tuple-element.162.refs_0_), channel_id=1, source_target_pairs={{0,2},{1,3},{2,0},{3,1},{4,6},{5,7},{6,4},{7,5},{8,10},{9,11},{10,... | collective-permute-start | bytes 1572872 | tf_op jit(solution)/shard_map/ppermute | solution.py:39
  220.2 34.6 %all-to-all-start.1 = ((bf16[4,3,256,256]{3,2,1,0:T(8,128)(2,1)}), bf16[4,3,256,256]{3,2,1,0:T(8,128)(2,1)}, u32[]{:S(2)}, u32[]{:S(2)}) async-start(bf16[4,3,256,256]{3,2,1,0:T(8,128)(2,1)} %get-tuple-element.126), calls=%async_computation.1 | async-start | bytes 3145728 | tf_op jit(solution)/shard_map/all_to_all | solution.py:623
  235.7 39.7 %collective-permute-start.30 = (bf16[1024,256]{1,0:T(8,128)(2,1)}, bf16[1024,256]{1,0:T(8,128)(2,1)S(1)}, u32[]{:S(2)}, u32[]{:S(2)}) collective-permute-start(bf16[1024,256]{1,0:T(8,128)(2,1)} %get-tuple-element.162.refs_0_), channel_id=1, source_target_pairs={{0,1},{1,0},{2,3},{3,2},{4,5},{5,4},{6,7},{7,6},{8,9},{9,8},{10,11... | collective-permute-start | bytes 1572872 | tf_op jit(solution)/shard_map/ppermute | solution.py:39
  237.7 37.7 %collective-permute-start.32 = (bf16[1024,256]{1,0:T(8,128)(2,1)}, bf16[1024,256]{1,0:T(8,128)(2,1)S(1)}, u32[]{:S(2)}, u32[]{:S(2)}) collective-permute-start(bf16[1024,256]{1,0:T(8,128)(2,1)} %collective-permute-done.31.refs_2_), channel_id=1, source_target_pairs={{0,1},{1,0},{2,3},{3,2},{4,5},{5,4},{6,7},{7,6},{8,9},{9,8},{10,11... | collective-permute-start | bytes 1572872 | tf_op jit(solution)/shard_map/ppermute | solution.py:39
  317.2 49.7 %collective-permute-start.33 = (bf16[128,1024]{1,0:T(8,128)(2,1)}, bf16[128,1024]{1,0:T(8,128)(2,1)S(1)}, u32[]{:S(2)}, u32[]{:S(2)}) collective-permute-start(bf16[128,1024]{1,0:T(8,128)(2,1)} %get-tuple-element.133), channel_id=1, source_target_pairs={{16,0},{20,4},{24,8},{28,12},{17,1},{21,5},{25,9},{29,13},{18,2},{... | collective-permute-start | bytes 786440 | tf_op jit(solution)/shard_map/ppermute | solution.py:39
  318.6 48.3 %collective-permute-start.34 = (bf16[128,1024]{1,0:T(8,128)(2,1)}, bf16[128,1024]{1,0:T(8,128)(2,1)S(1)}, u32[]{:S(2)}, u32[]{:S(2)}) collective-permute-start(bf16[128,1024]{1,0:T(8,128)(2,1)} %get-tuple-element.134), channel_id=1, source_target_pairs={{16,4},{20,8},{24,12},{28,0},{17,5},{21,9},{25,13},{29,1},{18,6},{... | collective-permute-start | bytes 786440 | tf_op jit(solution)/shard_map/ppermute | solution.py:39
  319.9 47.0 %collective-permute-start.35 = (bf16[128,1024]{1,0:T(8,128)(2,1)}, bf16[128,1024]{1,0:T(8,128)(2,1)S(1)}, u32[]{:S(2)}, u32[]{:S(2)}) collective-permute-start(bf16[128,1024]{1,0:T(8,128)(2,1)} %get-tuple-element.135), channel_id=1, source_target_pairs={{16,8},{20,12},{24,0},{28,4},{17,9},{21,13},{25,1},{29,5},{18,10},... | collective-permute-start | bytes 786440 | tf_op jit(solution)/shard_map/ppermute | solution.py:39
  321.2 45.7 %collective-permute-start.36 = (bf16[128,1024]{1,0:T(8,128)(2,1)}, bf16[128,1024]{1,0:T(8,128)(2,1)S(1)}, u32[]{:S(2)}, u32[]{:S(2)}) collective-permute-start(bf16[128,1024]{1,0:T(8,128)(2,1)} %get-tuple-element.136), channel_id=1, source_target_pairs={{16,12},{20,0},{24,4},{28,8},{17,13},{21,1},{25,5},{29,9},{18,14},... | collective-permute-start | bytes 786440 | tf_op jit(solution)/shard_map/ppermute | solution.py:39
  372.2 29.8 %collective-permute-start.40 = (bf16[128,1024]{1,0:T(8,128)(2,1)S(1)}, bf16[128,1024]{1,0:T(8,128)(2,1)S(1)}, u32[]{:S(2)}, u32[]{:S(2)}) collective-permute-start(bf16[128,1024]{1,0:T(8,128)(2,1)S(1)} %copy-done.28), channel_id=1, source_target_pairs={{16,8},{20,12},{24,0},{28,4},{17,9},{21,13},{25,1},{29,5},{18,10},... | collective-permute-start | bytes 786440 | tf_op jit(solution)/shard_map/ppermute | solution.py:39
  373.5 30.0 %collective-permute-start.41 = (bf16[128,1024]{1,0:T(8,128)(2,1)S(1)}, bf16[128,1024]{1,0:T(8,128)(2,1)S(1)}, u32[]{:S(2)}, u32[]{:S(2)}) collective-permute-start(bf16[128,1024]{1,0:T(8,128)(2,1)S(1)} %copy-done.27), channel_id=1, source_target_pairs={{16,12},{20,0},{24,4},{28,8},{17,13},{21,1},{25,5},{29,9},{18,14},... | collective-permute-start | bytes 786440 | tf_op jit(solution)/shard_map/ppermute | solution.py:39
  377.7 62.5 %collective-permute-start.50 = (bf16[4,1024,256]{2,1,0:T(8,128)(2,1)S(1)}, bf16[4,1024,256]{2,1,0:T(8,128)(2,1)}, u32[]{:S(2)}, u32[]{:S(2)}) collective-permute-start(bf16[4,1024,256]{2,1,0:T(8,128)(2,1)S(1)} %pad_maximum_fusion.6.refs_4_), channel_id=1, source_target_pairs={{16,17},{17,16},{18,19},{19,18},{20,21},{21,20},{22,23},{23,22},{2... | collective-permute-start | bytes 6291464 | tf_op jit(solution)/shard_map/ppermute | solution.py:39
  379.7 60.5 %collective-permute-start.52 = (bf16[4,1024,256]{2,1,0:T(8,128)(2,1)}, bf16[4,1024,256]{2,1,0:T(8,128)(2,1)}, u32[]{:S(2)}, u32[]{:S(2)}) collective-permute-start(bf16[4,1024,256]{2,1,0:T(8,128)(2,1)} %collective-permute-done.51.refs_6_), channel_id=1, source_target_pairs={{16,17},{17,16},{18,19},{19,18},{20,21},{21,20},{22,23},{23,22},{2... | collective-permute-start | bytes 6291464 | tf_op jit(solution)/shard_map/ppermute | solution.py:39
  464.5 61.9 %all-to-all-start.4 = ((bf16[4,256,1024]{2,1,0:T(8,128)(2,1)}), bf16[4,256,1024]{2,1,0:T(8,128)(2,1)}, u32[]{:S(2)}, u32[]{:S(2)}) async-start(bf16[4,256,1024]{2,1,0:T(8,128)(2,1)} %pad_maximum_fusion.7), calls=%async_computation.4 | async-start | bytes 4194304 | tf_op jit(solution)/shard_map/all_to_all | solution.py:623
  478.2 39.9 %collective-permute-start.54 = (bf16[3,512,256]{2,1,0:T(8,128)(2,1)}, bf16[3,512,256]{2,1,0:T(8,128)(2,1)}, u32[]{:S(2)}, u32[]{:S(2)}) collective-permute-start(bf16[3,512,256]{2,1,0:T(8,128)(2,1)} %get-tuple-element.161), channel_id=1, source_target_pairs={{0,2},{1,3},{2,0},{3,1},{4,6},{5,7},{6,4},{7,5},{8,10},{9,11},{10,... | collective-permute-start | bytes 2359304 | tf_op jit(solution)/shard_map/ppermute | solution.py:39
  484.0 30.6 %collective-permute-start.57 = (f32[138,256]{1,0:T(8,128)}, f32[138,256]{1,0:T(8,128)S(1)}, u32[]{:S(2)}, u32[]{:S(2)}) collective-permute-start(f32[138,256]{1,0:T(8,128)} %pad_maximum_fusion.13), channel_id=1, source_target_pairs={{0,2},{1,3},{2,0},{3,1},{16,18},{17,19},{18,16},{19,17},{4,6},{5,7... | collective-permute-start | bytes 423944 | tf_op jit(solution)/shard_map/ppermute | solution.py:39
  484.1 36.6 %collective-permute-start.56 = (f32[138,256]{1,0:T(8,128)}, f32[138,256]{1,0:T(8,128)}, u32[]{:S(2)}, u32[]{:S(2)}) collective-permute-start(f32[138,256]{1,0:T(8,128)} %pad_maximum_fusion.13), channel_id=1, source_target_pairs={{0,1},{1,0},{2,3},{3,2},{16,17},{17,16},{18,19},{19,18},{4,5},{5,4... | collective-permute-start | bytes 423944 | tf_op jit(solution)/shard_map/ppermute | solution.py:39
  (78 other events, 1178.0 us)
Sparse Core Ops, SparseCore 0:
  9.6 60.8 all-gather.2

commit v2 on v1

--- a/solution.py
+++ b/solution.py
@@ -90,16 +90,19 @@
 def cross_gather(shares, base, source, early, late=()):
     count = lax.axis_size("dp")
     half = base.shape[0] // 2
+    straight, *shares = shares
+    straight = send(straight, ("section", "dp"), lambda s, z: (1 - s, z) if s == source else None)
     arrivals = [
-        [
+        [straight[start : start + half]]
+        + [
             send(
-                side[shift],
+                side[shift - 1],
                 ("section", "dp"),
                 lambda s, z: (1 - s, (z + shift) % count) if s == source else None,
             )
-            for shift in range(count)
+            for shift in range(1, count)
         ]
-        for side in shares
+        for start, side in zip((0, half), shares)
     ]
 
     def total(index, values):
@@ -109,9 +112,12 @@
             result = result + value.astype(F32)
         return result.astype(BF16)
 
-    part, *early = together(total(0, arrivals[0]), *early)
+    part = total(0, arrivals[0])
+    if early:
+        part, *early = together(part, *early)
     first = dp_gather(part, 1 - source)
-    first[1], *arrivals[1] = together(first[1], *arrivals[1])
+    marker = min(2, count - 1)
+    first[marker], *arrivals[1] = together(first[marker], *arrivals[1])
     part, *late = together(total(1, arrivals[1]), *late)
     second = dp_gather(part, 1 - source)
     stack = jnp.stack([jnp.concatenate(pair, axis=0) for pair in zip(first, second)])
@@ -467,8 +473,11 @@
                 start = pl.multiple_of(q * feats, feats)
                 part = rows_ref[:, pl.ds(start, feats)].astype(F32)
                 total = (grads[q] - part * stat).astype(BF16)
-                outs[shift][...] = total[:half]
-                outs[count + shift][...] = total[half:]
+                if shift == 0:
+                    outs[0][...] = total
+                else:
+                    outs[shift][...] = total[:half]
+                    outs[count - 1 + shift][...] = total[half:]
 
     outs = pl.pallas_call(
         kernel,
@@ -481,17 +490,19 @@
                 pl.BlockSpec((rows, 1), lambda t, ctx: (0, 0)),
             ]
             + [pl.BlockSpec((3, tile, chans), lambda t, ctx: (0, t, 0))] * count,
-            out_specs=[pl.BlockSpec((half, feats), lambda t, ctx: (0, 0))] * (2 * count),
+            out_specs=[pl.BlockSpec((rows, feats), lambda t, ctx: (0, 0))]
+            + [pl.BlockSpec((half, feats), lambda t, ctx: (0, 0))] * (2 * count - 2),
             scratch_shapes=[
                 pltpu.VMEM((3, rows, chans), BF16),
                 pltpu.VMEM((count, rows, feats), F32),
             ],
         ),
-        out_shape=[jax.ShapeDtypeStruct((half, feats), BF16)] * (2 * count),
+        out_shape=[jax.ShapeDtypeStruct((rows, feats), BF16)]
+        + [jax.ShapeDtypeStruct((half, feats), BF16)] * (2 * count - 2),
         compiler_params=PARAMS,
         name="input_gradient",
     )(jnp.concatenate([ctx[None], targets(dp, count)]), gproj, rows_in, scale, *pieces)
-    return outs[:count], outs[count:]
+    return outs[0], outs[1:count], outs[count:]
 
 
 def grad_in_kernel(left, pieces, ctx):
@@ -583,12 +594,16 @@
                 flat[:, q * sub : (q + 1) * sub] = gated_ref[q]
 
         total = dot(flat[...], weights_ref[...]).astype(BF16)
-        for shift in range(parts):
+        @pl.when(pl.program_id(0) == 0)
+        def _():
+            outs[0][...] = total
+
+        for shift in range(1, parts):
 
             @pl.when(pl.program_id(0) == shift)
             def _():
                 outs[shift][...] = total[:half]
-                outs[parts + shift][...] = total[half:]
+                outs[parts - 1 + shift][...] = total[half:]
 
     outs = pl.pallas_call(
         kernel,
@@ -599,14 +614,16 @@
                 pl.BlockSpec(gated.shape, lambda q, where: (0, 0, 0)),
                 pl.BlockSpec((chans, width), lambda q, where: (0, where[q])),
             ],
-            out_specs=[pl.BlockSpec((half, width), lambda q, where: (0, 0))] * (2 * parts),
+            out_specs=[pl.BlockSpec((rows, width), lambda q, where: (0, 0))]
+            + [pl.BlockSpec((half, width), lambda q, where: (0, 0))] * (2 * parts - 2),
             scratch_shapes=[pltpu.VMEM((rows, chans), BF16)],
         ),
-        out_shape=[jax.ShapeDtypeStruct((half, width), BF16)] * (2 * parts),
+        out_shape=[jax.ShapeDtypeStruct((rows, width), BF16)]
+        + [jax.ShapeDtypeStruct((half, width), BF16)] * (2 * parts - 2),
         compiler_params=PARAMS,
         name="output_projection",
     )(targets(dp, parts), gated, weights)
-    return outs[:parts], outs[parts:]
+    return outs[0], outs[1:parts], outs[parts:]
 
 
 def ctx_swap_in(value, section):
@@ -718,25 +735,26 @@
     in_pieces = []
     for r in sorted(in_far):
         in_pieces += [in_far[r], ctx_xor(in_far[r], 1, (1,))]
+    def gated_gradient(parts):
+        total = dot_t(jnp.concatenate(parts, axis=1), out_full).astype(BF16)
+        split = jnp.transpose(total.reshape(rows, n_ctx, sub), (1, 0, 2))
+        return ctx_swap(split).reshape(seq, sub)
+
+    cot_parts = in_order(cot_stack, dp)
+    middle_stack, gated_grad_1 = together(middle_stack, gated_gradient(cot_parts))
     middle_all = jnp.concatenate(in_order(middle_stack, dp), axis=1)
     normed, proj_rows, scale = input_projection(middle_all, in_pieces, ctx)
     proj_1 = ctx_swap(proj_rows)
     gated_1, *saved_1 = conv_forward(proj_1, taps, kern, matrices)
 
-    def gated_gradient(parts):
-        total = dot_t(jnp.concatenate(parts, axis=1), out_full).astype(BF16)
-        split = jnp.transpose(total.reshape(rows, n_ctx, sub), (1, 0, 2))
-        return ctx_swap(split).reshape(seq, sub)
-
-    cot_parts = in_order(cot_stack, dp)
     gproj_1, gkern_1, gtaps_1 = conv_backward(
-        gated_gradient(cot_parts), proj_1, taps, kern, matrices, saved_1
+        gated_grad_1, proj_1, taps, kern, matrices, saved_1
     )
     gproj_1, *gated_all_0 = together(gproj_1, *gated_all_0)
     gproj_rows = ctx_swap(gproj_1)
     shares = input_gradient(gproj_rows, in_pieces, middle_all, scale, ctx, dp)
-    back_stack, (normed, gproj_1, gated_1), _ = cross_gather(
-        shares, cotangent, 1, [normed, gproj_1, gated_1]
+    back_stack, _, (normed, gproj_1, gated_1) = cross_gather(
+        shares, cotangent, 1, [], [normed, gproj_1, gated_1]
     )
 
     normed_cols = jnp.concatenate([part.T for part in ctx_swap_in(normed, 1)], axis=1)
@@ -751,6 +769,7 @@
 
     grads = jnp.stack([jnp.where(first, a, b) for a, b in zip(back_parts, cot_parts)])
     grad_cols = ctx_swap(grads).reshape(seq, feats)
+    grad_cols, table_grad = together(grad_cols, table_grad)
     grad_out = grad_out_kernel(gated_all_0, gproj_all, grad_cols, ctx, sec)
     table_pieces = ctx_gather(table_grad, (0,))
     grad_in = lax.cond(

time: 561 us -> 606 us (1.080)
  the two profiles are of different devices: /device:TPU:1 before, /device:TPU:21 now
where the time goes in v2:
time: 606 us; the launch traced here: 596 us
  waiting for transfers between devices  258 us (43%)
  starting transfers between devices  159 us (26%)
  Pallas kernels  95.5 us (16%)
  other arithmetic  36.9 us (6%)
  local copies, waits for them, and re-layouts  23.5 us (4%)
  between operations  15.4 us (3%)
  matrix products  8.58 us (1%)
    ppermute x57, waiting for transfers between devices, send(): return lax.ppermute(value, axes, pairs)  186 us
    ppermute x57, starting transfers between devices, send(): return lax.ppermute(value, axes, pairs)  134 us
    all_to_all x5, waiting for transfers between devices, ctx_swap(): return lax.all_to_all(value, 'ctx', split_axis=0, concat_axis=0, tiled=True)  52.2 us
    all_to_all x5, starting transfers between devices, ctx_swap(): return lax.all_to_all(value, 'ctx', split_axis=0, concat_axis=0, tiled=True)  24.1 us
    all_gather x1, waiting for transfers between devices, local(): out_full = lax.all_gather(weights_out, 'ctx', axis=1, tiled=True)  18.4 us
    pallas_call x1, Pallas kernels, input_gradient(): pl.pallas_call(kernel, grid_spec=pltpu.PrefetchScalarGridSpec(num_scalar_...  15.9 us
    pallas_call x2, Pallas kernels, conv_backward(): pl.pallas_call(backward_kernel if tokens is None else collect_kernel, out...  15.9 us
    pallas_call x1, Pallas kernels, input_projection(): pl.pallas_call(kernel, grid_spec=pltpu.PrefetchScalarGridSpec(num_scalar_...  15.5 us
  transfers between devices with their start and end apart: 63, of which 28 were waited for; matrix products, arithmetic and copies ran while one was open for 8% of the time, Pallas kernels for 9%

profile of v2, /device:TPU:21, one launch (start us, length us, event | category | flops | bytes accessed | tf_op | source)
XLA Modules:
  0.0 596.2 jit_solution(9217498983724856979)
XLA Ops:
  39.2 16.0 %collective-permute-done.7 = bf16[256,1024]{1,0:T(8,128)(2,1)S(1)} collective-permute-done((bf16[256,1024]{1,0:T(8,128)(2,1)S(1)}, bf16[256,1024]{1,0:T(8,128)(2,1)S(1)}, u32[]{:S(2)}, u32[]{:S(2)}) %collective-permute-start.7) | collective-permute-done | bytes 524320 | tf_op jit(solution)/shard_map/ppermute | solution.py:39
  71.4 8.7 %collective-permute-done.9 = bf16[256,1024]{1,0:T(8,128)(2,1)S(1)} collective-permute-done((bf16[256,1024]{1,0:T(8,128)(2,1)S(1)}, bf16[256,1024]{1,0:T(8,128)(2,1)S(1)}, u32[]{:S(2)}, u32[]{:S(2)}) %collective-permute-start.9) | collective-permute-done | bytes 524320 | tf_op jit(solution)/shard_map/ppermute | solution.py:39
  96.0 18.4 %all-gather.3.cloned.1.call-done = bf16[1,1024,4096]{2,1,0:T(8,128)(2,1)} async-done(((bf16[1,1024,1024]{2,1,0:T(8,128)(2,1)}), bf16[1,1024,4096]{2,1,0:T(8,128)(2,1)}) %all-gather.3.cloned.1.call-update) | async-done | bytes 8388624 | tf_op jit(solution)/shard_map/all_gather | solution.py:709
  114.4 8.0 %output_projection.1 = (bf16[256,1024]{1,0:T(8,128)(2,1)}, bf16[128,1024]{1,0:T(8,128)(2,1)}, bf16[128,1024]{1,0:T(8,128)(2,1)}, bf16[128,1024]{1,0:T(8,128)(2,1...) custom-call(s32[4]{0:T(128)} %and_select_fusion.where_ref, ...), custom_call_target="tpu_custom_call" | custom-call | tf_op jit(solution)/shard_map/output_projection/pallas_call | solution.py:608
  134.6 19.4 %collective-permute-done.15 = bf16[128,1024]{1,0:T(8,128)(2,1)S(1)} collective-permute-done((bf16[128,1024]{1,0:T(8,128)(2,1)}, bf16[128,1024]{1,0:T(8,128)(2,1)S(1)}, u32[]{:S(2)}, u32[]{:S(2)}) %collective-permute-start.15) | collective-permute-done | bytes 262176 | tf_op jit(solution)/shard_map/ppermute | solution.py:39
  154.9 8.3 %collective-permute-start.17 = (bf16[128,1024]{1,0:T(8,128)(2,1)S(1)}, bf16[128,1024]{1,0:T(8,128)(2,1)S(1)}, u32[]{:S(2)}, u32[]{:S(2)}) collective-permute-start(bf16[128,1024]{1,0:T(8,128)(2,1)S(1)} %fusion.32), channel_id=1, source_target_pairs={{16,20},{20,24},{24,28},{28,16},{17,21},{21,25},{25,29},{29,17},{1... | collective-permute-start | bytes 786440 | tf_op jit(solution)/shard_map/ppermute | solution.py:39
  172.1 13.1 %collective-permute-done.19 = bf16[128,1024]{1,0:T(8,128)(2,1)S(1)} collective-permute-done((bf16[128,1024]{1,0:T(8,128)(2,1)S(1)}, bf16[128,1024]{1,0:T(8,128)(2,1)S(1)}, u32[]{:S(2)}, u32[]{:S(2)}) %collective-permute-start.19) | collective-permute-done | bytes 262176 | tf_op jit(solution)/shard_map/ppermute | solution.py:39
  191.3 7.0 %collective-permute-start.28 = (bf16[3,1024,1024]{2,1,0:T(8,128)(2,1)}, bf16[3,1024,1024]{2,1,0:T(8,128)(2,1)}, u32[]{:S(2)}, u32[]{:S(2)}) collective-permute-start(bf16[3,1024,1024]{2,1,0:T(8,128)(2,1)} %collective-permute-done.22.refs_2_), channel_id=1, source_target_pairs={{16,17},{17,16},{18,19},{19,18},{20,21},{21,20},{22,23},{23,22},{2... | collective-permute-start | bytes 18874376 | tf_op jit(solution)/shard_map/ppermute | solution.py:39
  208.4 15.8 %collective-permute-start.24 = (bf16[128,1024]{1,0:T(8,128)(2,1)}, bf16[128,1024]{1,0:T(8,128)(2,1)S(1)}, u32[]{:S(2)}, u32[]{:S(2)}) collective-permute-start(bf16[128,1024]{1,0:T(8,128)(2,1)} %collective-permute-done.23), channel_id=1, source_target_pairs={{16,20},{20,24},{24,28},{28,16},{17,21},{21,25},{25,29},{29,17},{1... | collective-permute-start | bytes 786440 | tf_op jit(solution)/shard_map/ppermute | solution.py:39
  254.0 15.5 %input_projection.1 = (bf16[4,256,1024]{2,1,0:T(8,128)(2,1)}, bf16[4,3,256,256]{3,2,1,0:T(8,128)(2,1)}, f32[256,1]{1,0:T(8,128)}) custom-call(s32[1]{0:T(128)} %bitcast.3.ctx_ref, bf16[256,4096]{1,0:T(8,128)(2,1)} %pad_maximum_fusion.2.rows_ref, bf16[3,1024,1024]{2,1,0:T(8,128)(2,1)} %bitcast.14.weights_ref.refs_0_, ...), custom_call_target="tpu_custom_call" | custom-call | tf_op jit(solution)/shard_map/input_projection/pallas_call | solution.py:416
  278.4 14.8 %all-to-all-done.1.proj_ref = bf16[4,3,256,256]{3,2,1,0:T(8,128)(2,1)S(1)} async-done(((bf16[4,3,256,256]{3,2,1,0:T(8,128)(2,1)}), bf16[4,3,256,256]{3,2,1,0:T(8,128)(2,1)S(1)}, u32[]{:S(2)}, u32[]{:S(2)}) %all-to-all-start.1) | async-done | bytes 1572896 | tf_op jit(solution)/shard_map/all_to_all | solution.py:640
  299.4 7.5 %conv_backward.2 = (bf16[4,3,256,256]{3,2,1,0:T(8,128)(2,1)}, f32[128,256]{1,0:T(8,128)}, f32[9,256]{1,0:T(8,128)}) custom-call(bf16[1024,256]{1,0:T(8,128)(2,1)} %bitcast.42.gg_ref, bf16[4,3,256,256]{3,2,1,0:T(8,128)(2,1)} %copy-done.4, f32[9,256]{1,0:T(8,128)} %reshape.182.taps_ref, f32[128,256]{1,0:T(8,128)} %bitcast_multiply_fusion.kern_ref, ...), custom_call_target="tpu_custom_call" | custom-call | tf_op jit(solution)/shard_map/conv_backward/pallas_call | solution.py:345
  311.9 18.6 %all-to-all-done.2.gproj_ref = bf16[4,3,256,256]{3,2,1,0:T(8,128)(2,1)S(1)} async-done(((bf16[4,3,256,256]{3,2,1,0:T(8,128)(2,1)}), bf16[4,3,256,256]{3,2,1,0:T(8,128)(2,1)S(1)}, u32[]{:S(2)}, u32[]{:S(2)}) %all-to-all-start.2) | async-done | bytes 1572896 | tf_op jit(solution)/shard_map/all_to_all | solution.py:640
  331.7 15.9 %input_gradient.1 = (bf16[256,1024]{1,0:T(8,128)(2,1)}, bf16[128,1024]{1,0:T(8,128)(2,1)}, bf16[128,1024]{1,0:T(8,128)(2,1)}, bf16[128,1024]{1,0:T(8,128)(2,1)},...) custom-call(s32[5]{0:T(128)} %pad_add_fusion.ctx_ref, ...), custom_call_target="tpu_custom_call" | custom-call | tf_op jit(solution)/shard_map/input_gradient/pallas_call | solution.py:482
  355.9 13.2 %collective-permute-done.34 = bf16[128,1024]{1,0:T(8,128)(2,1)S(1)} collective-permute-done((bf16[128,1024]{1,0:T(8,128)(2,1)}, bf16[128,1024]{1,0:T(8,128)(2,1)S(1)}, u32[]{:S(2)}, u32[]{:S(2)}) %collective-permute-start.34) | collective-permute-done | bytes 262176 | tf_op jit(solution)/shard_map/ppermute | solution.py:39
  378.0 8.4 %collective-permute-start.38 = (bf16[128,1024]{1,0:T(8,128)(2,1)}, bf16[128,1024]{1,0:T(8,128)(2,1)S(1)}, u32[]{:S(2)}, u32[]{:S(2)}) collective-permute-start(bf16[128,1024]{1,0:T(8,128)(2,1)} %get-tuple-element.140), channel_id=1, source_target_pairs={{16,4},{20,8},{24,12},{28,0},{17,5},{21,9},{25,13},{29,1},{18,6},{... | collective-permute-start | bytes 786440 | tf_op jit(solution)/shard_map/ppermute | solution.py:39
  390.5 13.1 %collective-permute-done.39 = bf16[128,1024]{1,0:T(8,128)(2,1)S(1)} collective-permute-done((bf16[128,1024]{1,0:T(8,128)(2,1)}, bf16[128,1024]{1,0:T(8,128)(2,1)S(1)}, u32[]{:S(2)}, u32[]{:S(2)}) %collective-permute-start.39) | collective-permute-done | bytes 262176 | tf_op jit(solution)/shard_map/ppermute | solution.py:39
  415.2 43.5 %collective-permute-done.49.refs_6_ = bf16[4,1024,256]{2,1,0:T(8,128)(2,1)} collective-permute-done((bf16[4,1024,256]{2,1,0:T(8,128)(2,1)S(1)}, bf16[4,1024,256]{2,1,0:T(8,128)(2,1)}, u32[]{:S(2)}, u32[]{:S(2)}) %collective-permute-start.49) | collective-permute-done | bytes 2097184 | tf_op jit(solution)/shard_map/ppermute | solution.py:39
  483.0 10.5 %collective-permute-done.47 = bf16[256,1024]{1,0:T(8,128)(2,1)} collective-permute-done((bf16[256,1024]{1,0:T(8,128)(2,1)}, bf16[256,1024]{1,0:T(8,128)(2,1)}, u32[]{:S(2)}, u32[]{:S(2)}) %collective-permute-start.47) | collective-permute-done | bytes 524320 | tf_op jit(solution)/shard_map/ppermute | solution.py:39
  523.4 8.4 %conv_backward.3 = (bf16[3,512,256]{2,1,0:T(8,128)(2,1)}, f32[128,256]{1,0:T(8,128)}, f32[9,256]{1,0:T(8,128)}) custom-call(s32[1,1024]{1,0:T(1,128)} %maximum_convert_fusion.1.tokens_ref, f32[512,1]{1,0:T(8,128)} %copy.41.scale_ref, bf16[1024,256]{1,0:T(8,128)(2,1)} %bitcast.75.gg_ref, bf16[1,3,1024,256]{3,2,1,0:T(8,128)(2,1)} %get-tuple-element.160.proj_ref, ...), custom_call_target="tpu_custom_call" | custom-call | tf_op jit(solution)/shard_map/conv_backward/pallas_call | solution.py:345
  532.9 14.0 %all-to-all-done.3 = bf16[4,256,1024]{2,1,0:T(8,128)(2,1)} async-done(((bf16[4,256,1024]{2,1,0:T(8,128)(2,1)}), bf16[4,256,1024]{2,1,0:T(8,128)(2,1)}, u32[]{:S(2)}, u32[]{:S(2)}) %all-to-all-start.3) | async-done | bytes 2097184 | tf_op jit(solution)/shard_map/all_to_all | solution.py:640
  565.3 7.6 %grad_project_out.1 = f32[1024,1024]{1,0:T(8,128)} custom-call(s32[5]{0:T(128)} %stack.161.where_ref, bf16[1024,1024]{1,0:T(8,128)(2,1)} %bitcast.68.right_ref, bf16[1024,256]{1,0:T(8,128)(2,1)} %get-tuple-element.166.refs_0_, bf16[1024,256]{1,0:T(8,128)(2,1)} %collective-permute-done.29.refs_1_, bf16[1024,256]{1,0:T(8,128)(2,1)} %collective-permute-done.30.refs_2_, ...), custom_call_target="tpu_custom_call" | custom-call | tf_op jit(solution)/shard_map/grad_project_out/pallas_call | solution.py:558
  572.9 15.5 %conditional.1 = (f32[3,1024,1024]{2,1,0:T(8,128)}) conditional(s32[]{:T(128)} %convert_element_type.120, (s32[]{:T(128)}, bf16[1024,1024]{0,1:T(8,128)(2,1)}, bf16[4,1024,256]{2,1,0:T(8,128)(2,1)S(1)}, bf16[4,1024,256]{2,1,0:T(8,128)(2,1)}, bf16[4,1024,256]{2,1,0:T(8,128)(2,1)}, /*index=5*/bf16[4,1024,256]{2,1,0:T(8,128)(2,1)}) %tuple.33, ...), branch_computations={%region_1.2_spmd, %region_2.3_spmd} | conditional | bytes 5242916 | solution.py:775
  576.9 11.5 %grad_project_in.2 = f32[3,1024,1024]{2,1,0:T(8,128)} custom-call(s32[1]{0:T(128)} %bitcast.ctx_ref, bf16[1024,1024]{1,0:T(8,128)(2,1)} %copy.42.left_ref, bf16[4,1024,256]{2,1,0:T(8,128)(2,1)S(1)} %get-tuple-element.29.refs_0_, bf16[4,1024,256]{2,1,0:T(8,128)(2,1)} %get-tuple-element.30.refs_1_, bf16[4,1024,256]{2,1,0:T(8,128)(2,1)} %get-tuple-element.31.refs_2_, ...), custom_call_target="tpu_custom_call" | custom-call | tf_op jit(solution)/shard_map/cond/branch_0_fun/grad_project_in/pallas_call | solution.py:525
  (272 shorter events, 263.5 us)
Async XLA Ops:
  7.2 107.2 %all-gather.3.cloned.1.call-start = ((), (), s32[]{:S(2)}) async-start(), calls=%async_computation.5 | async-start | bytes 10485760 | tf_op jit(solution)/shard_map/all_gather | solution.py:709
  11.3 180.0 %collective-permute-start.22 = (bf16[3,1024,1024]{2,1,0:T(8,128)(2,1)}, bf16[3,1024,1024]{2,1,0:T(8,128)(2,1)}, u32[]{:S(2)}, u32[]{:S(2)}) collective-permute-start(bf16[3,1024,1024]{2,1,0:T(8,128)(2,1)} %bitcast.14.weights_ref.refs_0_), channel_id=1, source_target_pairs={{16,18},{17,19},{18,16},{19,17},{20,22},{21,23},{22,20},{23,21},{2... | collective-permute-start | bytes 18874376 | tf_op jit(solution)/shard_map/ppermute | solution.py:39
  21.7 36.2 %collective-permute-start.5 = (bf16[2,3,512,256]{3,2,1,0:T(8,128)(2,1)}, bf16[2,3,512,256]{3,2,1,0:T(8,128)(2,1)}, u32[]{:S(2)}, u32[]{:S(2)}) collective-permute-start(bf16[2,3,512,256]{3,2,1,0:T(8,128)(2,1)} %table_projection.3), channel_id=1, source_target_pairs={{0,1},{1,0},{2,3},{3,2},{4,5},{5,4},{6,7},{7,6},{8,9},{9,8},{10,11... | collective-permute-start | bytes 4718600 | tf_op jit(solution)/shard_map/ppermute | solution.py:39
  23.5 31.7 %collective-permute-start.7 = (bf16[256,1024]{1,0:T(8,128)(2,1)S(1)}, bf16[256,1024]{1,0:T(8,128)(2,1)S(1)}, u32[]{:S(2)}, u32[]{:S(2)}) collective-permute-start(bf16[256,1024]{1,0:T(8,128)(2,1)S(1)} %copy-done.15), channel_id=1, source_target_pairs={{16,20},{20,24},{24,28},{28,16},{17,21},{21,25},{25,29},{29,17},{1... | collective-permute-start | bytes 1572872 | tf_op jit(solution)/shard_map/ppermute | solution.py:39
  32.1 25.0 %collective-permute-start.3 = (f32[768]{0:T(1024)S(1)}, f32[768]{0:T(1024)S(1)}, u32[]{:S(2)}, u32[]{:S(2)}) collective-permute-start(f32[768]{0:T(1024)S(1)} %pad_maximum_fusion.16), channel_id=1, source_target_pairs={{0,2},{1,3},{2,0},{3,1},{4,6},{5,7},{6,4},{7,5},{8,10},{9,11},{10,... | collective-permute-start | bytes 9224 | tf_op jit(solution)/shard_map/ppermute | solution.py:39
  122.4 32.2 %collective-permute-start.13 = (bf16[256,1024]{1,0:T(8,128)(2,1)}, bf16[256,1024]{1,0:T(8,128)(2,1)S(1)}, u32[]{:S(2)}, u32[]{:S(2)}) collective-permute-start(bf16[256,1024]{1,0:T(8,128)(2,1)} %get-tuple-element.111), channel_id=1, source_target_pairs={{0,16},{4,20},{8,24},{12,28},{1,17},{5,21},{9,25},{13,29},{2,18},{... | collective-permute-start | bytes 1572872 | tf_op jit(solution)/shard_map/ppermute | solution.py:39
  125.2 28.8 %collective-permute-start.15 = (bf16[128,1024]{1,0:T(8,128)(2,1)}, bf16[128,1024]{1,0:T(8,128)(2,1)S(1)}, u32[]{:S(2)}, u32[]{:S(2)}) collective-permute-start(bf16[128,1024]{1,0:T(8,128)(2,1)} %get-tuple-element.113), channel_id=1, source_target_pairs={{0,24},{4,28},{8,16},{12,20},{1,25},{5,29},{9,17},{13,21},{2,26},{... | collective-permute-start | bytes 786440 | tf_op jit(solution)/shard_map/ppermute | solution.py:39
  126.5 27.6 %collective-permute-start.16 = (bf16[128,1024]{1,0:T(8,128)(2,1)}, bf16[128,1024]{1,0:T(8,128)(2,1)S(1)}, u32[]{:S(2)}, u32[]{:S(2)}) collective-permute-start(bf16[128,1024]{1,0:T(8,128)(2,1)} %get-tuple-element.114), channel_id=1, source_target_pairs={{0,28},{4,16},{8,20},{12,24},{1,29},{5,17},{9,21},{13,25},{2,30},{... | collective-permute-start | bytes 786440 | tf_op jit(solution)/shard_map/ppermute | solution.py:39
  164.4 25.6 %collective-permute-start.20 = (bf16[128,1024]{1,0:T(8,128)(2,1)S(1)}, bf16[128,1024]{1,0:T(8,128)(2,1)S(1)}, u32[]{:S(2)}, u32[]{:S(2)}) collective-permute-start(bf16[128,1024]{1,0:T(8,128)(2,1)S(1)} %copy-done.34), channel_id=1, source_target_pairs={{0,24},{4,28},{8,16},{12,20},{1,25},{5,29},{9,17},{13,21},{2,26},{... | collective-permute-start | bytes 786440 | tf_op jit(solution)/shard_map/ppermute | solution.py:39
  165.7 24.3 %collective-permute-start.21 = (bf16[128,1024]{1,0:T(8,128)(2,1)S(1)}, bf16[128,1024]{1,0:T(8,128)(2,1)S(1)}, u32[]{:S(2)}, u32[]{:S(2)}) collective-permute-start(bf16[128,1024]{1,0:T(8,128)(2,1)S(1)} %copy-done.33), channel_id=1, source_target_pairs={{0,28},{4,16},{8,20},{12,24},{1,29},{5,17},{9,21},{13,25},{2,30},{... | collective-permute-start | bytes 786440 | tf_op jit(solution)/shard_map/ppermute | solution.py:39
  185.2 68.8 %collective-permute-start.27 = (bf16[3,1024,1024]{2,1,0:T(8,128)(2,1)}, bf16[3,1024,1024]{2,1,0:T(8,128)(2,1)}, u32[]{:S(2)}, u32[]{:S(2)}) collective-permute-start(bf16[3,1024,1024]{2,1,0:T(8,128)(2,1)} %bitcast.14.weights_ref.refs_0_), channel_id=1, source_target_pairs={{16,17},{17,16},{18,19},{19,18},{20,21},{21,20},{22,23},{23,22},{2... | collective-permute-start | bytes 18874376 | tf_op jit(solution)/shard_map/ppermute | solution.py:39
  191.3 62.7 %collective-permute-start.28 = (bf16[3,1024,1024]{2,1,0:T(8,128)(2,1)}, bf16[3,1024,1024]{2,1,0:T(8,128)(2,1)}, u32[]{:S(2)}, u32[]{:S(2)}) collective-permute-start(bf16[3,1024,1024]{2,1,0:T(8,128)(2,1)} %collective-permute-done.22.refs_2_), channel_id=1, source_target_pairs={{16,17},{17,16},{18,19},{19,18},{20,21},{21,20},{22,23},{23,22},{2... | collective-permute-start | bytes 18874376 | tf_op jit(solution)/shard_map/ppermute | solution.py:39
  208.4 31.9 %collective-permute-start.24 = (bf16[128,1024]{1,0:T(8,128)(2,1)}, bf16[128,1024]{1,0:T(8,128)(2,1)S(1)}, u32[]{:S(2)}, u32[]{:S(2)}) collective-permute-start(bf16[128,1024]{1,0:T(8,128)(2,1)} %collective-permute-done.23), channel_id=1, source_target_pairs={{16,20},{20,24},{24,28},{28,16},{17,21},{21,25},{25,29},{29,17},{1... | collective-permute-start | bytes 786440 | tf_op jit(solution)/shard_map/ppermute | solution.py:39
  269.4 23.7 %all-to-all-start.1 = ((bf16[4,3,256,256]{3,2,1,0:T(8,128)(2,1)}), bf16[4,3,256,256]{3,2,1,0:T(8,128)(2,1)S(1)}, u32[]{:S(2)}, u32[]{:S(2)}) async-start(bf16[4,3,256,256]{3,2,1,0:T(8,128)(2,1)} %get-tuple-element.129), calls=%async_computation.1 | async-start | bytes 3145728 | tf_op jit(solution)/shard_map/all_to_all | solution.py:640
  275.5 31.4 %collective-permute-start.29 = (bf16[1024,256]{1,0:T(8,128)(2,1)S(1)}, bf16[1024,256]{1,0:T(8,128)(2,1)}, u32[]{:S(2)}, u32[]{:S(2)}) collective-permute-start(bf16[1024,256]{1,0:T(8,128)(2,1)S(1)} %copy-done.13), channel_id=1, source_target_pairs={{0,1},{1,0},{2,3},{3,2},{4,5},{5,4},{6,7},{7,6},{8,9},{9,8},{10,11... | collective-permute-start | bytes 1572872 | tf_op jit(solution)/shard_map/ppermute | solution.py:39
  276.9 30.0 %collective-permute-start.31 = (bf16[1024,256]{1,0:T(8,128)(2,1)}, bf16[1024,256]{1,0:T(8,128)(2,1)}, u32[]{:S(2)}, u32[]{:S(2)}) collective-permute-start(bf16[1024,256]{1,0:T(8,128)(2,1)} %collective-permute-done.30.refs_2_), channel_id=1, source_target_pairs={{0,1},{1,0},{2,3},{3,2},{4,5},{5,4},{6,7},{7,6},{8,9},{9,8},{10,11... | collective-permute-start | bytes 1572872 | tf_op jit(solution)/shard_map/ppermute | solution.py:39
  306.9 23.6 %all-to-all-start.2 = ((bf16[4,3,256,256]{3,2,1,0:T(8,128)(2,1)}), bf16[4,3,256,256]{3,2,1,0:T(8,128)(2,1)S(1)}, u32[]{:S(2)}, u32[]{:S(2)}) async-start(bf16[4,3,256,256]{3,2,1,0:T(8,128)(2,1)} %get-tuple-element.152), calls=%async_computation.2 | async-start | bytes 3145728 | tf_op jit(solution)/shard_map/all_to_all | solution.py:640
  347.6 29.5 %collective-permute-start.32 = (bf16[256,1024]{1,0:T(8,128)(2,1)}, bf16[256,1024]{1,0:T(8,128)(2,1)S(1)}, u32[]{:S(2)}, u32[]{:S(2)}) collective-permute-start(bf16[256,1024]{1,0:T(8,128)(2,1)} %get-tuple-element.136), channel_id=1, source_target_pairs={{16,0},{20,4},{24,8},{28,12},{17,1},{21,5},{25,9},{29,13},{18,2},{... | collective-permute-start | bytes 1572872 | tf_op jit(solution)/shard_map/ppermute | solution.py:39
  351.7 23.1 %collective-permute-start.35 = (bf16[128,1024]{1,0:T(8,128)(2,1)}, bf16[128,1024]{1,0:T(8,128)(2,1)S(1)}, u32[]{:S(2)}, u32[]{:S(2)}) collective-permute-start(bf16[128,1024]{1,0:T(8,128)(2,1)} %get-tuple-element.139), channel_id=1, source_target_pairs={{16,12},{20,0},{24,4},{28,8},{17,13},{21,1},{25,5},{29,9},{18,14},... | collective-permute-start | bytes 786440 | tf_op jit(solution)/shard_map/ppermute | solution.py:39
  409.8 48.8 %collective-permute-start.49 = (bf16[4,1024,256]{2,1,0:T(8,128)(2,1)S(1)}, bf16[4,1024,256]{2,1,0:T(8,128)(2,1)}, u32[]{:S(2)}, u32[]{:S(2)}) collective-permute-start(bf16[4,1024,256]{2,1,0:T(8,128)(2,1)S(1)} %pad_maximum_fusion.6.refs_4_), channel_id=1, source_target_pairs={{16,18},{17,19},{18,16},{19,17},{20,22},{21,23},{22,20},{23,21},{2... | collective-permute-start | bytes 6291464 | tf_op jit(solution)/shard_map/ppermute | solution.py:39
  412.5 85.9 %collective-permute-start.48 = (bf16[4,1024,256]{2,1,0:T(8,128)(2,1)S(1)}, bf16[4,1024,256]{2,1,0:T(8,128)(2,1)}, u32[]{:S(2)}, u32[]{:S(2)}) collective-permute-start(bf16[4,1024,256]{2,1,0:T(8,128)(2,1)S(1)} %pad_maximum_fusion.6.refs_4_), channel_id=1, source_target_pairs={{16,17},{17,16},{18,19},{19,18},{20,21},{21,20},{22,23},{23,22},{2... | collective-permute-start | bytes 6291464 | tf_op jit(solution)/shard_map/ppermute | solution.py:39
  458.7 39.7 %collective-permute-start.50 = (bf16[4,1024,256]{2,1,0:T(8,128)(2,1)}, bf16[4,1024,256]{2,1,0:T(8,128)(2,1)}, u32[]{:S(2)}, u32[]{:S(2)}) collective-permute-start(bf16[4,1024,256]{2,1,0:T(8,128)(2,1)} %collective-permute-done.49.refs_6_), channel_id=1, source_target_pairs={{16,17},{17,16},{18,19},{19,18},{20,21},{21,20},{22,23},{23,22},{2... | collective-permute-start | bytes 6291464 | tf_op jit(solution)/shard_map/ppermute | solution.py:39
  469.0 24.5 %collective-permute-start.47 = (bf16[256,1024]{1,0:T(8,128)(2,1)}, bf16[256,1024]{1,0:T(8,128)(2,1)}, u32[]{:S(2)}, u32[]{:S(2)}) collective-permute-start(bf16[256,1024]{1,0:T(8,128)(2,1)} %get-tuple-element.235), channel_id=1, source_target_pairs={{16,19},{17,18},{18,17},{19,16},{20,23},{21,22},{22,21},{23,20},{2... | collective-permute-start | bytes 1572872 | tf_op jit(solution)/shard_map/ppermute | solution.py:39
  516.7 30.2 %all-to-all-start.3 = ((bf16[4,256,1024]{2,1,0:T(8,128)(2,1)}), bf16[4,256,1024]{2,1,0:T(8,128)(2,1)}, u32[]{:S(2)}, u32[]{:S(2)}) async-start(bf16[4,256,1024]{2,1,0:T(8,128)(2,1)} %pad_maximum_fusion.7), calls=%async_computation.3 | async-start | bytes 4194304 | tf_op jit(solution)/shard_map/all_to_all | solution.py:640
  (76 other events, 1161.3 us)
Sparse Core Ops, SparseCore 0:
  9.6 104.7 all-gather.2

commit v3 on v2

--- a/solution.py
+++ b/solution.py
@@ -87,23 +87,24 @@
     return pieces
 
 
-def cross_gather(shares, base, source, early, late=()):
+def cross_gather(shares, base, source, early, late=(), begin=None):
     count = lax.axis_size("dp")
     half = base.shape[0] // 2
+    def move(value, shift):
+        return send(
+            value,
+            ("section", "dp"),
+            lambda s, z: (1 - s, (z + shift) % count) if s == source else None,
+        )
+
     straight, *shares = shares
-    straight = send(straight, ("section", "dp"), lambda s, z: (1 - s, z) if s == source else None)
-    arrivals = [
-        [straight[start : start + half]]
-        + [
-            send(
-                side[shift - 1],
-                ("section", "dp"),
-                lambda s, z: (1 - s, (z + shift) % count) if s == source else None,
-            )
-            for shift in range(1, count)
-        ]
-        for start, side in zip((0, half), shares)
-    ]
+    straight = move(straight, 0)
+    arrivals = [[move(shares[0][shift - 1], shift) for shift in range(1, count)]]
+    tied = together(*arrivals[0], *shares[1])
+    arrivals[0], shares_left = list(tied[: count - 1]), tied[count - 1 :]
+    arrivals.append([move(shares_left[shift - 1], shift) for shift in range(1, count)])
+    for index, start in enumerate((0, half)):
+        arrivals[index].append(straight[start : start + half])
 
     def total(index, values):
         start = index * half
@@ -115,13 +116,16 @@
     part = total(0, arrivals[0])
     if early:
         part, *early = together(part, *early)
+    begun = begin(*early) if begin else []
     first = dp_gather(part, 1 - source)
     marker = min(2, count - 1)
     first[marker], *arrivals[1] = together(first[marker], *arrivals[1])
     part, *late = together(total(1, arrivals[1]), *late)
     second = dp_gather(part, 1 - source)
+    if begun and count > 1:
+        second[1], *begun = together(second[1], *begun)
     stack = jnp.stack([jnp.concatenate(pair, axis=0) for pair in zip(first, second)])
-    return stack, early, late
+    return stack, early, begun or late
 
 
 def in_order(stack, me):
@@ -677,6 +681,12 @@
         table = lax.dynamic_slice_in_dim(
             lax.all_gather(embedding, "dp", axis=1, tiled=True), ctx * feats, feats, 1
         )
+    out_full = lax.all_gather(weights_out, "ctx", axis=1, tiled=True)
+    in_far = far_gather(weights_in, (1,))
+    far = sorted(in_far)[1:]
+    sibling = ctx_xor(weights_in, 1, (0, 1))
+    table, sibling = together(table, sibling)
+
     table_float = table.astype(F32)
     squares = jnp.sum(table_float * table_float, axis=1)
     tokens = token_ids.astype(F32)[None]
@@ -705,10 +715,6 @@
 
     vocabulary = jnp.arange(vocab, dtype=jnp.int32)[None, :]
     first_input = dot((token_ids[:, None] == vocabulary).astype(BF16), embedding)
-
-    out_full = lax.all_gather(weights_out, "ctx", axis=1, tiled=True)
-    in_far = far_gather(weights_in, (1,))
-    far = sorted(in_far)[1:]
 
     order = scatter_order(n_ctx)
     kept = order[: n_ctx // 2]
@@ -734,32 +740,37 @@
     in_far.update(zip(far, late))
     in_pieces = []
     for r in sorted(in_far):
-        in_pieces += [in_far[r], ctx_xor(in_far[r], 1, (1,))]
+        in_pieces += [in_far[r], ctx_xor(in_far[r], 1, (1,)) if r else sibling]
     def gated_gradient(parts):
         total = dot_t(jnp.concatenate(parts, axis=1), out_full).astype(BF16)
         split = jnp.transpose(total.reshape(rows, n_ctx, sub), (1, 0, 2))
         return ctx_swap(split).reshape(seq, sub)
 
     cot_parts = in_order(cot_stack, dp)
-    middle_stack, gated_grad_1 = together(middle_stack, gated_gradient(cot_parts))
     middle_all = jnp.concatenate(in_order(middle_stack, dp), axis=1)
     normed, proj_rows, scale = input_projection(middle_all, in_pieces, ctx)
     proj_1 = ctx_swap(proj_rows)
     gated_1, *saved_1 = conv_forward(proj_1, taps, kern, matrices)
 
     gproj_1, gkern_1, gtaps_1 = conv_backward(
-        gated_grad_1, proj_1, taps, kern, matrices, saved_1
+        gated_gradient(cot_parts), proj_1, taps, kern, matrices, saved_1
     )
     gproj_1, *gated_all_0 = together(gproj_1, *gated_all_0)
     gproj_rows = ctx_swap(gproj_1)
     shares = input_gradient(gproj_rows, in_pieces, middle_all, scale, ctx, dp)
-    back_stack, _, (normed, gproj_1, gated_1) = cross_gather(
-        shares, cotangent, 1, [], [normed, gproj_1, gated_1]
+    def begin_gather(normed, gproj, gated):
+        planes = gproj.transpose(1, 0, 2, 3).reshape(3, seq, sub)
+        planes = far_gather(jnp.concatenate([planes, gated[None]]), (1,))
+        return [normed] + [planes[r] for r in sorted(planes)]
+
+    back_stack, _, (normed, *planes) = cross_gather(
+        shares, cotangent, 1, [normed, gproj_1, gated_1], (), begin_gather
     )
 
     normed_cols = jnp.concatenate([part.T for part in ctx_swap_in(normed, 1)], axis=1)
-    gproj_1 = gproj_1.transpose(1, 0, 2, 3).reshape(3, seq, sub)
-    gproj_all = ctx_gather(jnp.concatenate([gproj_1, gated_1[None]]), (1,))
+    gproj_all = []
+    for plane in planes:
+        gproj_all += [plane, ctx_xor(plane, 1, (1,))]
 
     back_stack, normed_cols, *gproj_all = together(back_stack, normed_cols, *gproj_all)
     back_parts = in_order(back_stack, dp)
@@ -769,7 +780,6 @@
 
     grads = jnp.stack([jnp.where(first, a, b) for a, b in zip(back_parts, cot_parts)])
     grad_cols = ctx_swap(grads).reshape(seq, feats)
-    grad_cols, table_grad = together(grad_cols, table_grad)
     grad_out = grad_out_kernel(gated_all_0, gproj_all, grad_cols, ctx, sec)
     table_pieces = ctx_gather(table_grad, (0,))
     grad_in = lax.cond(

time: 606 us -> 569 us (0.939)
  the two profiles are of different devices: /device:TPU:21 before, /device:TPU:1 now
where the time goes in v3:
time: 569 us; the launch traced here: 561 us
  waiting for transfers between devices  200 us (35%)
  starting transfers between devices  189 us (33%)
  Pallas kernels  92.2 us (16%)
  other arithmetic  35.9 us (6%)
  local copies, waits for them, and re-layouts  19.7 us (3%)
  between operations  15.4 us (3%)
  matrix products  8.58 us (2%)
    ppermute x57, waiting for transfers between devices, send(): return lax.ppermute(value, axes, pairs)  166 us
    ppermute x57, starting transfers between devices, send(): return lax.ppermute(value, axes, pairs)  160 us
    all_to_all x5, waiting for transfers between devices, ctx_swap(): return lax.all_to_all(value, 'ctx', split_axis=0, concat_axis=0, tiled=True)  33.3 us
    all_to_all x5, starting transfers between devices, ctx_swap(): return lax.all_to_all(value, 'ctx', split_axis=0, concat_axis=0, tiled=True)  29.3 us
    pallas_call x1, Pallas kernels, input_gradient(): pl.pallas_call(kernel, grid_spec=pltpu.PrefetchScalarGridSpec(num_scalar_...  16 us
    pallas_call x2, Pallas kernels, conv_backward(): pl.pallas_call(backward_kernel if tokens is None else collect_kernel, out...  15.9 us
    pallas_call x1, Pallas kernels, input_projection(): pl.pallas_call(kernel, grid_spec=pltpu.PrefetchScalarGridSpec(num_scalar_...  15.5 us
  transfers between devices with their start and end apart: 63, of which 24 were waited for; matrix products, arithmetic and copies ran while one was open for 9% of the time, Pallas kernels for 12%

profile of v3, /device:TPU:1, one launch (start us, length us, event | category | flops | bytes accessed | tf_op | source)
XLA Modules:
  0.0 560.7 jit_solution(5844421309841419392)
XLA Ops:
  29.3 12.4 %collective-permute-start.6 = (bf16[2,3,512,256]{3,2,1,0:T(8,128)(2,1)}, bf16[2,3,512,256]{3,2,1,0:T(8,128)(2,1)S(1)}, u32[]{:S(2)}, u32[]{:S(2)}) collective-permute-start(bf16[2,3,512,256]{3,2,1,0:T(8,128)(2,1)} %table_projection.3), channel_id=1, source_target_pairs={{0,1},{1,0},{2,3},{3,2},{4,5},{5,4},{6,7},{7,6},{8,9},{9,8},{10,11... | collective-permute-start | bytes 4718600 | tf_op jit(solution)/shard_map/ppermute | solution.py:39
  45.0 31.9 %collective-permute-start.4 = (f32[768]{0:T(1024)S(1)}, f32[768]{0:T(1024)S(1)}, u32[]{:S(2)}, u32[]{:S(2)}) collective-permute-start(f32[768]{0:T(1024)S(1)} %pad_maximum_fusion.16), channel_id=1, source_target_pairs={{0,2},{1,3},{2,0},{3,1},{4,6},{5,7},{6,4},{7,5},{8,10},{9,11},{10,... | collective-permute-start | bytes 9224 | tf_op jit(solution)/shard_map/ppermute | solution.py:39
  94.6 16.5 %collective-permute-done.7 = bf16[1,3,512,256]{3,2,1,0:T(8,128)(2,1)} collective-permute-done((bf16[1,3,512,256]{3,2,1,0:T(8,128)(2,1)}, bf16[1,3,512,256]{3,2,1,0:T(8,128)(2,1)}, u32[]{:S(2)}, u32[]{:S(2)}) %collective-permute-start.7) | collective-permute-done | bytes 786464 | tf_op jit(solution)/shard_map/ppermute | solution.py:39
  134.4 8.0 %output_projection.1 = (bf16[256,1024]{1,0:T(8,128)(2,1)}, bf16[128,1024]{1,0:T(8,128)(2,1)}, bf16[128,1024]{1,0:T(8,128)(2,1)}, bf16[128,1024]{1,0:T(8,128)(2,1...) custom-call(s32[4]{0:T(128)} %and_select_fusion.where_ref, ...), custom_call_target="tpu_custom_call" | custom-call | tf_op jit(solution)/shard_map/output_projection/pallas_call | solution.py:612
  167.5 7.8 %collective-permute-start.21 = (bf16[128,1024]{1,0:T(8,128)(2,1)S(1)}, bf16[128,1024]{1,0:T(8,128)(2,1)S(1)}, u32[]{:S(2)}, u32[]{:S(2)}) collective-permute-start(bf16[128,1024]{1,0:T(8,128)(2,1)S(1)} %copy-done.37), channel_id=1, source_target_pairs={{0,24},{4,28},{8,16},{12,20},{1,25},{5,29},{9,17},{13,21},{2,26},{... | collective-permute-start | bytes 786440 | tf_op jit(solution)/shard_map/ppermute | solution.py:39
  179.9 6.1 %collective-permute-done.22 = bf16[128,1024]{1,0:T(8,128)(2,1)S(1)} collective-permute-done((bf16[128,1024]{1,0:T(8,128)(2,1)S(1)}, bf16[128,1024]{1,0:T(8,128)(2,1)S(1)}, u32[]{:S(2)}, u32[]{:S(2)}) %collective-permute-start.22) | collective-permute-done | bytes 262176 | tf_op jit(solution)/shard_map/ppermute | solution.py:39
  196.2 13.5 %collective-permute-start.27 = (bf16[128,1024]{1,0:T(8,128)(2,1)}, bf16[128,1024]{1,0:T(8,128)(2,1)S(1)}, u32[]{:S(2)}, u32[]{:S(2)}) collective-permute-start(bf16[128,1024]{1,0:T(8,128)(2,1)} %collective-permute-done.25), channel_id=1, source_target_pairs={{16,20},{20,24},{24,28},{28,16},{17,21},{21,25},{25,29},{29,17},{1... | collective-permute-start | bytes 786440 | tf_op jit(solution)/shard_map/ppermute | solution.py:39
  214.8 15.5 %input_projection.1 = (bf16[4,256,1024]{2,1,0:T(8,128)(2,1)}, bf16[4,3,256,256]{3,2,1,0:T(8,128)(2,1)}, f32[256,1]{1,0:T(8,128)}) custom-call(s32[1]{0:T(128)} %bitcast.3.ctx_ref, bf16[256,4096]{1,0:T(8,128)(2,1)} %pad_maximum_fusion.2.rows_ref, bf16[3,1024,1024]{2,1,0:T(8,128)(2,1)} %bitcast.163, bf16[3,1024,1024]{2,1,0:T(8,128)(2,1)} %collective-permute-done.3.refs_1_, ...), custom_call_target="tpu_custom_call" | custom-call | tf_op jit(solution)/shard_map/input_projection/pallas_call | solution.py:420
  230.3 6.6 %all-to-all-start.1 = ((bf16[4,3,256,256]{3,2,1,0:T(8,128)(2,1)}), bf16[4,3,256,256]{3,2,1,0:T(8,128)(2,1)}, u32[]{:S(2)}, u32[]{:S(2)}) async-start(bf16[4,3,256,256]{3,2,1,0:T(8,128)(2,1)} %get-tuple-element.149), calls=%async_computation.1 | async-start | bytes 3145728 | tf_op jit(solution)/shard_map/all_to_all | solution.py:644
  248.1 8.2 %all-to-all-done.1.proj_ref = bf16[4,3,256,256]{3,2,1,0:T(8,128)(2,1)} async-done(((bf16[4,3,256,256]{3,2,1,0:T(8,128)(2,1)}), bf16[4,3,256,256]{3,2,1,0:T(8,128)(2,1)}, u32[]{:S(2)}, u32[]{:S(2)}) %all-to-all-start.1) | async-done | bytes 1572896 | tf_op jit(solution)/shard_map/all_to_all | solution.py:644
  269.4 7.5 %conv_backward.2 = (bf16[4,3,256,256]{3,2,1,0:T(8,128)(2,1)}, f32[128,256]{1,0:T(8,128)}, f32[9,256]{1,0:T(8,128)}) custom-call(bf16[1024,256]{1,0:T(8,128)(2,1)} %bitcast.173, bf16[4,3,256,256]{3,2,1,0:T(8,128)(2,1)} %all-to-all-done.1.proj_ref, f32[9,256]{1,0:T(8,128)} %reshape.182.taps_ref, f32[128,256]{1,0:T(8,128)} %bitcast_multiply_fusion.kern_ref, ...), custom_call_target="tpu_custom_call" | custom-call | tf_op jit(solution)/shard_map/conv_backward/pallas_call | solution.py:349
  282.8 18.6 %all-to-all-done.2.gproj_ref = bf16[4,3,256,256]{3,2,1,0:T(8,128)(2,1)S(1)} async-done(((bf16[4,3,256,256]{3,2,1,0:T(8,128)(2,1)}), bf16[4,3,256,256]{3,2,1,0:T(8,128)(2,1)S(1)}, u32[]{:S(2)}, u32[]{:S(2)}) %all-to-all-start.2) | async-done | bytes 1572896 | tf_op jit(solution)/shard_map/all_to_all | solution.py:644
  302.6 16.0 %input_gradient.1 = (bf16[256,1024]{1,0:T(8,128)(2,1)}, bf16[128,1024]{1,0:T(8,128)(2,1)}, bf16[128,1024]{1,0:T(8,128)(2,1)}, bf16[128,1024]{1,0:T(8,128)(2,1)},...) custom-call(s32[5]{0:T(128)} %pad_add_fusion.ctx_ref, ...), custom_call_target="tpu_custom_call" | custom-call | tf_op jit(solution)/shard_map/input_gradient/pallas_call | solution.py:486
  323.9 36.3 %collective-permute-done.32 = bf16[128,1024]{1,0:T(8,128)(2,1)S(1)} collective-permute-done((bf16[128,1024]{1,0:T(8,128)(2,1)}, bf16[128,1024]{1,0:T(8,128)(2,1)S(1)}, u32[]{:S(2)}, u32[]{:S(2)}) %collective-permute-start.32) | collective-permute-done | bytes 262176 | tf_op jit(solution)/shard_map/ppermute | solution.py:39
  360.2 8.9 %collective-permute-done.33 = bf16[128,1024]{1,0:T(8,128)(2,1)S(1)} collective-permute-done((bf16[128,1024]{1,0:T(8,128)(2,1)}, bf16[128,1024]{1,0:T(8,128)(2,1)S(1)}, u32[]{:S(2)}, u32[]{:S(2)}) %collective-permute-start.33) | collective-permute-done | bytes 262176 | tf_op jit(solution)/shard_map/ppermute | solution.py:39
  369.1 8.9 %collective-permute-done.35 = bf16[256,1024]{1,0:T(8,128)(2,1)S(1)} collective-permute-done((bf16[256,1024]{1,0:T(8,128)(2,1)}, bf16[256,1024]{1,0:T(8,128)(2,1)S(1)}, u32[]{:S(2)}, u32[]{:S(2)}) %collective-permute-start.35) | collective-permute-done | bytes 524320 | tf_op jit(solution)/shard_map/ppermute | solution.py:39
  393.6 13.1 %collective-permute-done.39 = bf16[128,1024]{1,0:T(8,128)(2,1)S(1)} collective-permute-done((bf16[128,1024]{1,0:T(8,128)(2,1)S(1)}, bf16[128,1024]{1,0:T(8,128)(2,1)S(1)}, u32[]{:S(2)}, u32[]{:S(2)}) %collective-permute-start.39) | collective-permute-done | bytes 262176 | tf_op jit(solution)/shard_map/ppermute | solution.py:39
  406.9 7.8 %collective-permute-start.41 = (bf16[128,1024]{1,0:T(8,128)(2,1)S(1)}, bf16[128,1024]{1,0:T(8,128)(2,1)S(1)}, u32[]{:S(2)}, u32[]{:S(2)}) collective-permute-start(bf16[128,1024]{1,0:T(8,128)(2,1)S(1)} %add_convert_fusion), channel_id=1, source_target_pairs={{0,4},{4,8},{8,12},{12,0},{1,5},{5,9},{9,13},{13,1},{2,6},{6,10},{... | collective-permute-start | bytes 786440 | tf_op jit(solution)/shard_map/ppermute | solution.py:39
  456.8 8.7 %all-to-all-start.3 = ((bf16[4,256,256]{2,1,0:T(8,128)(2,1)}), bf16[4,256,256]{2,1,0:T(8,128)(2,1)}, u32[]{:S(2)}, u32[]{:S(2)}) async-start(bf16[4,256,256]{2,1,0:T(8,128)(2,1)} %bitcast.174), calls=%async_computation.3 | async-start | bytes 1048576 | tf_op jit(solution)/shard_map/all_to_all | solution.py:644
  478.9 8.4 %conv_backward.3 = (bf16[3,512,256]{2,1,0:T(8,128)(2,1)}, f32[128,256]{1,0:T(8,128)}, f32[9,256]{1,0:T(8,128)}) custom-call(s32[1,1024]{1,0:T(1,128)} %maximum_convert_fusion.1.tokens_ref, f32[512,1]{1,0:T(8,128)} %copy.41.scale_ref, bf16[1024,256]{1,0:T(8,128)(2,1)} %bitcast.74.gg_ref, bf16[1,3,1024,256]{3,2,1,0:T(8,128)(2,1)} %get-tuple-element.190.proj_ref, ...), custom_call_target="tpu_custom_call" | custom-call | tf_op jit(solution)/shard_map/conv_backward/pallas_call | solution.py:349
  493.8 29.9 %collective-permute-done.55 = f32[138,256]{1,0:T(8,128)S(1)} collective-permute-done((f32[138,256]{1,0:T(8,128)}, f32[138,256]{1,0:T(8,128)S(1)}, u32[]{:S(2)}, u32[]{:S(2)}) %collective-permute-start.55) | collective-permute-done | bytes 141344 | tf_op jit(solution)/shard_map/ppermute | solution.py:39
  535.5 7.7 %grad_project_out.1 = f32[1024,1024]{1,0:T(8,128)} custom-call(s32[5]{0:T(128)} %stack.160.where_ref, bf16[1024,1024]{1,0:T(8,128)(2,1)} %bitcast.78.right_ref, bf16[1024,256]{1,0:T(8,128)(2,1)} %get-tuple-element.194.refs_0_, bf16[1024,256]{1,0:T(8,128)(2,1)} %copy-done.17, bf16[1024,256]{1,0:T(8,128)(2,1)} %collective-permute-done.30.refs_2_, ...), custom_call_target="tpu_custom_call" | custom-call | tf_op jit(solution)/shard_map/grad_project_out/pallas_call | solution.py:562
  543.2 9.8 %conditional.1 = (f32[3,1024,1024]{2,1,0:T(8,128)}) conditional(s32[]{:T(128)} %convert_element_type.120, (s32[]{:T(128)}, bf16[1024,1024]{0,1:T(8,128)(2,1)}, bf16[4,1024,256]{2,1,0:T(8,128)(2,1)S(1)}, bf16[4,1024,256]{2,1,0:T(8,128)(2,1)}, bf16[4,1024,256]{2,1,0:T(8,128)(2,1)}, /*index=5*/bf16[4,1024,256]{2,1,0:T(8,128)(2,1)}) %tuple.38, ...), branch_computations={%region_1.2_spmd, %region_2.3_spmd} | conditional | bytes 4194312 | solution.py:785
  544.5 8.4 %grad_project_in.3 = f32[3,1024,1024]{2,1,0:T(8,128)} custom-call(s32[1]{0:T(128)} %bitcast.1.ctx_ref, bf16[1024,512]{1,0:T(8,128)(2,1)} %bitcast.172, bf16[3,512,256]{2,1,0:T(8,128)(2,1)} %get-tuple-element.35.refs_0_, bf16[3,512,256]{2,1,0:T(8,128)(2,1)} %get-tuple-element.36.refs_1_, bf16[3,512,256]{2,1,0:T(8,128)(2,1)} %get-tuple-element.37.refs_2_, ...), custom_call_target="tpu_custom_call" | custom-call | tf_op jit(solution)/shard_map/cond/branch_1_fun/grad_project_in/pallas_call | solution.py:529
  (280 shorter events, 238.7 us)
Async XLA Ops:
  7.2 127.2 %all-gather.3.cloned.1.call-start = ((), (), s32[]{:S(2)}) async-start(), calls=%async_computation.5 | async-start | bytes 10485760 | tf_op jit(solution)/shard_map/all_gather | solution.py:684
  12.5 173.8 %collective-permute-start.23 = (bf16[3,1024,1024]{2,1,0:T(8,128)(2,1)}, bf16[3,1024,1024]{2,1,0:T(8,128)(2,1)}, u32[]{:S(2)}, u32[]{:S(2)}) collective-permute-start(bf16[3,1024,1024]{2,1,0:T(8,128)(2,1)} %bitcast.160), channel_id=1, source_target_pairs={{16,18},{17,19},{18,16},{19,17},{20,22},{21,23},{22,20},{23,21},{2... | collective-permute-start | bytes 18874376 | tf_op jit(solution)/shard_map/ppermute | solution.py:39
  18.7 23.7 %collective-permute-start.8 = (bf16[256,1024]{1,0:T(8,128)(2,1)S(1)}, bf16[256,1024]{1,0:T(8,128)(2,1)}, u32[]{:S(2)}, u32[]{:S(2)}) collective-permute-start(bf16[256,1024]{1,0:T(8,128)(2,1)S(1)} %copy-done.12), channel_id=1, source_target_pairs={{16,20},{20,24},{24,28},{28,16},{17,21},{21,25},{25,29},{29,17},{1... | collective-permute-start | bytes 1572872 | tf_op jit(solution)/shard_map/ppermute | solution.py:39
  29.3 57.3 %collective-permute-start.6 = (bf16[2,3,512,256]{3,2,1,0:T(8,128)(2,1)}, bf16[2,3,512,256]{3,2,1,0:T(8,128)(2,1)S(1)}, u32[]{:S(2)}, u32[]{:S(2)}) collective-permute-start(bf16[2,3,512,256]{3,2,1,0:T(8,128)(2,1)} %table_projection.3), channel_id=1, source_target_pairs={{0,1},{1,0},{2,3},{3,2},{4,5},{5,4},{6,7},{7,6},{8,9},{9,8},{10,11... | collective-permute-start | bytes 4718600 | tf_op jit(solution)/shard_map/ppermute | solution.py:39
  42.4 35.8 %collective-permute-start.9 = (bf16[256,1024]{1,0:T(8,128)(2,1)}, bf16[256,1024]{1,0:T(8,128)(2,1)S(1)}, u32[]{:S(2)}, u32[]{:S(2)}) collective-permute-start(bf16[256,1024]{1,0:T(8,128)(2,1)} %collective-permute-done.8), channel_id=1, source_target_pairs={{16,20},{20,24},{24,28},{28,16},{17,21},{21,25},{25,29},{29,17},{1... | collective-permute-start | bytes 1572872 | tf_op jit(solution)/shard_map/ppermute | solution.py:39
  45.0 39.1 %collective-permute-start.4 = (f32[768]{0:T(1024)S(1)}, f32[768]{0:T(1024)S(1)}, u32[]{:S(2)}, u32[]{:S(2)}) collective-permute-start(f32[768]{0:T(1024)S(1)} %pad_maximum_fusion.16), channel_id=1, source_target_pairs={{0,2},{1,3},{2,0},{3,1},{4,6},{5,7},{6,4},{7,5},{8,10},{9,11},{10,... | collective-permute-start | bytes 9224 | tf_op jit(solution)/shard_map/ppermute | solution.py:39
  186.3 28.5 %collective-permute-start.28 = (bf16[3,1024,1024]{2,1,0:T(8,128)(2,1)}, bf16[3,1024,1024]{2,1,0:T(8,128)(2,1)}, u32[]{:S(2)}, u32[]{:S(2)}) collective-permute-start(bf16[3,1024,1024]{2,1,0:T(8,128)(2,1)} %collective-permute-done.23.refs_2_), channel_id=1, source_target_pairs={{16,17},{17,16},{18,19},{19,18},{20,21},{21,20},{22,23},{23,22},{2... | collective-permute-start | bytes 18874376 | tf_op jit(solution)/shard_map/ppermute | solution.py:39
  192.3 46.8 %collective-permute-start.30 = (bf16[1024,256]{1,0:T(8,128)(2,1)}, bf16[1024,256]{1,0:T(8,128)(2,1)}, u32[]{:S(2)}, u32[]{:S(2)}) collective-permute-start(bf16[1024,256]{1,0:T(8,128)(2,1)} %get-tuple-element.194.refs_0_), channel_id=1, source_target_pairs={{0,2},{1,3},{2,0},{3,1},{4,6},{5,7},{6,4},{7,5},{8,10},{9,11},{10,... | collective-permute-start | bytes 1572872 | tf_op jit(solution)/shard_map/ppermute | solution.py:39
  230.3 25.9 %all-to-all-start.1 = ((bf16[4,3,256,256]{3,2,1,0:T(8,128)(2,1)}), bf16[4,3,256,256]{3,2,1,0:T(8,128)(2,1)}, u32[]{:S(2)}, u32[]{:S(2)}) async-start(bf16[4,3,256,256]{3,2,1,0:T(8,128)(2,1)} %get-tuple-element.149), calls=%async_computation.1 | async-start | bytes 3145728 | tf_op jit(solution)/shard_map/all_to_all | solution.py:644
  237.1 39.7 %collective-permute-start.29 = (bf16[1024,256]{1,0:T(8,128)(2,1)}, bf16[1024,256]{1,0:T(8,128)(2,1)S(1)}, u32[]{:S(2)}, u32[]{:S(2)}) collective-permute-start(bf16[1024,256]{1,0:T(8,128)(2,1)} %get-tuple-element.194.refs_0_), channel_id=1, source_target_pairs={{0,1},{1,0},{2,3},{3,2},{4,5},{5,4},{6,7},{7,6},{8,9},{9,8},{10,11... | collective-permute-start | bytes 1572872 | tf_op jit(solution)/shard_map/ppermute | solution.py:39
  239.1 37.7 %collective-permute-start.31 = (bf16[1024,256]{1,0:T(8,128)(2,1)}, bf16[1024,256]{1,0:T(8,128)(2,1)S(1)}, u32[]{:S(2)}, u32[]{:S(2)}) collective-permute-start(bf16[1024,256]{1,0:T(8,128)(2,1)} %collective-permute-done.30.refs_2_), channel_id=1, source_target_pairs={{0,1},{1,0},{2,3},{3,2},{4,5},{5,4},{6,7},{7,6},{8,9},{9,8},{10,11... | collective-permute-start | bytes 1572872 | tf_op jit(solution)/shard_map/ppermute | solution.py:39
  277.8 23.6 %all-to-all-start.2 = ((bf16[4,3,256,256]{3,2,1,0:T(8,128)(2,1)}), bf16[4,3,256,256]{3,2,1,0:T(8,128)(2,1)S(1)}, u32[]{:S(2)}, u32[]{:S(2)}) async-start(bf16[4,3,256,256]{3,2,1,0:T(8,128)(2,1)} %get-tuple-element.177), calls=%async_computation.2 | async-start | bytes 3145728 | tf_op jit(solution)/shard_map/all_to_all | solution.py:644
  318.5 59.5 %collective-permute-start.35 = (bf16[256,1024]{1,0:T(8,128)(2,1)}, bf16[256,1024]{1,0:T(8,128)(2,1)S(1)}, u32[]{:S(2)}, u32[]{:S(2)}) collective-permute-start(bf16[256,1024]{1,0:T(8,128)(2,1)} %get-tuple-element.165), channel_id=1, source_target_pairs={{16,0},{20,4},{24,8},{28,12},{17,1},{21,5},{25,9},{29,13},{18,2},{... | collective-permute-start | bytes 1572872 | tf_op jit(solution)/shard_map/ppermute | solution.py:39
  320.0 40.2 %collective-permute-start.32 = (bf16[128,1024]{1,0:T(8,128)(2,1)}, bf16[128,1024]{1,0:T(8,128)(2,1)S(1)}, u32[]{:S(2)}, u32[]{:S(2)}) collective-permute-start(bf16[128,1024]{1,0:T(8,128)(2,1)} %get-tuple-element.156), channel_id=1, source_target_pairs={{16,4},{20,8},{24,12},{28,0},{17,5},{21,9},{25,13},{29,1},{18,6},{... | collective-permute-start | bytes 786440 | tf_op jit(solution)/shard_map/ppermute | solution.py:39
  321.3 47.8 %collective-permute-start.33 = (bf16[128,1024]{1,0:T(8,128)(2,1)}, bf16[128,1024]{1,0:T(8,128)(2,1)S(1)}, u32[]{:S(2)}, u32[]{:S(2)}) collective-permute-start(bf16[128,1024]{1,0:T(8,128)(2,1)} %get-tuple-element.157), channel_id=1, source_target_pairs={{16,8},{20,12},{24,0},{28,4},{17,9},{21,13},{25,1},{29,5},{18,10},... | collective-permute-start | bytes 786440 | tf_op jit(solution)/shard_map/ppermute | solution.py:39
  322.6 46.5 %collective-permute-start.34 = (bf16[128,1024]{1,0:T(8,128)(2,1)}, bf16[128,1024]{1,0:T(8,128)(2,1)S(1)}, u32[]{:S(2)}, u32[]{:S(2)}) collective-permute-start(bf16[128,1024]{1,0:T(8,128)(2,1)} %get-tuple-element.158), channel_id=1, source_target_pairs={{16,12},{20,0},{24,4},{28,8},{17,13},{21,1},{25,5},{29,9},{18,14},... | collective-permute-start | bytes 786440 | tf_op jit(solution)/shard_map/ppermute | solution.py:39
  378.6 42.0 %collective-permute-start.42 = (bf16[4,1024,256]{2,1,0:T(8,128)(2,1)S(1)}, bf16[4,1024,256]{2,1,0:T(8,128)(2,1)}, u32[]{:S(2)}, u32[]{:S(2)}) collective-permute-start(bf16[4,1024,256]{2,1,0:T(8,128)(2,1)S(1)} %pad_maximum_fusion.3.refs_4_), channel_id=1, source_target_pairs={{16,18},{17,19},{18,16},{19,17},{20,22},{21,23},{22,20},{23,21},{2... | collective-permute-start | bytes 6291464 | tf_op jit(solution)/shard_map/ppermute | solution.py:39
  383.9 22.7 %collective-permute-start.39 = (bf16[128,1024]{1,0:T(8,128)(2,1)S(1)}, bf16[128,1024]{1,0:T(8,128)(2,1)S(1)}, u32[]{:S(2)}, u32[]{:S(2)}) collective-permute-start(bf16[128,1024]{1,0:T(8,128)(2,1)S(1)} %copy-done.34), channel_id=1, source_target_pairs={{16,8},{20,12},{24,0},{28,4},{17,9},{21,13},{25,1},{29,5},{18,10},... | collective-permute-start | bytes 786440 | tf_op jit(solution)/shard_map/ppermute | solution.py:39
  420.6 29.5 %collective-permute-start.49 = (bf16[4,1024,256]{2,1,0:T(8,128)(2,1)S(1)}, bf16[4,1024,256]{2,1,0:T(8,128)(2,1)}, u32[]{:S(2)}, u32[]{:S(2)}) collective-permute-start(bf16[4,1024,256]{2,1,0:T(8,128)(2,1)S(1)} %pad_maximum_fusion.3.refs_4_), channel_id=1, source_target_pairs={{16,17},{17,16},{18,19},{19,18},{20,21},{21,20},{22,23},{23,22},{2... | collective-permute-start | bytes 6291464 | tf_op jit(solution)/shard_map/ppermute | solution.py:39
  422.6 27.5 %collective-permute-start.50 = (bf16[4,1024,256]{2,1,0:T(8,128)(2,1)}, bf16[4,1024,256]{2,1,0:T(8,128)(2,1)}, u32[]{:S(2)}, u32[]{:S(2)}) collective-permute-start(bf16[4,1024,256]{2,1,0:T(8,128)(2,1)} %collective-permute-done.42.refs_6_), channel_id=1, source_target_pairs={{16,17},{17,16},{18,19},{19,18},{20,21},{21,20},{22,23},{23,22},{2... | collective-permute-start | bytes 6291464 | tf_op jit(solution)/shard_map/ppermute | solution.py:39
  473.6 61.9 %all-to-all-start.4 = ((bf16[4,256,1024]{2,1,0:T(8,128)(2,1)}), bf16[4,256,1024]{2,1,0:T(8,128)(2,1)}, u32[]{:S(2)}, u32[]{:S(2)}) async-start(bf16[4,256,1024]{2,1,0:T(8,128)(2,1)} %pad_maximum_fusion.7), calls=%async_computation.4 | async-start | bytes 4194304 | tf_op jit(solution)/shard_map/all_to_all | solution.py:644
  487.3 39.9 %collective-permute-start.52 = (bf16[3,512,256]{2,1,0:T(8,128)(2,1)}, bf16[3,512,256]{2,1,0:T(8,128)(2,1)}, u32[]{:S(2)}, u32[]{:S(2)}) collective-permute-start(bf16[3,512,256]{2,1,0:T(8,128)(2,1)} %get-tuple-element.193), channel_id=1, source_target_pairs={{0,2},{1,3},{2,0},{3,1},{4,6},{5,7},{6,4},{7,5},{8,10},{9,11},{10,... | collective-permute-start | bytes 2359304 | tf_op jit(solution)/shard_map/ppermute | solution.py:39
  493.1 30.6 %collective-permute-start.55 = (f32[138,256]{1,0:T(8,128)}, f32[138,256]{1,0:T(8,128)S(1)}, u32[]{:S(2)}, u32[]{:S(2)}) collective-permute-start(f32[138,256]{1,0:T(8,128)} %pad_maximum_fusion.13), channel_id=1, source_target_pairs={{0,2},{1,3},{2,0},{3,1},{16,18},{17,19},{18,16},{19,17},{4,6},{5,7... | collective-permute-start | bytes 423944 | tf_op jit(solution)/shard_map/ppermute | solution.py:39
  493.2 36.6 %collective-permute-start.54 = (f32[138,256]{1,0:T(8,128)}, f32[138,256]{1,0:T(8,128)}, u32[]{:S(2)}, u32[]{:S(2)}) collective-permute-start(f32[138,256]{1,0:T(8,128)} %pad_maximum_fusion.13), channel_id=1, source_target_pairs={{0,1},{1,0},{2,3},{3,2},{16,17},{17,16},{18,19},{19,18},{4,5},{5,4... | collective-permute-start | bytes 423944 | tf_op jit(solution)/shard_map/ppermute | solution.py:39
  (80 other events, 1154.7 us)
Sparse Core Ops, SparseCore 0:
  9.6 60.7 all-gather.2

commit v4 on v3

--- a/solution.py
+++ b/solution.py
@@ -120,8 +120,9 @@
     first = dp_gather(part, 1 - source)
     marker = min(2, count - 1)
     first[marker], *arrivals[1] = together(first[marker], *arrivals[1])
-    part, *late = together(total(1, arrivals[1]), *late)
-    second = dp_gather(part, 1 - source)
+    second = dp_gather(total(1, arrivals[1]), 1 - source)
+    if late:
+        first[-1], second[-1], *late = together(first[-1], second[-1], *late)
     if begun and count > 1:
         second[1], *begun = together(second[1], *begun)
     stack = jnp.stack([jnp.concatenate(pair, axis=0) for pair in zip(first, second)])
@@ -392,11 +393,11 @@
 def input_projection(rows_in, pieces, ctx):
     rows, full_width = rows_in.shape
     feats, chans = pieces[0].shape[1:]
-    count = len(pieces)
-    sub = chans // count
+    count = full_width // feats
+    places = sorted(pieces)
 
     def kernel(ctx_ref, rows_ref, *refs):
-        weights, (normed_ref, proj_ref, scale_ref) = refs[:count], refs[count:]
+        weights, (normed_ref, part_ref, scale_ref) = refs[: len(places)], refs[len(places) :]
 
         @pl.when(pl.program_id(0) == 0)
         def _():
@@ -410,12 +411,10 @@
                 normed_ref[q] = (part * scale_ref[...]).astype(BF16)
 
         total = jnp.zeros((rows, chans), F32)
-        for r in range(count):
+        for r, weight in zip(places, weights):
             start = pl.multiple_of((ctx_ref[0] ^ r) * feats, feats)
-            total = total + dot(rows_ref[:, pl.ds(start, feats)], weights[r][0])
-        total = (total * scale_ref[...]).astype(BF16)
-        for q in range(count):
-            proj_ref[q, 0] = total[:, q * sub : (q + 1) * sub]
+            total = total + dot(rows_ref[:, pl.ds(start, feats)], weight[0])
+        part_ref[0] = total
 
     return pl.pallas_call(
         kernel,
@@ -423,21 +422,58 @@
             num_scalar_prefetch=1,
             grid=(3,),
             in_specs=[pl.BlockSpec((rows, full_width), lambda m, ctx: (0, 0))]
-            + [pl.BlockSpec((1, feats, chans), lambda m, ctx: (m, 0, 0))] * count,
+            + [pl.BlockSpec((1, feats, chans), lambda m, ctx: (m, 0, 0))] * len(places),
             out_specs=[
                 pl.BlockSpec((count, rows, feats), lambda m, ctx: (0, 0, 0)),
-                pl.BlockSpec((count, 1, rows, sub), lambda m, ctx: (0, m, 0, 0)),
+                pl.BlockSpec((1, rows, chans), lambda m, ctx: (m, 0, 0)),
                 pl.BlockSpec((rows, 1), lambda m, ctx: (0, 0)),
             ],
         ),
         out_shape=(
             jax.ShapeDtypeStruct((count, rows, feats), BF16),
-            jax.ShapeDtypeStruct((count, 3, rows, sub), BF16),
+            jax.ShapeDtypeStruct((3, rows, chans), F32),
             jax.ShapeDtypeStruct((rows, 1), F32),
         ),
         compiler_params=PARAMS,
         name="input_projection",
-    )(ctx[None], rows_in, *pieces)
+    )(ctx[None], rows_in, *[pieces[r] for r in places])
+
+
+def input_projection_rest(rows_in, pieces, part, scale, ctx):
+    rows, full_width = rows_in.shape
+    chans = part.shape[2]
+    feats = next(iter(pieces.values())).shape[1]
+    count = full_width // feats
+    sub = chans // count
+    places = sorted(pieces)
+
+    def kernel(ctx_ref, rows_ref, part_ref, scale_ref, *refs):
+        weights, proj_ref = refs[:-1], refs[-1]
+        total = part_ref[0]
+        for r, weight in zip(places, weights):
+            start = pl.multiple_of((ctx_ref[0] ^ r) * feats, feats)
+            total = total + dot(rows_ref[:, pl.ds(start, feats)], weight[0])
+        total = (total * scale_ref[...]).astype(BF16)
+        for q in range(count):
+            proj_ref[q, 0] = total[:, q * sub : (q + 1) * sub]
+
+    return pl.pallas_call(
+        kernel,
+        grid_spec=pltpu.PrefetchScalarGridSpec(
+            num_scalar_prefetch=1,
+            grid=(3,),
+            in_specs=[
+                pl.BlockSpec((rows, full_width), lambda m, ctx: (0, 0)),
+                pl.BlockSpec((1, rows, chans), lambda m, ctx: (m, 0, 0)),
+                pl.BlockSpec((rows, 1), lambda m, ctx: (0, 0)),
+            ]
+            + [pl.BlockSpec((1, feats, chans), lambda m, ctx: (m, 0, 0))] * len(places),
+            out_specs=pl.BlockSpec((count, 1, rows, sub), lambda m, ctx: (0, m, 0, 0)),
+        ),
+        out_shape=jax.ShapeDtypeStruct((count, 3, rows, sub), BF16),
+        compiler_params=PARAMS,
+        name="input_projection_rest",
+    )(ctx[None], rows_in, part, scale, *[pieces[r] for r in places])
 
 
 def input_gradient(gproj, pieces, rows_in, scale, ctx, dp):
@@ -684,8 +720,7 @@
     out_full = lax.all_gather(weights_out, "ctx", axis=1, tiled=True)
     in_far = far_gather(weights_in, (1,))
     far = sorted(in_far)[1:]
-    sibling = ctx_xor(weights_in, 1, (0, 1))
-    table, sibling = together(table, sibling)
+    sibling = ctx_xor(weights_in, 1, (1,))
 
     table_float = table.astype(F32)
     squares = jnp.sum(table_float * table_float, axis=1)
@@ -729,7 +764,7 @@
     table_proj = (partial[0] * table_inv).astype(BF16)
     gated_0, *saved_0, proj_0 = conv_forward(table_proj, taps, kern, matrices, tokens)
     cot_stack = jnp.stack(dp_gather(cotangent, 1))
-    gated_0, cot_stack = together(gated_0, cot_stack)
+    gated_0, cot_stack, sibling = together(gated_0, cot_stack, sibling)
     gated_rows = jnp.stack(ctx_swap_in(gated_0.reshape(n_ctx, rows, sub), 0))
     shares = output_projection(gated_rows, out_full, dp)
     middle_stack, (gated_0,), late = cross_gather(
@@ -748,8 +783,10 @@
 
     cot_parts = in_order(cot_stack, dp)
     middle_all = jnp.concatenate(in_order(middle_stack, dp), axis=1)
-    normed, proj_rows, scale = input_projection(middle_all, in_pieces, ctx)
-    proj_1 = ctx_swap(proj_rows)
+    soon = {r: in_pieces[r] for r in range(n_ctx) if r == 1 or r % 2 == 0}
+    rest = {r: in_pieces[r] for r in range(n_ctx) if r not in soon}
+    normed, part, scale = input_projection(middle_all, soon, ctx)
+    proj_1 = ctx_swap(input_projection_rest(middle_all, rest, part, scale, ctx))
     gated_1, *saved_1 = conv_forward(proj_1, taps, kern, matrices)
 
     gproj_1, gkern_1, gtaps_1 = conv_backward(

time: 569 us -> 572 us (level)
  starting transfers between devices: 189 us -> 178 us
  waiting for transfers between devices: 200 us -> 207 us
    ppermute x57, starting transfers between devices: 160 us -> 149 us  [send(): return lax.ppermute(value, axes, pairs)]
    pallas_call x0 -> x1, Pallas kernels: none -> 7.19 us  [input_projection_rest(): pl.pallas_call(kernel, grid_spec=pltpu.PrefetchScalarGridSpec(num_scalar_...]
    ppermute x57, waiting for transfers between devices: 166 us -> 173 us  [send(): return lax.ppermute(value, axes, pairs)]
  transfers between devices with their start and end apart: 63 -> 63, of which waited for: 24 -> 25; matrix products, arithmetic and copies ran while one was open for 9% -> 9% of each run, Pallas kernels for 12% -> 13%
where the time goes in v4:
time: 572 us; the launch traced here: 564 us
  waiting for transfers between devices  207 us (36%)
  starting transfers between devices  178 us (31%)
  Pallas kernels  97.1 us (17%)
  other arithmetic  35.3 us (6%)
  local copies, waits for them, and re-layouts  23.6 us (4%)
  between operations  15.5 us (3%)
  matrix products  8.58 us (2%)
    ppermute x57, waiting for transfers between devices, send(): return lax.ppermute(value, axes, pairs)  173 us
    ppermute x57, starting transfers between devices, send(): return lax.ppermute(value, axes, pairs)  149 us
    all_to_all x5, waiting for transfers between devices, ctx_swap(): return lax.all_to_all(value, 'ctx', split_axis=0, concat_axis=0, tiled=True)  33.3 us
    all_to_all x5, starting transfers between devices, ctx_swap(): return lax.all_to_all(value, 'ctx', split_axis=0, concat_axis=0, tiled=True)  28.5 us
    pallas_call x1, Pallas kernels, input_gradient(): pl.pallas_call(kernel, grid_spec=pltpu.PrefetchScalarGridSpec(num_scalar_...  15.9 us
    pallas_call x2, Pallas kernels, conv_backward(): pl.pallas_call(backward_kernel if tokens is None else collect_kernel, out...  15.8 us
    pallas_call x1, Pallas kernels, input_projection(): pl.pallas_call(kernel, grid_spec=pltpu.PrefetchScalarGridSpec(num_scalar_...  13.2 us
  transfers between devices with their start and end apart: 63, of which 25 were waited for; matrix products, arithmetic and copies ran while one was open for 9% of the time, Pallas kernels for 13%

profile of v4, /device:TPU:1, one launch (start us, length us, event | category | flops | bytes accessed | tf_op | source)
XLA Modules:
  0.0 564.4 jit_solution(12301531771169317955)
XLA Ops:
  31.8 12.8 %collective-permute-start.5 = (bf16[2,3,512,256]{3,2,1,0:T(8,128)(2,1)}, bf16[2,3,512,256]{3,2,1,0:T(8,128)(2,1)}, u32[]{:S(2)}, u32[]{:S(2)}) collective-permute-start(bf16[2,3,512,256]{3,2,1,0:T(8,128)(2,1)} %table_projection.3), channel_id=1, source_target_pairs={{0,1},{1,0},{2,3},{3,2},{4,5},{5,4},{6,7},{7,6},{8,9},{9,8},{10,11... | collective-permute-start | bytes 4718600 | tf_op jit(solution)/shard_map/ppermute | solution.py:39
  47.9 20.5 %collective-permute-start.3 = (f32[768]{0:T(1024)S(1)}, f32[768]{0:T(1024)S(1)}, u32[]{:S(2)}, u32[]{:S(2)}) collective-permute-start(f32[768]{0:T(1024)S(1)} %pad_maximum_fusion.16), channel_id=1, source_target_pairs={{0,2},{1,3},{2,0},{3,1},{4,6},{5,7},{6,4},{7,5},{8,10},{9,11},{10,... | collective-permute-start | bytes 9224 | tf_op jit(solution)/shard_map/ppermute | solution.py:39
  89.7 14.6 %collective-permute-done.6 = bf16[1,3,512,256]{3,2,1,0:T(8,128)(2,1)} collective-permute-done((bf16[1,3,512,256]{3,2,1,0:T(8,128)(2,1)}, bf16[1,3,512,256]{3,2,1,0:T(8,128)(2,1)}, u32[]{:S(2)}, u32[]{:S(2)}) %collective-permute-start.6) | collective-permute-done | bytes 786464 | tf_op jit(solution)/shard_map/ppermute | solution.py:39
  127.1 8.0 %output_projection.1 = (bf16[256,1024]{1,0:T(8,128)(2,1)}, bf16[128,1024]{1,0:T(8,128)(2,1)}, bf16[128,1024]{1,0:T(8,128)(2,1)}, bf16[128,1024]{1,0:T(8,128)(2,1...) custom-call(s32[4]{0:T(128)} %and_select_fusion.where_ref, ...), custom_call_target="tpu_custom_call" | custom-call | tf_op jit(solution)/shard_map/output_projection/pallas_call | solution.py:648
  141.0 6.2 %collective-permute-done.14 = bf16[128,1024]{1,0:T(8,128)(2,1)S(1)} collective-permute-done((bf16[128,1024]{1,0:T(8,128)(2,1)}, bf16[128,1024]{1,0:T(8,128)(2,1)S(1)}, u32[]{:S(2)}, u32[]{:S(2)}) %collective-permute-start.14) | collective-permute-done | bytes 262176 | tf_op jit(solution)/shard_map/ppermute | solution.py:39
  187.6 15.0 %collective-permute-start.30 = (bf16[1024,256]{1,0:T(8,128)(2,1)}, bf16[1024,256]{1,0:T(8,128)(2,1)}, u32[]{:S(2)}, u32[]{:S(2)}) collective-permute-start(bf16[1024,256]{1,0:T(8,128)(2,1)} %get-tuple-element.194.refs_0_), channel_id=1, source_target_pairs={{0,2},{1,3},{2,0},{3,1},{4,6},{5,7},{6,4},{7,5},{8,10},{9,11},{10,... | collective-permute-start | bytes 1572872 | tf_op jit(solution)/shard_map/ppermute | solution.py:39
  206.8 13.2 %input_projection.1 = (bf16[4,256,1024]{2,1,0:T(8,128)(2,1)}, f32[3,256,1024]{2,1,0:T(8,128)}, f32[256,1]{1,0:T(8,128)}) custom-call(s32[1]{0:T(128)} %bitcast.3.ctx_ref, bf16[256,4096]{1,0:T(8,128)(2,1)} %pad_maximum_fusion.2.rows_ref, bf16[3,1024,1024]{2,1,0:T(8,128)(2,1)} %bitcast.163, bf16[3,1024,1024]{2,1,0:T(8,128)(2,1)} %collective-permute-done.10.refs_1_, ...), custom_call_target="tpu_custom_call" | custom-call | tf_op jit(solution)/shard_map/input_projection/pallas_call | solution.py:419
  220.0 7.2 %input_projection_rest.1 = bf16[4,3,256,256]{3,2,1,0:T(8,128)(2,1)} custom-call(s32[1]{0:T(128)} %bitcast.3.ctx_ref, bf16[256,4096]{1,0:T(8,128)(2,1)} %pad_maximum_fusion.2.rows_ref, f32[3,256,1024]{2,1,0:T(8,128)} %get-tuple-element.149.part_ref, f32[256,1]{1,0:T(8,128)} %get-tuple-element.150.scale_ref, ...), custom_call_target="tpu_custom_call" | custom-call | tf_op jit(solution)/shard_map/input_projection_rest/pallas_call | solution.py:460
  227.2 6.6 %all-to-all-start.1 = ((bf16[4,3,256,256]{3,2,1,0:T(8,128)(2,1)}), bf16[4,3,256,256]{3,2,1,0:T(8,128)(2,1)}, u32[]{:S(2)}, u32[]{:S(2)}) async-start(bf16[4,3,256,256]{3,2,1,0:T(8,128)(2,1)} %input_projection_rest.1), calls=%async_computation.1 | async-start | bytes 3145728 | tf_op jit(solution)/shard_map/all_to_all | solution.py:680
  244.9 8.2 %all-to-all-done.1.proj_ref = bf16[4,3,256,256]{3,2,1,0:T(8,128)(2,1)} async-done(((bf16[4,3,256,256]{3,2,1,0:T(8,128)(2,1)}), bf16[4,3,256,256]{3,2,1,0:T(8,128)(2,1)}, u32[]{:S(2)}, u32[]{:S(2)}) %all-to-all-start.1) | async-done | bytes 1572896 | tf_op jit(solution)/shard_map/all_to_all | solution.py:680
  266.2 7.5 %conv_backward.2 = (bf16[4,3,256,256]{3,2,1,0:T(8,128)(2,1)}, f32[128,256]{1,0:T(8,128)}, f32[9,256]{1,0:T(8,128)}) custom-call(bf16[1024,256]{1,0:T(8,128)(2,1)} %bitcast.173, bf16[4,3,256,256]{3,2,1,0:T(8,128)(2,1)} %all-to-all-done.1.proj_ref, f32[9,256]{1,0:T(8,128)} %reshape.182.taps_ref, f32[128,256]{1,0:T(8,128)} %bitcast_multiply_fusion.kern_ref, ...), custom_call_target="tpu_custom_call" | custom-call | tf_op jit(solution)/shard_map/conv_backward/pallas_call | solution.py:350
  279.7 18.6 %all-to-all-done.2.gproj_ref = bf16[4,3,256,256]{3,2,1,0:T(8,128)(2,1)S(1)} async-done(((bf16[4,3,256,256]{3,2,1,0:T(8,128)(2,1)}), bf16[4,3,256,256]{3,2,1,0:T(8,128)(2,1)S(1)}, u32[]{:S(2)}, u32[]{:S(2)}) %all-to-all-start.2) | async-done | bytes 1572896 | tf_op jit(solution)/shard_map/all_to_all | solution.py:680
  299.5 15.9 %input_gradient.1 = (bf16[256,1024]{1,0:T(8,128)(2,1)}, bf16[128,1024]{1,0:T(8,128)(2,1)}, bf16[128,1024]{1,0:T(8,128)(2,1)}, bf16[128,1024]{1,0:T(8,128)(2,1)},...) custom-call(s32[5]{0:T(128)} %pad_add_fusion.ctx_ref, ...), custom_call_target="tpu_custom_call" | custom-call | tf_op jit(solution)/shard_map/input_gradient/pallas_call | solution.py:522
  320.7 40.9 %collective-permute-done.32 = bf16[128,1024]{1,0:T(8,128)(2,1)S(1)} collective-permute-done((bf16[128,1024]{1,0:T(8,128)(2,1)}, bf16[128,1024]{1,0:T(8,128)(2,1)S(1)}, u32[]{:S(2)}, u32[]{:S(2)}) %collective-permute-start.32) | collective-permute-done | bytes 262176 | tf_op jit(solution)/shard_map/ppermute | solution.py:39
  361.6 12.2 %collective-permute-done.33 = bf16[128,1024]{1,0:T(8,128)(2,1)S(1)} collective-permute-done((bf16[128,1024]{1,0:T(8,128)(2,1)}, bf16[128,1024]{1,0:T(8,128)(2,1)S(1)}, u32[]{:S(2)}, u32[]{:S(2)}) %collective-permute-start.33) | collective-permute-done | bytes 262176 | tf_op jit(solution)/shard_map/ppermute | solution.py:39
  373.9 9.2 %collective-permute-done.35 = bf16[256,1024]{1,0:T(8,128)(2,1)S(1)} collective-permute-done((bf16[256,1024]{1,0:T(8,128)(2,1)}, bf16[256,1024]{1,0:T(8,128)(2,1)S(1)}, u32[]{:S(2)}, u32[]{:S(2)}) %collective-permute-start.35) | collective-permute-done | bytes 524320 | tf_op jit(solution)/shard_map/ppermute | solution.py:39
  398.6 13.4 %collective-permute-done.39 = bf16[128,1024]{1,0:T(8,128)(2,1)S(1)} collective-permute-done((bf16[128,1024]{1,0:T(8,128)(2,1)S(1)}, bf16[128,1024]{1,0:T(8,128)(2,1)S(1)}, u32[]{:S(2)}, u32[]{:S(2)}) %collective-permute-start.39) | collective-permute-done | bytes 262176 | tf_op jit(solution)/shard_map/ppermute | solution.py:39
  412.2 7.8 %collective-permute-start.41 = (bf16[128,1024]{1,0:T(8,128)(2,1)S(1)}, bf16[128,1024]{1,0:T(8,128)(2,1)S(1)}, u32[]{:S(2)}, u32[]{:S(2)}) collective-permute-start(bf16[128,1024]{1,0:T(8,128)(2,1)S(1)} %add_convert_fusion), channel_id=1, source_target_pairs={{0,4},{4,8},{8,12},{12,0},{1,5},{5,9},{9,13},{13,1},{2,6},{6,10},{... | collective-permute-start | bytes 786440 | tf_op jit(solution)/shard_map/ppermute | solution.py:39
  461.3 7.9 %all-to-all-start.3 = ((bf16[4,256,256]{2,1,0:T(8,128)(2,1)}), bf16[4,256,256]{2,1,0:T(8,128)(2,1)}, u32[]{:S(2)}, u32[]{:S(2)}) async-start(bf16[4,256,256]{2,1,0:T(8,128)(2,1)} %bitcast.174), calls=%async_computation.3 | async-start | bytes 1048576 | tf_op jit(solution)/shard_map/all_to_all | solution.py:680
  482.6 8.4 %conv_backward.3 = (bf16[3,512,256]{2,1,0:T(8,128)(2,1)}, f32[128,256]{1,0:T(8,128)}, f32[9,256]{1,0:T(8,128)}) custom-call(s32[1,1024]{1,0:T(1,128)} %maximum_convert_fusion.1.tokens_ref, f32[512,1]{1,0:T(8,128)} %copy.41.scale_ref, bf16[1024,256]{1,0:T(8,128)(2,1)} %bitcast.74.gg_ref, bf16[1,3,1024,256]{3,2,1,0:T(8,128)(2,1)} %get-tuple-element.190.proj_ref, ...), custom_call_target="tpu_custom_call" | custom-call | tf_op jit(solution)/shard_map/conv_backward/pallas_call | solution.py:350
  497.5 29.9 %collective-permute-done.55 = f32[138,256]{1,0:T(8,128)S(1)} collective-permute-done((f32[138,256]{1,0:T(8,128)}, f32[138,256]{1,0:T(8,128)S(1)}, u32[]{:S(2)}, u32[]{:S(2)}) %collective-permute-start.55) | collective-permute-done | bytes 141344 | tf_op jit(solution)/shard_map/ppermute | solution.py:39
  539.2 7.6 %grad_project_out.1 = f32[1024,1024]{1,0:T(8,128)} custom-call(s32[5]{0:T(128)} %stack.160.where_ref, bf16[1024,1024]{1,0:T(8,128)(2,1)} %bitcast.78.right_ref, bf16[1024,256]{1,0:T(8,128)(2,1)} %get-tuple-element.194.refs_0_, bf16[1024,256]{1,0:T(8,128)(2,1)} %copy-done.18, bf16[1024,256]{1,0:T(8,128)(2,1)} %collective-permute-done.30.refs_2_, ...), custom_call_target="tpu_custom_call" | custom-call | tf_op jit(solution)/shard_map/grad_project_out/pallas_call | solution.py:598
  546.9 9.7 %conditional.1 = (f32[3,1024,1024]{2,1,0:T(8,128)}) conditional(s32[]{:T(128)} %convert_element_type.120, (s32[]{:T(128)}, bf16[1024,1024]{0,1:T(8,128)(2,1)}, bf16[4,1024,256]{2,1,0:T(8,128)(2,1)S(1)}, bf16[4,1024,256]{2,1,0:T(8,128)(2,1)}, bf16[4,1024,256]{2,1,0:T(8,128)(2,1)}, /*index=5*/bf16[4,1024,256]{2,1,0:T(8,128)(2,1)}) %tuple.36, ...), branch_computations={%region_1.2_spmd, %region_2.3_spmd} | conditional | bytes 4194312 | solution.py:822
  548.2 8.4 %grad_project_in.3 = f32[3,1024,1024]{2,1,0:T(8,128)} custom-call(s32[1]{0:T(128)} %bitcast.1.ctx_ref, bf16[1024,512]{1,0:T(8,128)(2,1)} %bitcast.172, bf16[3,512,256]{2,1,0:T(8,128)(2,1)} %get-tuple-element.35.refs_0_, bf16[3,512,256]{2,1,0:T(8,128)(2,1)} %get-tuple-element.36.refs_1_, bf16[3,512,256]{2,1,0:T(8,128)(2,1)} %get-tuple-element.37.refs_2_, ...), custom_call_target="tpu_custom_call" | custom-call | tf_op jit(solution)/shard_map/cond/branch_1_fun/grad_project_in/pallas_call | solution.py:565
  (299 shorter events, 248.8 us)
Async XLA Ops:
  7.2 119.9 %all-gather.3.cloned.1.call-start = ((), (), s32[]{:S(2)}) async-start(), calls=%async_computation.5 | async-start | bytes 10485760 | tf_op jit(solution)/shard_map/all_gather | solution.py:720
  7.9 104.2 %collective-permute-start.10 = (bf16[3,1024,1024]{2,1,0:T(8,128)(2,1)}, bf16[3,1024,1024]{2,1,0:T(8,128)(2,1)}, u32[]{:S(2)}, u32[]{:S(2)}) collective-permute-start(bf16[3,1024,1024]{2,1,0:T(8,128)(2,1)} %bitcast.159), channel_id=1, source_target_pairs={{16,17},{17,16},{18,19},{19,18},{20,21},{21,20},{22,23},{23,22},{2... | collective-permute-start | bytes 18874376 | tf_op jit(solution)/shard_map/ppermute | solution.py:39
  15.3 167.5 %collective-permute-start.27 = (bf16[3,1024,1024]{2,1,0:T(8,128)(2,1)}, bf16[3,1024,1024]{2,1,0:T(8,128)(2,1)}, u32[]{:S(2)}, u32[]{:S(2)}) collective-permute-start(bf16[3,1024,1024]{2,1,0:T(8,128)(2,1)} %bitcast.160), channel_id=1, source_target_pairs={{16,18},{17,19},{18,16},{19,17},{20,22},{21,23},{22,20},{23,21},{2... | collective-permute-start | bytes 18874376 | tf_op jit(solution)/shard_map/ppermute | solution.py:39
  31.8 46.1 %collective-permute-start.5 = (bf16[2,3,512,256]{3,2,1,0:T(8,128)(2,1)}, bf16[2,3,512,256]{3,2,1,0:T(8,128)(2,1)}, u32[]{:S(2)}, u32[]{:S(2)}) collective-permute-start(bf16[2,3,512,256]{3,2,1,0:T(8,128)(2,1)} %table_projection.3), channel_id=1, source_target_pairs={{0,1},{1,0},{2,3},{3,2},{4,5},{5,4},{6,7},{7,6},{8,9},{9,8},{10,11... | collective-permute-start | bytes 4718600 | tf_op jit(solution)/shard_map/ppermute | solution.py:39
  44.5 30.3 %collective-permute-start.7 = (bf16[256,1024]{1,0:T(8,128)(2,1)S(1)}, bf16[256,1024]{1,0:T(8,128)(2,1)S(1)}, u32[]{:S(2)}, u32[]{:S(2)}) collective-permute-start(bf16[256,1024]{1,0:T(8,128)(2,1)S(1)} %copy-done.13), channel_id=1, source_target_pairs={{16,20},{20,24},{24,28},{28,16},{17,21},{21,25},{25,29},{29,17},{1... | collective-permute-start | bytes 1572872 | tf_op jit(solution)/shard_map/ppermute | solution.py:39
  47.9 27.7 %collective-permute-start.3 = (f32[768]{0:T(1024)S(1)}, f32[768]{0:T(1024)S(1)}, u32[]{:S(2)}, u32[]{:S(2)}) collective-permute-start(f32[768]{0:T(1024)S(1)} %pad_maximum_fusion.16), channel_id=1, source_target_pairs={{0,2},{1,3},{2,0},{3,1},{4,6},{5,7},{6,4},{7,5},{8,10},{9,11},{10,... | collective-permute-start | bytes 9224 | tf_op jit(solution)/shard_map/ppermute | solution.py:39
  135.1 24.4 %collective-permute-start.17 = (bf16[256,1024]{1,0:T(8,128)(2,1)}, bf16[256,1024]{1,0:T(8,128)(2,1)S(1)}, u32[]{:S(2)}, u32[]{:S(2)}) collective-permute-start(bf16[256,1024]{1,0:T(8,128)(2,1)} %get-tuple-element.135), channel_id=1, source_target_pairs={{0,16},{4,20},{8,24},{12,28},{1,17},{5,21},{9,25},{13,29},{2,18},{... | collective-permute-start | bytes 1572872 | tf_op jit(solution)/shard_map/ppermute | solution.py:39
  184.3 35.7 %collective-permute-start.28 = (bf16[3,1024,1024]{2,1,0:T(8,128)(2,1)}, bf16[3,1024,1024]{2,1,0:T(8,128)(2,1)}, u32[]{:S(2)}, u32[]{:S(2)}) collective-permute-start(bf16[3,1024,1024]{2,1,0:T(8,128)(2,1)} %collective-permute-done.27.refs_2_), channel_id=1, source_target_pairs={{16,17},{17,16},{18,19},{19,18},{20,21},{21,20},{22,23},{23,22},{2... | collective-permute-start | bytes 18874376 | tf_op jit(solution)/shard_map/ppermute | solution.py:39
  187.6 48.4 %collective-permute-start.30 = (bf16[1024,256]{1,0:T(8,128)(2,1)}, bf16[1024,256]{1,0:T(8,128)(2,1)}, u32[]{:S(2)}, u32[]{:S(2)}) collective-permute-start(bf16[1024,256]{1,0:T(8,128)(2,1)} %get-tuple-element.194.refs_0_), channel_id=1, source_target_pairs={{0,2},{1,3},{2,0},{3,1},{4,6},{5,7},{6,4},{7,5},{8,10},{9,11},{10,... | collective-permute-start | bytes 1572872 | tf_op jit(solution)/shard_map/ppermute | solution.py:39
  227.2 25.9 %all-to-all-start.1 = ((bf16[4,3,256,256]{3,2,1,0:T(8,128)(2,1)}), bf16[4,3,256,256]{3,2,1,0:T(8,128)(2,1)}, u32[]{:S(2)}, u32[]{:S(2)}) async-start(bf16[4,3,256,256]{3,2,1,0:T(8,128)(2,1)} %input_projection_rest.1), calls=%async_computation.1 | async-start | bytes 3145728 | tf_op jit(solution)/shard_map/all_to_all | solution.py:680
  234.0 39.7 %collective-permute-start.29 = (bf16[1024,256]{1,0:T(8,128)(2,1)}, bf16[1024,256]{1,0:T(8,128)(2,1)S(1)}, u32[]{:S(2)}, u32[]{:S(2)}) collective-permute-start(bf16[1024,256]{1,0:T(8,128)(2,1)} %get-tuple-element.194.refs_0_), channel_id=1, source_target_pairs={{0,1},{1,0},{2,3},{3,2},{4,5},{5,4},{6,7},{7,6},{8,9},{9,8},{10,11... | collective-permute-start | bytes 1572872 | tf_op jit(solution)/shard_map/ppermute | solution.py:39
  236.0 37.7 %collective-permute-start.31 = (bf16[1024,256]{1,0:T(8,128)(2,1)}, bf16[1024,256]{1,0:T(8,128)(2,1)S(1)}, u32[]{:S(2)}, u32[]{:S(2)}) collective-permute-start(bf16[1024,256]{1,0:T(8,128)(2,1)} %collective-permute-done.30.refs_2_), channel_id=1, source_target_pairs={{0,1},{1,0},{2,3},{3,2},{4,5},{5,4},{6,7},{7,6},{8,9},{9,8},{10,11... | collective-permute-start | bytes 1572872 | tf_op jit(solution)/shard_map/ppermute | solution.py:39
  274.7 23.6 %all-to-all-start.2 = ((bf16[4,3,256,256]{3,2,1,0:T(8,128)(2,1)}), bf16[4,3,256,256]{3,2,1,0:T(8,128)(2,1)S(1)}, u32[]{:S(2)}, u32[]{:S(2)}) async-start(bf16[4,3,256,256]{3,2,1,0:T(8,128)(2,1)} %get-tuple-element.177), calls=%async_computation.2 | async-start | bytes 3145728 | tf_op jit(solution)/shard_map/all_to_all | solution.py:680
  315.4 67.7 %collective-permute-start.35 = (bf16[256,1024]{1,0:T(8,128)(2,1)}, bf16[256,1024]{1,0:T(8,128)(2,1)S(1)}, u32[]{:S(2)}, u32[]{:S(2)}) collective-permute-start(bf16[256,1024]{1,0:T(8,128)(2,1)} %get-tuple-element.165), channel_id=1, source_target_pairs={{16,0},{20,4},{24,8},{28,12},{17,1},{21,5},{25,9},{29,13},{18,2},{... | collective-permute-start | bytes 1572872 | tf_op jit(solution)/shard_map/ppermute | solution.py:39
  316.8 44.8 %collective-permute-start.32 = (bf16[128,1024]{1,0:T(8,128)(2,1)}, bf16[128,1024]{1,0:T(8,128)(2,1)S(1)}, u32[]{:S(2)}, u32[]{:S(2)}) collective-permute-start(bf16[128,1024]{1,0:T(8,128)(2,1)} %get-tuple-element.156), channel_id=1, source_target_pairs={{16,4},{20,8},{24,12},{28,0},{17,5},{21,9},{25,13},{29,1},{18,6},{... | collective-permute-start | bytes 786440 | tf_op jit(solution)/shard_map/ppermute | solution.py:39
  318.1 55.7 %collective-permute-start.33 = (bf16[128,1024]{1,0:T(8,128)(2,1)}, bf16[128,1024]{1,0:T(8,128)(2,1)S(1)}, u32[]{:S(2)}, u32[]{:S(2)}) collective-permute-start(bf16[128,1024]{1,0:T(8,128)(2,1)} %get-tuple-element.157), channel_id=1, source_target_pairs={{16,8},{20,12},{24,0},{28,4},{17,9},{21,13},{25,1},{29,5},{18,10},... | collective-permute-start | bytes 786440 | tf_op jit(solution)/shard_map/ppermute | solution.py:39
  319.4 54.4 %collective-permute-start.34 = (bf16[128,1024]{1,0:T(8,128)(2,1)}, bf16[128,1024]{1,0:T(8,128)(2,1)S(1)}, u32[]{:S(2)}, u32[]{:S(2)}) collective-permute-start(bf16[128,1024]{1,0:T(8,128)(2,1)} %get-tuple-element.158), channel_id=1, source_target_pairs={{16,12},{20,0},{24,4},{28,8},{17,13},{21,1},{25,5},{29,9},{18,14},... | collective-permute-start | bytes 786440 | tf_op jit(solution)/shard_map/ppermute | solution.py:39
  383.7 41.5 %collective-permute-start.42 = (bf16[4,1024,256]{2,1,0:T(8,128)(2,1)S(1)}, bf16[4,1024,256]{2,1,0:T(8,128)(2,1)}, u32[]{:S(2)}, u32[]{:S(2)}) collective-permute-start(bf16[4,1024,256]{2,1,0:T(8,128)(2,1)S(1)} %pad_maximum_fusion.3.refs_4_), channel_id=1, source_target_pairs={{16,18},{17,19},{18,16},{19,17},{20,22},{21,23},{22,20},{23,21},{2... | collective-permute-start | bytes 6291464 | tf_op jit(solution)/shard_map/ppermute | solution.py:39
  425.1 29.4 %collective-permute-start.49 = (bf16[4,1024,256]{2,1,0:T(8,128)(2,1)S(1)}, bf16[4,1024,256]{2,1,0:T(8,128)(2,1)}, u32[]{:S(2)}, u32[]{:S(2)}) collective-permute-start(bf16[4,1024,256]{2,1,0:T(8,128)(2,1)S(1)} %pad_maximum_fusion.3.refs_4_), channel_id=1, source_target_pairs={{16,17},{17,16},{18,19},{19,18},{20,21},{21,20},{22,23},{23,22},{2... | collective-permute-start | bytes 6291464 | tf_op jit(solution)/shard_map/ppermute | solution.py:39
  427.1 27.5 %collective-permute-start.50 = (bf16[4,1024,256]{2,1,0:T(8,128)(2,1)}, bf16[4,1024,256]{2,1,0:T(8,128)(2,1)}, u32[]{:S(2)}, u32[]{:S(2)}) collective-permute-start(bf16[4,1024,256]{2,1,0:T(8,128)(2,1)} %collective-permute-done.42.refs_6_), channel_id=1, source_target_pairs={{16,17},{17,16},{18,19},{19,18},{20,21},{21,20},{22,23},{23,22},{2... | collective-permute-start | bytes 6291464 | tf_op jit(solution)/shard_map/ppermute | solution.py:39
  477.3 61.9 %all-to-all-start.4 = ((bf16[4,256,1024]{2,1,0:T(8,128)(2,1)}), bf16[4,256,1024]{2,1,0:T(8,128)(2,1)}, u32[]{:S(2)}, u32[]{:S(2)}) async-start(bf16[4,256,1024]{2,1,0:T(8,128)(2,1)} %pad_maximum_fusion.7), calls=%async_computation.4 | async-start | bytes 4194304 | tf_op jit(solution)/shard_map/all_to_all | solution.py:680
  490.9 40.0 %collective-permute-start.52 = (bf16[3,512,256]{2,1,0:T(8,128)(2,1)}, bf16[3,512,256]{2,1,0:T(8,128)(2,1)}, u32[]{:S(2)}, u32[]{:S(2)}) collective-permute-start(bf16[3,512,256]{2,1,0:T(8,128)(2,1)} %get-tuple-element.193), channel_id=1, source_target_pairs={{0,2},{1,3},{2,0},{3,1},{4,6},{5,7},{6,4},{7,5},{8,10},{9,11},{10,... | collective-permute-start | bytes 2359304 | tf_op jit(solution)/shard_map/ppermute | solution.py:39
  496.8 30.6 %collective-permute-start.55 = (f32[138,256]{1,0:T(8,128)}, f32[138,256]{1,0:T(8,128)S(1)}, u32[]{:S(2)}, u32[]{:S(2)}) collective-permute-start(f32[138,256]{1,0:T(8,128)} %pad_maximum_fusion.13), channel_id=1, source_target_pairs={{0,2},{1,3},{2,0},{3,1},{16,18},{17,19},{18,16},{19,17},{4,6},{5,7... | collective-permute-start | bytes 423944 | tf_op jit(solution)/shard_map/ppermute | solution.py:39
  496.9 36.6 %collective-permute-start.54 = (f32[138,256]{1,0:T(8,128)}, f32[138,256]{1,0:T(8,128)}, u32[]{:S(2)}, u32[]{:S(2)}) collective-permute-start(f32[138,256]{1,0:T(8,128)} %pad_maximum_fusion.13), channel_id=1, source_target_pairs={{0,1},{1,0},{2,3},{3,2},{16,17},{17,16},{18,19},{19,18},{4,5},{5,4... | collective-permute-start | bytes 423944 | tf_op jit(solution)/shard_map/ppermute | solution.py:39
  (89 other events, 1196.0 us)
Sparse Core Ops, SparseCore 0:
  9.6 60.7 all-gather.2

commit v5 on v4

--- a/solution.py
+++ b/solution.py
@@ -770,7 +770,6 @@
     middle_stack, (gated_0,), late = cross_gather(
         shares, first_input, 0, [gated_0], [in_far[r] for r in far]
     )
-    gated_all_0 = ctx_gather(gated_0, (0,))
 
     in_far.update(zip(far, late))
     in_pieces = []
@@ -786,7 +785,10 @@
     soon = {r: in_pieces[r] for r in range(n_ctx) if r == 1 or r % 2 == 0}
     rest = {r: in_pieces[r] for r in range(n_ctx) if r not in soon}
     normed, part, scale = input_projection(middle_all, soon, ctx)
-    proj_1 = ctx_swap(input_projection_rest(middle_all, rest, part, scale, ctx))
+    proj_rows = input_projection_rest(middle_all, rest, part, scale, ctx)
+    proj_rows, gated_0 = together(proj_rows, gated_0)
+    gated_all_0 = ctx_gather(gated_0, (0,))
+    proj_1 = ctx_swap(proj_rows)
     gated_1, *saved_1 = conv_forward(proj_1, taps, kern, matrices)
 
     gproj_1, gkern_1, gtaps_1 = conv_backward(

time: 572 us -> 565 us (0.988)
  the two profiles are of different devices: /device:TPU:1 before, /device:TPU:5 now
where the time goes in v5:
time: 565 us; the launch traced here: 556 us
  waiting for transfers between devices  216 us (38%)
  starting transfers between devices  154 us (27%)
  Pallas kernels  100 us (18%)
  other arithmetic  34.8 us (6%)
  local copies, waits for them, and re-layouts  26.1 us (5%)
  between operations  15.8 us (3%)
  matrix products  8.58 us (2%)
    ppermute x57, waiting for transfers between devices, send(): return lax.ppermute(value, axes, pairs)  167 us
    ppermute x57, starting transfers between devices, send(): return lax.ppermute(value, axes, pairs)  131 us
    all_to_all x5, waiting for transfers between devices, ctx_swap(): return lax.all_to_all(value, 'ctx', split_axis=0, concat_axis=0, tiled=True)  36.1 us
    all_to_all x5, starting transfers between devices, ctx_swap(): return lax.all_to_all(value, 'ctx', split_axis=0, concat_axis=0, tiled=True)  22.9 us
    pallas_call x1, Pallas kernels, input_gradient(): pl.pallas_call(kernel, grid_spec=pltpu.PrefetchScalarGridSpec(num_scalar_...  15.9 us
    pallas_call x2, Pallas kernels, conv_backward(): pl.pallas_call(backward_kernel if tokens is None else collect_kernel, out...  15.8 us
    pallas_call x1, Pallas kernels, input_projection(): pl.pallas_call(kernel, grid_spec=pltpu.PrefetchScalarGridSpec(num_scalar_...  13.2 us
    all_gather x1, waiting for transfers between devices, local(): out_full = lax.all_gather(weights_out, 'ctx', axis=1, tiled=True)  12.4 us
  transfers between devices with their start and end apart: 63, of which 27 were waited for; matrix products, arithmetic and copies ran while one was open for 9% of the time, Pallas kernels for 12%

profile of v5, /device:TPU:5, one launch (start us, length us, event | category | flops | bytes accessed | tf_op | source)
XLA Modules:
  0.0 555.6 jit_solution(8370168081130380337)
XLA Ops:
  25.8 25.1 %collective-permute-start.7 = (bf16[256,1024]{1,0:T(8,128)(2,1)S(1)}, bf16[256,1024]{1,0:T(8,128)(2,1)S(1)}, u32[]{:S(2)}, u32[]{:S(2)}) collective-permute-start(bf16[256,1024]{1,0:T(8,128)(2,1)S(1)} %copy-done.13), channel_id=1, source_target_pairs={{16,20},{20,24},{24,28},{28,16},{17,21},{21,25},{25,29},{29,17},{1... | collective-permute-start | bytes 1572872 | tf_op jit(solution)/shard_map/ppermute | solution.py:39
  75.4 9.6 %collective-permute-done.9 = bf16[256,1024]{1,0:T(8,128)(2,1)S(1)} collective-permute-done((bf16[256,1024]{1,0:T(8,128)(2,1)S(1)}, bf16[256,1024]{1,0:T(8,128)(2,1)S(1)}, u32[]{:S(2)}, u32[]{:S(2)}) %collective-permute-start.9) | collective-permute-done | bytes 524320 | tf_op jit(solution)/shard_map/ppermute | solution.py:39
  101.0 12.4 %all-gather.3.cloned.1.call-done = bf16[1,1024,4096]{2,1,0:T(8,128)(2,1)} async-done(((bf16[1,1024,1024]{2,1,0:T(8,128)(2,1)}), bf16[1,1024,4096]{2,1,0:T(8,128)(2,1)}) %all-gather.3.cloned.1.call-update) | async-done | bytes 8388624 | tf_op jit(solution)/shard_map/all_gather | solution.py:720
  113.4 8.0 %output_projection.1 = (bf16[256,1024]{1,0:T(8,128)(2,1)}, bf16[128,1024]{1,0:T(8,128)(2,1)}, bf16[128,1024]{1,0:T(8,128)(2,1)}, bf16[128,1024]{1,0:T(8,128)(2,1...) custom-call(s32[4]{0:T(128)} %and_select_fusion.where_ref, ...), custom_call_target="tpu_custom_call" | custom-call | tf_op jit(solution)/shard_map/output_projection/pallas_call | solution.py:648
  127.3 9.3 %collective-permute-done.14 = bf16[128,1024]{1,0:T(8,128)(2,1)S(1)} collective-permute-done((bf16[128,1024]{1,0:T(8,128)(2,1)}, bf16[128,1024]{1,0:T(8,128)(2,1)S(1)}, u32[]{:S(2)}, u32[]{:S(2)}) %collective-permute-start.14) | collective-permute-done | bytes 262176 | tf_op jit(solution)/shard_map/ppermute | solution.py:39
  136.5 11.8 %collective-permute-done.15 = bf16[128,1024]{1,0:T(8,128)(2,1)S(1)} collective-permute-done((bf16[128,1024]{1,0:T(8,128)(2,1)}, bf16[128,1024]{1,0:T(8,128)(2,1)S(1)}, u32[]{:S(2)}, u32[]{:S(2)}) %collective-permute-start.15) | collective-permute-done | bytes 262176 | tf_op jit(solution)/shard_map/ppermute | solution.py:39
  148.4 11.3 %collective-permute-done.17 = bf16[256,1024]{1,0:T(8,128)(2,1)S(1)} collective-permute-done((bf16[256,1024]{1,0:T(8,128)(2,1)}, bf16[256,1024]{1,0:T(8,128)(2,1)S(1)}, u32[]{:S(2)}, u32[]{:S(2)}) %collective-permute-start.17) | collective-permute-done | bytes 524320 | tf_op jit(solution)/shard_map/ppermute | solution.py:39
  174.0 11.9 %collective-permute-done.21 = bf16[128,1024]{1,0:T(8,128)(2,1)S(1)} collective-permute-done((bf16[128,1024]{1,0:T(8,128)(2,1)S(1)}, bf16[128,1024]{1,0:T(8,128)(2,1)S(1)}, u32[]{:S(2)}, u32[]{:S(2)}) %collective-permute-start.21) | collective-permute-done | bytes 262176 | tf_op jit(solution)/shard_map/ppermute | solution.py:39
  186.8 7.8 %collective-permute-start.23 = (bf16[128,1024]{1,0:T(8,128)(2,1)S(1)}, bf16[128,1024]{1,0:T(8,128)(2,1)S(1)}, u32[]{:S(2)}, u32[]{:S(2)}) collective-permute-start(bf16[128,1024]{1,0:T(8,128)(2,1)S(1)} %fusion.28), channel_id=1, source_target_pairs={{16,20},{20,24},{24,28},{28,16},{17,21},{21,25},{25,29},{29,17},{1... | collective-permute-start | bytes 786440 | tf_op jit(solution)/shard_map/ppermute | solution.py:39
  231.1 13.2 %input_projection.1 = (bf16[4,256,1024]{2,1,0:T(8,128)(2,1)}, f32[3,256,1024]{2,1,0:T(8,128)}, f32[256,1]{1,0:T(8,128)}) custom-call(s32[1]{0:T(128)} %bitcast.3.ctx_ref, bf16[256,4096]{1,0:T(8,128)(2,1)} %pad_maximum_fusion.2.rows_ref, bf16[3,1024,1024]{2,1,0:T(8,128)(2,1)} %bitcast.163, bf16[3,1024,1024]{2,1,0:T(8,128)(2,1)} %collective-permute-done.10.refs_1_, ...), custom_call_target="tpu_custom_call" | custom-call | tf_op jit(solution)/shard_map/input_projection/pallas_call | solution.py:419
  244.3 7.2 %input_projection_rest.1 = bf16[4,3,256,256]{3,2,1,0:T(8,128)(2,1)} custom-call(s32[1]{0:T(128)} %bitcast.3.ctx_ref, bf16[256,4096]{1,0:T(8,128)(2,1)} %pad_maximum_fusion.2.rows_ref, f32[3,256,1024]{2,1,0:T(8,128)} %get-tuple-element.151.part_ref, f32[256,1]{1,0:T(8,128)} %get-tuple-element.152.scale_ref, ...), custom_call_target="tpu_custom_call" | custom-call | tf_op jit(solution)/shard_map/input_projection_rest/pallas_call | solution.py:460
  265.5 11.1 %all-to-all-done.1.proj_ref = bf16[4,3,256,256]{3,2,1,0:T(8,128)(2,1)} async-done(((bf16[4,3,256,256]{3,2,1,0:T(8,128)(2,1)}), bf16[4,3,256,256]{3,2,1,0:T(8,128)(2,1)}, u32[]{:S(2)}, u32[]{:S(2)}) %all-to-all-start.1) | async-done | bytes 1572896 | tf_op jit(solution)/shard_map/all_to_all | solution.py:680
  289.8 7.5 %conv_backward.2 = (bf16[4,3,256,256]{3,2,1,0:T(8,128)(2,1)}, f32[128,256]{1,0:T(8,128)}, f32[9,256]{1,0:T(8,128)}) custom-call(bf16[1024,256]{1,0:T(8,128)(2,1)} %bitcast.173, bf16[4,3,256,256]{3,2,1,0:T(8,128)(2,1)} %all-to-all-done.1.proj_ref, f32[9,256]{1,0:T(8,128)} %reshape.182.taps_ref, f32[128,256]{1,0:T(8,128)} %bitcast_multiply_fusion.kern_ref, ...), custom_call_target="tpu_custom_call" | custom-call | tf_op jit(solution)/shard_map/conv_backward/pallas_call | solution.py:350
  303.4 18.6 %all-to-all-done.2.gproj_ref = bf16[4,3,256,256]{3,2,1,0:T(8,128)(2,1)S(1)} async-done(((bf16[4,3,256,256]{3,2,1,0:T(8,128)(2,1)}), bf16[4,3,256,256]{3,2,1,0:T(8,128)(2,1)S(1)}, u32[]{:S(2)}, u32[]{:S(2)}) %all-to-all-start.2) | async-done | bytes 1572896 | tf_op jit(solution)/shard_map/all_to_all | solution.py:680
  323.1 15.9 %input_gradient.1 = (bf16[256,1024]{1,0:T(8,128)(2,1)}, bf16[128,1024]{1,0:T(8,128)(2,1)}, bf16[128,1024]{1,0:T(8,128)(2,1)}, bf16[128,1024]{1,0:T(8,128)(2,1)},...) custom-call(s32[5]{0:T(128)} %pad_add_fusion.ctx_ref, ...), custom_call_target="tpu_custom_call" | custom-call | tf_op jit(solution)/shard_map/input_gradient/pallas_call | solution.py:522
  358.8 9.5 %collective-permute-done.35 = bf16[256,1024]{1,0:T(8,128)(2,1)S(1)} collective-permute-done((bf16[256,1024]{1,0:T(8,128)(2,1)}, bf16[256,1024]{1,0:T(8,128)(2,1)S(1)}, u32[]{:S(2)}, u32[]{:S(2)}) %collective-permute-start.35) | collective-permute-done | bytes 524320 | tf_op jit(solution)/shard_map/ppermute | solution.py:39
  393.3 23.5 %collective-permute-done.42.refs_6_ = bf16[4,1024,256]{2,1,0:T(8,128)(2,1)} collective-permute-done((bf16[4,1024,256]{2,1,0:T(8,128)(2,1)S(1)}, bf16[4,1024,256]{2,1,0:T(8,128)(2,1)}, u32[]{:S(2)}, u32[]{:S(2)}) %collective-permute-start.42) | collective-permute-done | bytes 2097184 | tf_op jit(solution)/shard_map/ppermute | solution.py:39
  440.5 7.5 %collective-permute-done.47 = bf16[256,1024]{1,0:T(8,128)(2,1)S(1)} collective-permute-done((bf16[256,1024]{1,0:T(8,128)(2,1)S(1)}, bf16[256,1024]{1,0:T(8,128)(2,1)S(1)}, u32[]{:S(2)}, u32[]{:S(2)}) %collective-permute-start.47) | collective-permute-done | bytes 524320 | tf_op jit(solution)/shard_map/ppermute | solution.py:39
  447.9 11.3 %collective-permute-done.48 = bf16[256,1024]{1,0:T(8,128)(2,1)S(1)} collective-permute-done((bf16[256,1024]{1,0:T(8,128)(2,1)S(1)}, bf16[256,1024]{1,0:T(8,128)(2,1)S(1)}, u32[]{:S(2)}, u32[]{:S(2)}) %collective-permute-start.48) | collective-permute-done | bytes 524320 | tf_op jit(solution)/shard_map/ppermute | solution.py:39
  485.8 8.4 %conv_backward.3 = (bf16[3,512,256]{2,1,0:T(8,128)(2,1)}, f32[128,256]{1,0:T(8,128)}, f32[9,256]{1,0:T(8,128)}) custom-call(s32[1,1024]{1,0:T(1,128)} %maximum_convert_fusion.1.tokens_ref, f32[512,1]{1,0:T(8,128)} %copy.41.scale_ref, bf16[1024,256]{1,0:T(8,128)(2,1)} %bitcast.74.gg_ref, bf16[1,3,1024,256]{3,2,1,0:T(8,128)(2,1)} %get-tuple-element.194.proj_ref, ...), custom_call_target="tpu_custom_call" | custom-call | tf_op jit(solution)/shard_map/conv_backward/pallas_call | solution.py:350
  499.5 14.3 %collective-permute-done.55 = f32[138,256]{1,0:T(8,128)S(1)} collective-permute-done((f32[138,256]{1,0:T(8,128)}, f32[138,256]{1,0:T(8,128)S(1)}, u32[]{:S(2)}, u32[]{:S(2)}) %collective-permute-start.55) | collective-permute-done | bytes 141344 | tf_op jit(solution)/shard_map/ppermute | solution.py:39
  524.4 7.6 %grad_project_out.1 = f32[1024,1024]{1,0:T(8,128)} custom-call(s32[5]{0:T(128)} %stack.160.where_ref, bf16[1024,1024]{1,0:T(8,128)(2,1)} %bitcast.78.right_ref, bf16[1024,256]{1,0:T(8,128)(2,1)} %get-tuple-element.198.refs_0_, bf16[1024,256]{1,0:T(8,128)(2,1)} %copy-done.18, bf16[1024,256]{1,0:T(8,128)(2,1)} %collective-permute-done.30.refs_2_, ...), custom_call_target="tpu_custom_call" | custom-call | tf_op jit(solution)/shard_map/grad_project_out/pallas_call | solution.py:598
  532.1 15.5 %conditional.1 = (f32[3,1024,1024]{2,1,0:T(8,128)}) conditional(s32[]{:T(128)} %convert_element_type.120, (s32[]{:T(128)}, bf16[1024,1024]{0,1:T(8,128)(2,1)}, bf16[4,1024,256]{2,1,0:T(8,128)(2,1)S(1)}, bf16[4,1024,256]{2,1,0:T(8,128)(2,1)}, bf16[4,1024,256]{2,1,0:T(8,128)(2,1)}, /*index=5*/bf16[4,1024,256]{2,1,0:T(8,128)(2,1)}) %tuple.38, ...), branch_computations={%region_1.2_spmd, %region_2.3_spmd} | conditional | bytes 4194312 | solution.py:824
  536.0 11.5 %grad_project_in.2 = f32[3,1024,1024]{2,1,0:T(8,128)} custom-call(s32[1]{0:T(128)} %bitcast.ctx_ref, bf16[1024,1024]{1,0:T(8,128)(2,1)} %copy.42.left_ref, bf16[4,1024,256]{2,1,0:T(8,128)(2,1)S(1)} %get-tuple-element.29.refs_0_, bf16[4,1024,256]{2,1,0:T(8,128)(2,1)} %get-tuple-element.30.refs_1_, bf16[4,1024,256]{2,1,0:T(8,128)(2,1)} %get-tuple-element.31.refs_2_, ...), custom_call_target="tpu_custom_call" | custom-call | tf_op jit(solution)/shard_map/cond/branch_0_fun/grad_project_in/pallas_call | solution.py:565
  (299 shorter events, 265.4 us)
Async XLA Ops:
  7.2 106.3 %all-gather.3.cloned.1.call-start = ((), (), s32[]{:S(2)}) async-start(), calls=%async_computation.5 | async-start | bytes 10485760 | tf_op jit(solution)/shard_map/all_gather | solution.py:720
  7.9 88.4 %collective-permute-start.10 = (bf16[3,1024,1024]{2,1,0:T(8,128)(2,1)}, bf16[3,1024,1024]{2,1,0:T(8,128)(2,1)}, u32[]{:S(2)}, u32[]{:S(2)}) collective-permute-start(bf16[3,1024,1024]{2,1,0:T(8,128)(2,1)} %bitcast.159), channel_id=1, source_target_pairs={{16,17},{17,16},{18,19},{19,18},{20,21},{21,20},{22,23},{23,22},{2... | collective-permute-start | bytes 18874376 | tf_op jit(solution)/shard_map/ppermute | solution.py:39
  13.5 198.8 %collective-permute-start.27 = (bf16[3,1024,1024]{2,1,0:T(8,128)(2,1)}, bf16[3,1024,1024]{2,1,0:T(8,128)(2,1)}, u32[]{:S(2)}, u32[]{:S(2)}) collective-permute-start(bf16[3,1024,1024]{2,1,0:T(8,128)(2,1)} %bitcast.160), channel_id=1, source_target_pairs={{16,18},{17,19},{18,16},{19,17},{20,22},{21,23},{22,20},{23,21},{2... | collective-permute-start | bytes 18874376 | tf_op jit(solution)/shard_map/ppermute | solution.py:39
  24.0 39.4 %collective-permute-start.5 = (bf16[2,3,512,256]{3,2,1,0:T(8,128)(2,1)}, bf16[2,3,512,256]{3,2,1,0:T(8,128)(2,1)}, u32[]{:S(2)}, u32[]{:S(2)}) collective-permute-start(bf16[2,3,512,256]{3,2,1,0:T(8,128)(2,1)} %table_projection.3), channel_id=1, source_target_pairs={{0,1},{1,0},{2,3},{3,2},{4,5},{5,4},{6,7},{7,6},{8,9},{9,8},{10,11... | collective-permute-start | bytes 4718600 | tf_op jit(solution)/shard_map/ppermute | solution.py:39
  25.8 34.9 %collective-permute-start.7 = (bf16[256,1024]{1,0:T(8,128)(2,1)S(1)}, bf16[256,1024]{1,0:T(8,128)(2,1)S(1)}, u32[]{:S(2)}, u32[]{:S(2)}) collective-permute-start(bf16[256,1024]{1,0:T(8,128)(2,1)S(1)} %copy-done.13), channel_id=1, source_target_pairs={{16,20},{20,24},{24,28},{28,16},{17,21},{21,25},{25,29},{29,17},{1... | collective-permute-start | bytes 1572872 | tf_op jit(solution)/shard_map/ppermute | solution.py:39
  68.7 19.1 %collective-permute-start.6 = (bf16[1,3,512,256]{3,2,1,0:T(8,128)(2,1)}, bf16[1,3,512,256]{3,2,1,0:T(8,128)(2,1)}, u32[]{:S(2)}, u32[]{:S(2)}) collective-permute-start(bf16[1,3,512,256]{3,2,1,0:T(8,128)(2,1)} %split.19), channel_id=1, source_target_pairs={{0,2},{1,3},{2,0},{3,1},{4,6},{5,7},{6,4},{7,5},{8,10},{9,11},{10,... | collective-permute-start | bytes 2359304 | tf_op jit(solution)/shard_map/ppermute | solution.py:39
  121.4 38.2 %collective-permute-start.17 = (bf16[256,1024]{1,0:T(8,128)(2,1)}, bf16[256,1024]{1,0:T(8,128)(2,1)S(1)}, u32[]{:S(2)}, u32[]{:S(2)}) collective-permute-start(bf16[256,1024]{1,0:T(8,128)(2,1)} %get-tuple-element.137), channel_id=1, source_target_pairs={{0,16},{4,20},{8,24},{12,28},{1,17},{5,21},{9,25},{13,29},{2,18},{... | collective-permute-start | bytes 1572872 | tf_op jit(solution)/shard_map/ppermute | solution.py:39
  124.2 24.2 %collective-permute-start.15 = (bf16[128,1024]{1,0:T(8,128)(2,1)}, bf16[128,1024]{1,0:T(8,128)(2,1)S(1)}, u32[]{:S(2)}, u32[]{:S(2)}) collective-permute-start(bf16[128,1024]{1,0:T(8,128)(2,1)} %get-tuple-element.129), channel_id=1, source_target_pairs={{0,24},{4,28},{8,16},{12,20},{1,25},{5,29},{9,17},{13,21},{2,26},{... | collective-permute-start | bytes 786440 | tf_op jit(solution)/shard_map/ppermute | solution.py:39
  125.5 22.9 %collective-permute-start.16 = (bf16[128,1024]{1,0:T(8,128)(2,1)}, bf16[128,1024]{1,0:T(8,128)(2,1)S(1)}, u32[]{:S(2)}, u32[]{:S(2)}) collective-permute-start(bf16[128,1024]{1,0:T(8,128)(2,1)} %get-tuple-element.130), channel_id=1, source_target_pairs={{0,28},{4,16},{8,20},{12,24},{1,29},{5,17},{9,21},{13,25},{2,30},{... | collective-permute-start | bytes 786440 | tf_op jit(solution)/shard_map/ppermute | solution.py:39
  163.1 22.8 %collective-permute-start.21 = (bf16[128,1024]{1,0:T(8,128)(2,1)S(1)}, bf16[128,1024]{1,0:T(8,128)(2,1)S(1)}, u32[]{:S(2)}, u32[]{:S(2)}) collective-permute-start(bf16[128,1024]{1,0:T(8,128)(2,1)S(1)} %copy-done.46), channel_id=1, source_target_pairs={{0,24},{4,28},{8,16},{12,20},{1,25},{5,29},{9,17},{13,21},{2,26},{... | collective-permute-start | bytes 786440 | tf_op jit(solution)/shard_map/ppermute | solution.py:39
  164.4 21.5 %collective-permute-start.22 = (bf16[128,1024]{1,0:T(8,128)(2,1)S(1)}, bf16[128,1024]{1,0:T(8,128)(2,1)S(1)}, u32[]{:S(2)}, u32[]{:S(2)}) collective-permute-start(bf16[128,1024]{1,0:T(8,128)(2,1)S(1)} %copy-done.45), channel_id=1, source_target_pairs={{0,28},{4,16},{8,20},{12,24},{1,29},{5,17},{9,21},{13,25},{2,30},{... | collective-permute-start | bytes 786440 | tf_op jit(solution)/shard_map/ppermute | solution.py:39
  220.7 23.7 %collective-permute-start.28 = (bf16[3,1024,1024]{2,1,0:T(8,128)(2,1)}, bf16[3,1024,1024]{2,1,0:T(8,128)(2,1)}, u32[]{:S(2)}, u32[]{:S(2)}) collective-permute-start(bf16[3,1024,1024]{2,1,0:T(8,128)(2,1)} %collective-permute-done.27.refs_2_), channel_id=1, source_target_pairs={{16,17},{17,16},{18,19},{19,18},{20,21},{21,20},{22,23},{23,22},{2... | collective-permute-start | bytes 18874376 | tf_op jit(solution)/shard_map/ppermute | solution.py:39
  253.0 23.6 %all-to-all-start.1 = ((bf16[4,3,256,256]{3,2,1,0:T(8,128)(2,1)}), bf16[4,3,256,256]{3,2,1,0:T(8,128)(2,1)}, u32[]{:S(2)}, u32[]{:S(2)}) async-start(bf16[4,3,256,256]{3,2,1,0:T(8,128)(2,1)} %input_projection_rest.1), calls=%async_computation.1 | async-start | bytes 3145728 | tf_op jit(solution)/shard_map/all_to_all | solution.py:680
  257.5 39.8 %collective-permute-start.29 = (bf16[1024,256]{1,0:T(8,128)(2,1)}, bf16[1024,256]{1,0:T(8,128)(2,1)S(1)}, u32[]{:S(2)}, u32[]{:S(2)}) collective-permute-start(bf16[1024,256]{1,0:T(8,128)(2,1)} %get-tuple-element.198.refs_0_), channel_id=1, source_target_pairs={{0,1},{1,0},{2,3},{3,2},{4,5},{5,4},{6,7},{7,6},{8,9},{9,8},{10,11... | collective-permute-start | bytes 1572872 | tf_op jit(solution)/shard_map/ppermute | solution.py:39
  258.2 39.1 %collective-permute-start.31 = (bf16[1024,256]{1,0:T(8,128)(2,1)}, bf16[1024,256]{1,0:T(8,128)(2,1)S(1)}, u32[]{:S(2)}, u32[]{:S(2)}) collective-permute-start(bf16[1024,256]{1,0:T(8,128)(2,1)} %collective-permute-done.30.refs_2_), channel_id=1, source_target_pairs={{0,1},{1,0},{2,3},{3,2},{4,5},{5,4},{6,7},{7,6},{8,9},{9,8},{10,11... | collective-permute-start | bytes 1572872 | tf_op jit(solution)/shard_map/ppermute | solution.py:39
  298.4 23.6 %all-to-all-start.2 = ((bf16[4,3,256,256]{3,2,1,0:T(8,128)(2,1)}), bf16[4,3,256,256]{3,2,1,0:T(8,128)(2,1)S(1)}, u32[]{:S(2)}, u32[]{:S(2)}) async-start(bf16[4,3,256,256]{3,2,1,0:T(8,128)(2,1)} %get-tuple-element.181), calls=%async_computation.2 | async-start | bytes 3145728 | tf_op jit(solution)/shard_map/all_to_all | solution.py:680
  339.1 29.3 %collective-permute-start.35 = (bf16[256,1024]{1,0:T(8,128)(2,1)}, bf16[256,1024]{1,0:T(8,128)(2,1)S(1)}, u32[]{:S(2)}, u32[]{:S(2)}) collective-permute-start(bf16[256,1024]{1,0:T(8,128)(2,1)} %get-tuple-element.169), channel_id=1, source_target_pairs={{16,0},{20,4},{24,8},{28,12},{17,1},{21,5},{25,9},{29,13},{18,2},{... | collective-permute-start | bytes 1572872 | tf_op jit(solution)/shard_map/ppermute | solution.py:39
  368.9 47.8 %collective-permute-start.42 = (bf16[4,1024,256]{2,1,0:T(8,128)(2,1)S(1)}, bf16[4,1024,256]{2,1,0:T(8,128)(2,1)}, u32[]{:S(2)}, u32[]{:S(2)}) collective-permute-start(bf16[4,1024,256]{2,1,0:T(8,128)(2,1)S(1)} %pad_maximum_fusion.3.refs_4_), channel_id=1, source_target_pairs={{16,18},{17,19},{18,16},{19,17},{20,22},{21,23},{22,20},{23,21},{2... | collective-permute-start | bytes 6291464 | tf_op jit(solution)/shard_map/ppermute | solution.py:39
  416.7 44.6 %collective-permute-start.49 = (bf16[4,1024,256]{2,1,0:T(8,128)(2,1)S(1)}, bf16[4,1024,256]{2,1,0:T(8,128)(2,1)}, u32[]{:S(2)}, u32[]{:S(2)}) collective-permute-start(bf16[4,1024,256]{2,1,0:T(8,128)(2,1)S(1)} %pad_maximum_fusion.3.refs_4_), channel_id=1, source_target_pairs={{16,17},{17,16},{18,19},{19,18},{20,21},{21,20},{22,23},{23,22},{2... | collective-permute-start | bytes 6291464 | tf_op jit(solution)/shard_map/ppermute | solution.py:39
  421.0 40.3 %collective-permute-start.50 = (bf16[4,1024,256]{2,1,0:T(8,128)(2,1)}, bf16[4,1024,256]{2,1,0:T(8,128)(2,1)}, u32[]{:S(2)}, u32[]{:S(2)}) collective-permute-start(bf16[4,1024,256]{2,1,0:T(8,128)(2,1)} %collective-permute-done.42.refs_6_), channel_id=1, source_target_pairs={{16,17},{17,16},{18,19},{19,18},{20,21},{21,20},{22,23},{23,22},{2... | collective-permute-start | bytes 6291464 | tf_op jit(solution)/shard_map/ppermute | solution.py:39
  435.1 24.2 %collective-permute-start.48 = (bf16[256,1024]{1,0:T(8,128)(2,1)S(1)}, bf16[256,1024]{1,0:T(8,128)(2,1)S(1)}, u32[]{:S(2)}, u32[]{:S(2)}) collective-permute-start(bf16[256,1024]{1,0:T(8,128)(2,1)S(1)} %get-tuple-element.263), channel_id=1, source_target_pairs={{16,19},{17,18},{18,17},{19,16},{20,23},{21,22},{22,21},{23,20},{2... | collective-permute-start | bytes 1572872 | tf_op jit(solution)/shard_map/ppermute | solution.py:39
  480.5 43.9 %all-to-all-start.4 = ((bf16[4,256,1024]{2,1,0:T(8,128)(2,1)}), bf16[4,256,1024]{2,1,0:T(8,128)(2,1)}, u32[]{:S(2)}, u32[]{:S(2)}) async-start(bf16[4,256,1024]{2,1,0:T(8,128)(2,1)} %pad_maximum_fusion.7), calls=%async_computation.4 | async-start | bytes 4194304 | tf_op jit(solution)/shard_map/all_to_all | solution.py:680
  494.2 22.7 %collective-permute-start.52 = (bf16[3,512,256]{2,1,0:T(8,128)(2,1)}, bf16[3,512,256]{2,1,0:T(8,128)(2,1)}, u32[]{:S(2)}, u32[]{:S(2)}) collective-permute-start(bf16[3,512,256]{2,1,0:T(8,128)(2,1)} %get-tuple-element.197), channel_id=1, source_target_pairs={{0,2},{1,3},{2,0},{3,1},{4,6},{5,7},{6,4},{7,5},{8,10},{9,11},{10,... | collective-permute-start | bytes 2359304 | tf_op jit(solution)/shard_map/ppermute | solution.py:39
  498.9 19.8 %collective-permute-start.54 = (f32[138,256]{1,0:T(8,128)}, f32[138,256]{1,0:T(8,128)}, u32[]{:S(2)}, u32[]{:S(2)}) collective-permute-start(f32[138,256]{1,0:T(8,128)} %pad_maximum_fusion.13), channel_id=1, source_target_pairs={{0,1},{1,0},{2,3},{3,2},{16,17},{17,16},{18,19},{19,18},{4,5},{5,4... | collective-permute-start | bytes 423944 | tf_op jit(solution)/shard_map/ppermute | solution.py:39
  (89 other events, 1170.9 us)
Sparse Core Ops, SparseCore 0:
  9.6 103.8 all-gather.2
